TPU v7x, 32 devices: a whole 2x2x4 slice. The times are simulated.
32 devices in a mesh: pop: 4 (over z), tp: 8 (over y, x, core).
Axes of the slice: x: 2, y: 2, z: 4, core: 2. Of those that a mesh axis runs over, the one named last changes fastest.
Arguments:
- in_spikes: int32 [4, 15, 4096], replicated, may hold values 0 or 1
- w_in: bfloat16 [4096, 4096], P(None, 'tp'), may hold values from -0.1875 to 0.1875
- w_rec: bfloat16 [4096, 4096], P(None, 'tp'), may hold values from -0.1875 to 0.1875
- leak_rate: float32 [4096], P('tp'), may hold values from 0.5 to 0.95
- neuron_bias: float32 [4096], P('tp'), may hold values from -2.5 to 2.5
- readout: float32 [4096], P('tp'), may hold values from -0.1875 to 0.1875
- pert_table: bfloat16 [256, 4096], P(None, 'tp'), may hold values from -4 to 4
- pert_idx: int32 [128, 2], P('pop'), may hold values from 0 to 255
- member_ranks: int32 [128], P('pop'), may hold values from 0 to 127, each once
Outputs:
- returns: float32 [128], P('pop')
- grad_rec: bfloat16 [4096, 4096], P(None, 'tp')
Inputs may be any that keep to these rules, and one draw needn't show every extreme that they name: member_ranks holds each of 0 to 127 once.
All inputs are finite; a program needn't handle non-finite values.
Results may differ from a plain program's by a relative error of at most 0.0044.
Values may be sent and summed in bfloat16 or wider, within the bound.
No kernel may reach another device: no remote copies, remote signals or barrier semaphores. Data moves between devices by JAX's collectives and lax.ppermute only.
A program may use at most 64 MiB of HBM per device.

v0:
```python
import jax
import jax.numpy as jnp
from jax import lax
from jax.sharding import PartitionSpec as P

sigma_scale = 0.01


def shards(
    in_spikes, w_in, w_rec, leak_rate, neuron_bias, readout, pert_table, pert_idx, member_ranks
):
    step_count, episodes, inputs = in_spikes.shape
    members_dev = pert_idx.shape[0]
    local_width = w_rec.shape[1]
    row_count = members_dev * episodes
    member_count = members_dev * lax.axis_size("pop")
    spike_input = in_spikes.astype(jnp.bfloat16).reshape(step_count * episodes, inputs)
    input_drive = jnp.dot(spike_input, w_in, preferred_element_type=jnp.float32) + neuron_bias
    input_drive = input_drive.reshape(step_count, episodes, local_width)
    post_side = jnp.take(pert_table, pert_idx[:, 1], axis=0).astype(jnp.float32)
    pre_local = jnp.take(pert_table, pert_idx[:, 0], axis=0)
    membrane = jnp.zeros((members_dev, episodes, local_width), jnp.float32)
    spikes = jnp.zeros((members_dev, episodes, local_width), jnp.bfloat16)
    readout_sum = jnp.zeros((members_dev, episodes), jnp.float32)
    for moment in range(step_count):
        current = input_drive[moment][None]
        if moment > 0:
            flat_spikes = spikes.reshape(row_count, local_width)
            recurrent = jnp.dot(
                lax.all_gather(flat_spikes, "tp", axis=1, tiled=True),
                w_rec,
                preferred_element_type=jnp.float32,
            )
            partial_proj = jnp.einsum(
                "men,mn->me", spikes, pre_local, preferred_element_type=jnp.float32
            )
            projection = lax.psum(partial_proj, "tp")
            current = (
                current
                + recurrent.reshape(members_dev, episodes, local_width)
                + sigma_scale * projection[:, :, None] * post_side[:, None, :]
            )
        membrane = leak_rate * (membrane - spikes.astype(jnp.float32)) + current
        spikes = jax.nn.sigmoid(4.0 * (membrane - 1.0)).astype(jnp.bfloat16)
        readout_sum = readout_sum + jnp.einsum(
            "men,n->me", spikes.astype(jnp.float32), readout, precision=lax.Precision.HIGHEST
        )
    returns = lax.psum(jnp.sum(readout_sum, axis=1), "tp") / (episodes * step_count)
    fitness = member_ranks.astype(jnp.float32) / (member_count - 1) - 0.5 + returns
    full_table = lax.all_gather(pert_table, "tp", axis=1, tiled=True)
    pre_side = jnp.take(full_table, pert_idx[:, 0], axis=0)
    weighted = pre_side.astype(jnp.float32) * fitness[:, None]
    partial_grad = jnp.dot(weighted.T, post_side, precision=lax.Precision.HIGHEST)
    grad_total = lax.psum(partial_grad, "pop")
    grad_rec = (grad_total * jnp.sqrt(12.0 / member_count)).astype(jnp.bfloat16)
    return (returns, grad_rec)


def solution(mesh):
    placed = (
        P(),
        P(None, "tp"),
        P(None, "tp"),
        P("tp"),
        P("tp"),
        P("tp"),
        P(None, "tp"),
        P("pop", None),
        P("pop"),
    )
    return jax.shard_map(
        shards, mesh=mesh, in_specs=placed, out_specs=(P("pop"), P(None, "tp")), check_vma=False
    )
```

profile of v0, /device:TPU:0, one launch (start us, length us, event | category | flops | bytes accessed | tf_op | source)
XLA Modules:
  0.0 498.6 jit_solution(7472254372093253523)
XLA Ops:
  7.9 1.4 convert_element_type.61
  9.8 3.1 convolution_add_fusion
  13.1 1.1 divide_convert_fusion.5
  15.9 25.9 %psum.35 = f32[32,15]{1,0:T(8,128)S(1)} all-reduce(f32[32,15]{1,0:T(8,128)S(1)} %bitcast.55), channel_id=1, replica_groups=mesh['pop'=4,'tp'=8] {'tp'}, use_global_device_ids=true, to_apply=%region_0.0 | all-reduce | flops 480 | bytes 3840 | tf_op jit(solution)/shard_map/psum | solution.py:37
  42.1 1.1 add.178
  43.5 9.9 %all-gather.5.cloned.1.call-done = bf16[480,4096]{1,0:T(8,128)(2,1)} async-done(((bf16[480,512]{1,0:T(8,128)(2,1)}), bf16[480,4096]{1,0:T(8,128)(2,1)}) %all-gather.5.cloned.1.call-update) | async-done | bytes 3932176 | tf_op jit(solution)/shard_map/all_gather | solution.py:30
  53.5 7.4 %divide_convert_fusion.4 = (bf16[480,512]{1,0:T(8,128)(2,1)}, f32[480,512]{1,0:T(8,128)}, f32[480,512]{1,0:T(8,128)S(1)}) fusion(f32[480,512]{1,0:T(8,128)S(1)} %mul.165, f32[480]{0:T(512)S(1)} %mul.163, f32[480,512]{1,0:T(8,128)} %add.178, f32[480,512]{1,0:T(8,128)S(1)} %add.169, f32[512]{0:T(512)S(1)} %broadcast_multiply_fusion.3, f32[512]{0:T(512)S(1)} %copy-done.3, ...), kind=kOutput, calls=%fused_computation.20 | convolution fusion | flops 2018181120 | bytes 13539200 | tf_op jit(solution)/shard_map/dot_general | solution.py:29
  61.8 1.1 add.189
  63.7 23.8 %psum.36 = f32[32,15]{1,0:T(8,128)S(1)} all-reduce(f32[32,15]{1,0:T(8,128)S(1)} %bitcast.56), channel_id=1, replica_groups=mesh['pop'=4,'tp'=8] {'tp'}, use_global_device_ids=true, to_apply=%region_1.3 | all-reduce | flops 480 | bytes 3840 | tf_op jit(solution)/shard_map/psum | solution.py:37
  87.6 9.8 %all-gather.7.cloned.1.call-done = bf16[480,4096]{1,0:T(8,128)(2,1)} async-done(((bf16[480,512]{1,0:T(8,128)(2,1)}), bf16[480,4096]{1,0:T(8,128)(2,1)}) %all-gather.7.cloned.1.call-update) | async-done | bytes 3932176 | tf_op jit(solution)/shard_map/all_gather | solution.py:30
  97.4 7.5 %divide_convert_fusion.3 = (bf16[480,512]{1,0:T(8,128)(2,1)}, f32[480,512]{1,0:T(8,128)}) fusion(f32[480,512]{1,0:T(8,128)S(1)} %mul.165, f32[480,512]{1,0:T(8,128)} %add.189, f32[480,512]{1,0:T(8,128)} %get-tuple-element.8, f32[480]{0:T(512)S(1)} %mul.174, f32[512]{0:T(512)S(1)} %copy-done.3, bf16[480,4096]{1,0:T(8,128)(2,1)} %all-gather.7.cloned.1.call-done, ...), kind=kOutput, calls=%fused_computation.19 | convolution fusion | flops 2017935360 | bytes 12554112 | tf_op jit(solution)/shard_map/dot_general | solution.py:29
  105.2 22.3 %all-gather.11.cloned.1.call-done = bf16[256,4096]{1,0:T(8,128)(2,1)} async-done(((bf16[256,512]{1,0:T(8,128)(2,1)}), bf16[256,4096]{1,0:T(8,128)(2,1)}) %all-gather.11.cloned.1.call-update) | async-done | bytes 2097168 | tf_op jit(solution)/shard_map/all_gather | solution.py:50
  127.5 2.8 gather_fusion
  131.2 1.3 reshape.61
  132.6 1.9 divide_convert_fusion.1
  135.4 0.7 fusion.13
  136.5 24.1 %psum.37 = f32[32,15]{1,0:T(8,128)S(1)} all-reduce(f32[32,15]{1,0:T(8,128)S(1)} %bitcast.54), channel_id=1, replica_groups=mesh['pop'=4,'tp'=8] {'tp'}, use_global_device_ids=true, to_apply=%region_2.4 | all-reduce | flops 480 | bytes 3840 | tf_op jit(solution)/shard_map/psum | solution.py:37
  160.7 5.1 %all-gather.9.cloned.1.call-done = bf16[480,4096]{1,0:T(8,128)(2,1)} async-done(((bf16[480,512]{1,0:T(8,128)(2,1)}), bf16[480,4096]{1,0:T(8,128)(2,1)}) %all-gather.9.cloned.1.call-update) | async-done | bytes 3932176 | tf_op jit(solution)/shard_map/all_gather | solution.py:30
  165.8 6.5 %fusion.38 = f32[480,512]{1,0:T(8,128)} fusion(bf16[480,4096]{1,0:T(8,128)(2,1)} %all-gather.9.cloned.1.call-done, bf16[4096,512]{1,0:T(8,128)(2,1)} %param.13), kind=kOutput, calls=%fused_computation.72 | convolution fusion | flops 2013265920 | bytes 9109504 | tf_op jit(solution)/shard_map/dot_general | solution.py:29
  172.3 1.3 reshape.62
  175.1 13.1 %psum.38 = f32[32]{0:T(128)S(1)} all-reduce(f32[32]{0:T(128)S(1)} %fusion.31), channel_id=1, replica_groups=mesh['pop'=4,'tp'=8] {'tp'}, use_global_device_ids=true, to_apply=%region_4.6 | all-reduce | flops 32 | bytes 256 | tf_op jit(solution)/shard_map/psum | solution.py:48
  188.7 5.8 %fusion.8 = f32[4096,512]{1,0:T(8,128)} fusion(f32[32]{0:T(128)S(1)} %get-tuple-element.3, bf16[32,4096]{1,0:T(8,128)(2,1)S(1)} %gather_fusion, pred[32]{0:T(512)(128)(4,1)S(1)} %and_bitcast_fusion, bf16[32,512]{1,0:T(8,128)(2,1)S(1)} %gather_fusion.2, pred[32]{0:T(512)(128)(4,1)S(1)} %get-tuple-element.18), kind=kOutput, calls=%fused_computation.23 | convolution fusion | flops 805715968 | bytes 8683712 | tf_op jit(solution)/shard_map/dot_general | solution.py:53
  194.5 291.0 %all-reduce.2.cloned.1.call-done = f32[4096,512]{1,0:T(8,128)} async-done(((f32[4096,512]{1,0:T(8,128)}), f32[4096,512]{1,0:T(8,128)}) %all-reduce.2.cloned.1.call-update) | async-done | bytes 8388624 | tf_op jit(solution)/shard_map/psum | solution.py:54
  485.5 6.6 %multiply_convert_fusion = bf16[4096,512]{1,0:T(8,128)(2,1)} fusion(f32[4096,512]{1,0:T(8,128)} %all-reduce.2.cloned.1.call-done), kind=kLoop, calls=%fused_computation.3 | loop fusion | flops 4194304 | bytes 12582912 | tf_op jit(solution)/shard_map/convert_element_type | solution.py:55
  (62 shorter events, 9.9 us)
Async XLA Ops:
  7.2 123.1 %copy-start = (f32[512]{0:T(512)S(1)}, f32[512]{0:T(512)}, u32[]{:S(2)}) copy-start(f32[512]{0:T(512)} %param.16) | copy-start | bytes 6148
  7.2 46.3 %all-gather.5.cloned.1.call-start = ((), (), s32[]{:S(2)}) async-start(), calls=%async_computation | async-start | bytes 4423680 | tf_op jit(solution)/shard_map/all_gather | solution.py:30
  9.8 4.5 copy-start.4
  9.8 4.5 copy-start.2
  14.2 83.2 %all-gather.7.cloned.1.call-start = ((), (), s32[]{:S(2)}) async-start(), calls=%async_computation.1 | async-start | bytes 4423680 | tf_op jit(solution)/shard_map/all_gather | solution.py:30
  15.9 37.5 %copy-start.3 = (f32[512]{0:T(512)S(1)}, f32[512]{0:T(512)}, u32[]{:S(2)}) copy-start(f32[512]{0:T(512)} %param.14) | copy-start | bytes 6148
  60.9 66.6 %all-gather.11.cloned.1.call-start = ((), (), s32[]{:S(2)}) async-start(), calls=%async_computation.3 | async-start | bytes 2359296 | tf_op jit(solution)/shard_map/all_gather | solution.py:50
  61.6 104.2 %all-gather.9.cloned.1.call-start = ((), (), s32[]{:S(2)}) async-start(), calls=%async_computation.2 | async-start | bytes 4423680 | tf_op jit(solution)/shard_map/all_gather | solution.py:30
  104.9 380.6 %all-reduce.2.cloned.1.call-start = ((), (), s32[]{:S(2)}) async-start(), calls=%async_computation.4 | async-start | bytes 16777216 | tf_op jit(solution)/shard_map/psum | solution.py:54
  160.7 13.0 %copy-start.1 = (f32[32,15,512]{2,1,0:T(8,128)S(1)}, f32[32,15,512]{2,1,0:T(8,128)}, u32[]{:S(2)}) copy-start(f32[32,15,512]{2,1,0:T(8,128)} %get-tuple-element.6) | copy-start | bytes 2949124
  172.3 15.9 %copy-start.5 = (s32[32]{0:T(128)S(1)}, s32[32]{0:T(128)}, u32[]{:S(2)}) copy-start(s32[32]{0:T(128)} %param.19) | copy-start | bytes 388
Sparse Core Ops, SparseCore 0:
  14.3 39.0 all-gather.4
  61.0 36.3 all-gather.6
  99.3 28.1 all-gather.10
  129.2 36.4 all-gather.8
  194.6 290.8 all-reduce.1
where the time goes:
time: 499 us
  waiting for transfers between devices  339 us (68%)
  blocking collectives  87 us (17%)
  matrix products  34 us (7%)
  between operations  14 us (3%)
  other arithmetic  13.3 us (3%)
  local copies, waits for them, and re-layouts  11 us (2%)
    psum x1, waiting for transfers between devices, shards(): grad_total = lax.psum(partial_grad, 'pop')  291 us
    psum x3, blocking collectives, shards(): projection = lax.psum(partial_proj, 'tp')  73.9 us
    all_gather x3, waiting for transfers between devices, shards(): lax.all_gather(flat_spikes, 'tp', axis=1, tiled=True)  24.8 us
    all_gather x1, waiting for transfers between devices, shards(): full_table = lax.all_gather(pert_table, 'tp', axis=1, tiled=True)  22.3 us
    dot_general x3, matrix products, shards(): jnp.dot(lax.all_gather(flat_spikes, 'tp', axis=1, tiled=True), w_rec, pre...  21.4 us
    psum x1, blocking collectives, shards(): lax.psum(jnp.sum(readout_sum, axis=1), 'tp') / (episodes * step_count)  13.1 us
  transfers between devices with their start and end apart: 5, of which 5 were waited for; matrix products, arithmetic and copies ran while one was open for 4% of the time, Pallas kernels for 0%

commit v1 on v0

v1 whole, which is shorter than its diff:
```python
import jax
import jax.numpy as jnp
from jax import lax
from jax.sharding import PartitionSpec as P

sigma_scale = 0.01
f32 = jnp.float32
bf16 = jnp.bfloat16


def spike(membrane):
    return jax.nn.sigmoid(4.0 * (membrane - 1.0)).astype(bf16)


def swap(x, axis, mask):
    return lax.ppermute(x, axis, [(i, i ^ mask) for i in range(lax.axis_size(axis))])


def chip_blocks(x):
    chips = lax.axis_size("tp") // 2
    chip = lax.axis_index("tp") // 2
    if chips != 4:
        groups = [[2 * q + c for q in range(chips)] for c in range(2)]
        every = lax.all_gather(x, "tp", axis_index_groups=groups)
        return [(every[q], jnp.int32(q)) for q in range(chips)]
    half = x.shape[1] // 2
    over_x = swap(x, "tp", 2)
    over_y = swap(x, "tp", 4)
    left = swap(over_x[:, :half], "tp", 4)
    right = swap(over_y[:, half:], "tp", 2)
    return [(x, chip), (over_x, chip ^ 1), (over_y, chip ^ 2), (jnp.concatenate([left, right], 1), chip ^ 3)]


def shards(
    in_spikes, w_in, w_rec, leak_rate, neuron_bias, readout, pert_table, pert_idx, member_ranks
):
    steps, epis, inputs = in_spikes.shape
    members = pert_idx.shape[0]
    half = members // 2
    width = w_rec.shape[1]
    tp, pop = lax.axis_size("tp"), lax.axis_size("pop")
    me, plane = lax.axis_index("tp"), lax.axis_index("pop")
    chip, core = me // 2, me % 2
    member_count = members * pop
    epad = -(-epis // 16) * 16

    w_sib = swap(w_rec, "tp", 1)
    spike_input = in_spikes.astype(bf16).reshape(steps * epis, inputs)
    drive = (jnp.dot(spike_input, w_in, preferred_element_type=f32) + neuron_bias).reshape(steps, epis, width)
    s0 = spike(drive[0])
    side = jnp.concatenate([drive.reshape(steps * epis, width), leak_rate[None], readout[None]], 0)
    side_sib = swap(side, "tp", 1)
    pre_loc = jnp.take(pert_table, pert_idx[:, 0], axis=0)
    post_loc = jnp.take(pert_table, pert_idx[:, 1], axis=0)
    s0p = jnp.pad(s0, ((0, epad - epis), (0, 0)))
    load = jnp.stack(
        [jnp.concatenate([s0p, pre_loc[c * half:(c + 1) * half], post_loc[c * half:(c + 1) * half]], 0) for c in range(2)]
    )
    load = jnp.broadcast_to(load[None], (tp // 2,) + load.shape).reshape((tp,) + load.shape[1:])
    got = lax.all_to_all(load, "tp", 0, 0)
    s0_full, pre_full, post_full = got[:, :epis], got[:, epad:epad + half], got[:, epad + half:]
    w_own = w_rec.reshape(tp, width, width)
    base = leak_rate * (drive[0] - s0.astype(f32)) + drive[1] + jnp.einsum("jek,jkn->en", s0_full, w_own, preferred_element_type=f32)
    proj1 = jnp.einsum("jek,jmk->em", s0_full, pre_full, preferred_element_type=f32)
    base_full = lax.all_to_all(jnp.broadcast_to(base[None], (tp,) + base.shape), "tp", 0, 0)
    mem1 = base_full[:, :, None, :] + sigma_scale * proj1[None, :, :, None] * post_full.astype(f32)[:, None, :, :]
    s1 = spike(mem1)
    rows = epis * half
    proj2 = jnp.einsum("jemk,jmk->em", s1.astype(f32), pre_full.astype(f32))
    s1f = s1.reshape(tp, rows, width)
    is_low = core == 0

    def pair(own, sib, axis):
        return jnp.concatenate([jnp.where(is_low, own, sib), jnp.where(is_low, sib, own)], axis)

    sides = pair(side, side_sib, 1)
    drives = sides[: steps * epis].reshape(steps, epis, 1, 2 * width)
    leak, read = sides[steps * epis], sides[steps * epis + 1]
    w2 = pair(w_rec, w_sib, 1)

    def chip_cols(x):
        two = lax.dynamic_slice_in_dim(x, chip * 2, 2, 0)
        return jnp.concatenate([two[0], two[1]], -1)

    post = chip_cols(post_full).astype(f32)[None]
    s1c = chip_cols(s1).astype(f32)
    m1c = chip_cols(mem1)
    rec = jnp.einsum("jrk,jkn->rn", s1f, w2.reshape(tp, width, 2 * width), preferred_element_type=f32)
    mem2 = leak * (m1c - s1c) + drives[2] + rec.reshape(epis, half, 2 * width) + sigma_scale * proj2[:, :, None] * post
    s2 = spike(mem2)
    blocks = chip_blocks(s2.reshape(rows, 2 * width))
    pre_z = [pre_full] + [swap(pre_full, "pop", s) for s in range(1, pop)]
    post_z = [post_loc] + [swap(post_loc, "pop", s) for s in range(1, pop)]
    pre_own = jnp.stack(pre_z).transpose(0, 2, 1, 3).reshape(pop * half, inputs)
    pre_oth = swap(pre_own, "tp", 1)
    pre_all = pair(pre_own.reshape(pop, half, inputs), pre_oth.reshape(pop, half, inputs), 1).reshape(member_count, inputs)
    post_all = jnp.stack(post_z).reshape(member_count, width)

    mem3 = leak * (mem2 - s2.astype(f32)) + drives[3]
    proj3 = 0.0
    pre_w = pre_full.transpose(1, 0, 2).reshape(half, inputs)
    for block, q in blocks:
        wq = lax.dynamic_slice_in_dim(w2, q * 2 * width, 2 * width, 0)
        pq = lax.dynamic_slice_in_dim(pre_w, q * 2 * width, 2 * width, 1)
        mem3 = mem3 + jnp.dot(block, wq, preferred_element_type=f32).reshape(mem3.shape)
        proj3 = proj3 + jnp.einsum("emk,mk->em", block.reshape(epis, half, 2 * width).astype(f32), pq.astype(f32))
    mem3 = mem3 + sigma_scale * proj3[:, :, None] * post
    s3 = spike(mem3)
    s0c = chip_cols(s0_full).astype(f32)
    total = (
        jnp.sum(s0c * read)
        + jnp.sum((s1c + s2.astype(f32) + s3.astype(f32)) * read, axis=(0, 2))
    )
    ranks = lax.dynamic_slice_in_dim(member_ranks, core * half, half, 0).astype(f32)
    note = jnp.stack([total, ranks])
    notes = lax.all_to_all(jnp.broadcast_to(note[None], (pop * tp,) + note.shape), ("pop", "tp"), 0, 0)
    notes = notes.reshape(pop, tp // 2, 2, 2, half)
    returns = jnp.sum(notes[:, :, :, 0], axis=1).reshape(pop, members) / (epis * steps)
    ranks_all = notes[:, 0, :, 1].reshape(pop, members)
    fitness = ranks_all / (member_count - 1) - 0.5 + returns
    order = plane ^ jnp.arange(pop)
    scale = (jnp.take(fitness, order, axis=0) * jnp.sqrt(12.0 / member_count)).reshape(member_count, 1)
    weighted = post_all.astype(f32) * scale
    high = weighted.astype(bf16)
    low = (weighted - high.astype(f32)).astype(bf16)
    both = jnp.concatenate([high, low], 0)
    pre_two = jnp.concatenate([pre_all, pre_all], 0)
    grad = lax.dot_general(pre_two, both, (((0,), (0,)), ((), ())), preferred_element_type=f32).astype(bf16)
    mine = lax.dynamic_slice_in_dim(returns, plane, 1, 0)[0]
    return (mine, grad)


def solution(mesh):
    placed = (
        P(),
        P(None, "tp"),
        P(None, "tp"),
        P("tp"),
        P("tp"),
        P("tp"),
        P(None, "tp"),
        P("pop", None),
        P("pop"),
    )
    return jax.shard_map(
        shards, mesh=mesh, in_specs=placed, out_specs=(P("pop"), P(None, "tp")), check_vma=False
    )
```

time: 499 us -> 144 us (0.29)
  waiting for transfers between devices: 339 us -> 25.2 us
  blocking collectives: 87 us -> 0 us
  other arithmetic: 13.3 us -> 40.9 us
  starting transfers between devices: 0.38 us -> 27.3 us
  between operations: 14 us -> 1.12 us
  local copies, waits for them, and re-layouts: 11 us -> 16.5 us
    psum x1 -> x0, waiting for transfers between devices: 291 us -> none  [shards(): grad_total = lax.psum(partial_grad, 'pop')]
    psum x4 -> x0, blocking collectives: 87 us -> none  [the longest x3 73.9 us: shards(): projection = lax.psum(partial_proj, 'tp')]
    all_gather x4 -> x0, waiting for transfers between devices: 47.1 us -> none  [the longest x3 24.8 us: shards(): lax.all_gather(flat_spikes, 'tp', axis=1, tiled=True)]
    ppermute x0 -> x13, starting transfers between devices: none -> 14.8 us  [swap(): lax.ppermute(x, axis, [(i, i ^ mask) for i in range(lax.axis_size(axis))])]
    all_to_all x0 -> x3, waiting for transfers between devices: none -> 13.9 us  [the longest x1 5.97 us: shards(): lax.all_to_all(jnp.broadcast_to(note[None], (pop * tp,) + note.shape), ('...]
    all_to_all x0 -> x3, starting transfers between devices: none -> 12.5 us  [the longest x1 4.89 us: shards(): lax.all_to_all(jnp.broadcast_to(note[None], (pop * tp,) + note.shape), ('...]
    ppermute x0 -> x13, waiting for transfers between devices: none -> 11.3 us  [swap(): lax.ppermute(x, axis, [(i, i ^ mask) for i in range(lax.axis_size(axis))])]
    concatenate x0 -> x4, other arithmetic: none -> 10 us  [the longest x3 10 us: pair(): jnp.concatenate([jnp.where(is_low, own, sib), jnp.where(is_low, sib, own)...]
  transfers between devices with their start and end apart: 5 -> 16, of which waited for: 5 -> 5; matrix products, arithmetic and copies ran while one was open for 4% -> 35% of each run, Pallas kernels for 0% -> 0%
where the time goes in v1:
time: 144 us; the launch traced here: 143 us
  other arithmetic  40.9 us (28%)
  matrix products  31.7 us (22%)
  starting transfers between devices  27.3 us (19%)
  waiting for transfers between devices  25.2 us (18%)
  local copies, waits for them, and re-layouts  16.5 us (11%)
    ppermute x13, starting transfers between devices, swap(): lax.ppermute(x, axis, [(i, i ^ mask) for i in range(lax.axis_size(axis))])  14.8 us
    ppermute x13, waiting for transfers between devices, swap(): lax.ppermute(x, axis, [(i, i ^ mask) for i in range(lax.axis_size(axis))])  11.3 us
    concatenate x3, other arithmetic, pair(): jnp.concatenate([jnp.where(is_low, own, sib), jnp.where(is_low, sib, own)...  10 us
    convert_element_type x2, other arithmetic, spike(): return jax.nn.sigmoid(4.0 * (membrane - 1.0)).astype(bf16)  8.94 us
    dot_general x4, matrix products, shards(): jnp.dot(block, wq, preferred_element_type=f32).reshape(mem3.shape)  8.18 us
    select_n x3, other arithmetic, pair(): jnp.where(is_low, own, sib)  7.62 us
    dot_general x1, matrix products, shards(): jnp.einsum('jrk,jkn->rn', s1f, w2.reshape(tp, width, 2 * width), preferre...  7.46 us
    all_to_all x1, waiting for transfers between devices, shards(): lax.all_to_all(jnp.broadcast_to(note[None], (pop * tp,) + note.shape), ('...  5.97 us
  transfers between devices with their start and end apart: 16, of which 5 were waited for; matrix products, arithmetic and copies ran while one was open for 35% of the time, Pallas kernels for 0%

profile of v1, /device:TPU:0, one launch (start us, length us, event | category | flops | bytes accessed | tf_op | source)
XLA Modules:
  0.0 142.8 jit_solution(11279738514338671658)
XLA Ops:
  2.3 3.1 %collective-permute-start.10 = (bf16[32,512]{1,0:T(8,128)(2,1)S(1)}, bf16[32,512]{1,0:T(8,128)(2,1)S(1)}, u32[]{:S(2)}, u32[]{:S(2)}) collective-permute-start(bf16[32,512]{1,0:T(8,128)(2,1)S(1)} %broadcast_select_fusion.6), channel_id=1, source_target_pairs={{0,8},{8,0},{16,24},{24,16},{1,9},{9,1},{17,25},{25,17},{2,10},{10... | collective-permute-start | bytes 98312 | tf_op jit(solution)/shard_map/ppermute | solution.py:16
  5.4 2.6 %collective-permute-start.11 = (bf16[32,512]{1,0:T(8,128)(2,1)S(1)}, bf16[32,512]{1,0:T(8,128)(2,1)S(1)}, u32[]{:S(2)}, u32[]{:S(2)}) collective-permute-start(bf16[32,512]{1,0:T(8,128)(2,1)S(1)} %broadcast_select_fusion.6), channel_id=1, source_target_pairs={{0,16},{8,24},{16,0},{24,8},{1,17},{9,25},{17,1},{25,9},{2,18},{10... | collective-permute-start | bytes 98312 | tf_op jit(solution)/shard_map/ppermute | solution.py:16
  9.9 3.0 %convolution_add_fusion = f32[60,512]{1,0:T(8,128)S(1)} fusion(bf16[60,4096]{1,0:T(8,128)(2,1)S(1)} %reshape.165, bf16[4096,512]{1,0:T(8,128)(2,1)} %param.12, f32[512]{0:T(512)} %param.15), kind=kOutput, calls=%fused_computation.46 | convolution fusion | flops 251688960 | bytes 4810752 | tf_op jit(solution)/shard_map/dot_general | solution.py:49
  15.2 4.0 %all-to-all-start = ((bf16[8,48,512]{2,1,0:T(8,128)(2,1)}), bf16[8,48,512]{2,1,0:T(8,128)(2,1)S(1)}, u32[]{:S(2)}, u32[]{:S(2)}) async-start(bf16[8,48,512]{2,1,0:T(8,128)(2,1)} %bitcast.4), calls=%async_computation | async-start | bytes 786432 | tf_op jit(solution)/shard_map/all_to_all | solution.py:60
  22.4 5.2 %all-to-all-done = bf16[8,48,512]{2,1,0:T(8,128)(2,1)S(1)} async-done(((bf16[8,48,512]{2,1,0:T(8,128)(2,1)}), bf16[8,48,512]{2,1,0:T(8,128)(2,1)S(1)}, u32[]{:S(2)}, u32[]{:S(2)}) %all-to-all-start) | async-done | bytes 393248 | tf_op jit(solution)/shard_map/all_to_all | solution.py:60
  29.4 2.5 %collective-permute-start.6 = (bf16[8,16,512]{2,1,0:T(8,128)(2,1)S(1)}, bf16[8,16,512]{2,1,0:T(8,128)(2,1)S(1)}, u32[]{:S(2)}, u32[]{:S(2)}) collective-permute-start(bf16[8,16,512]{2,1,0:T(8,128)(2,1)S(1)} %get-tuple-element.24), channel_id=1, source_target_pairs={{0,8},{8,0},{16,24},{24,16},{1,9},{9,1},{17,25},{25,17},{2,10},{10... | collective-permute-start | bytes 393224 | tf_op jit(solution)/shard_map/ppermute | solution.py:16
  32.1 2.8 %fusion.30 = f32[15,512]{1,0:T(8,128)S(1)} fusion(bf16[8,512,512]{2,1,0:T(8,128)(2,1)} %bitcast.144, f32[60,512]{1,0:T(8,128)S(1)} %convolution_add_fusion, bf16[15,512]{1,0:T(8,128)(2,1)S(1)} %divide_convert_fusion.2, f32[512]{0:T(512)S(1)} %copy-done.16, bf16[8,48,512]{2,1,0:T(8,128)(2,1)S(1)} %all-to-all-done), kind=kOutput, calls=%fused_computation.48 | convolution fusion | flops 62952960 | bytes 4440064 | tf_op jit(solution)/shard_map/jek,jkn->en/dot_general | solution.py:63
  35.7 3.6 %all-to-all-start.1 = ((f32[8,15,512]{2,1,0:T(8,128)}), f32[8,15,512]{2,1,0:T(8,128)S(1)}, u32[]{:S(2)}, u32[]{:S(2)}) async-start(f32[8,15,512]{2,1,0:T(8,128)} %broadcast_in_dim.29), calls=%async_computation.1 | async-start | bytes 524288 | tf_op jit(solution)/shard_map/all_to_all | solution.py:65
  43.2 2.7 %all-to-all-done.1 = f32[8,15,512]{2,1,0:T(8,128)S(1)} async-done(((f32[8,15,512]{2,1,0:T(8,128)}), f32[8,15,512]{2,1,0:T(8,128)S(1)}, u32[]{:S(2)}, u32[]{:S(2)}) %all-to-all-start.1) | async-done | bytes 245792 | tf_op jit(solution)/shard_map/all_to_all | solution.py:65
  46.0 3.2 %multiply_add_fusion = (f32[8,15,16,512]{3,2,1,0:T(8,128)}, bf16[8,15,16,512]{3,2,1,0:T(8,128)(2,1)S(1)}) fusion(f32[8,16,512]{2,1,0:T(8,128)S(1)} %get-tuple-element.22, f32[15,16]{1,0:T(8,128)S(1)} %fusion.31, f32[8,15,512]{2,1,0:T(8,128)S(1)} %all-to-all-done.1), kind=kLoop, calls=%fused_computation.24 | loop fusion | flops 7864320 | bytes 6407104 | tf_op jit(solution)/shard_map/add | solution.py:66
  50.2 8.9 %fusion.6 = bf16[8,240,512]{2,0,1:T(8,128)(2,1)} fusion(f32[8,240,512]{2,1,0:T(8,128)S(1)} %bitcast.145, f32[8,240,512]{2,1,0:T(8,128)S(1)} %bitcast.146, f32[240]{0:T(256)S(1)} %mul.206), kind=kLoop, calls=%fused_computation.25 | loop fusion | flops 7864320 | bytes 9831360 | tf_op jit(solution)/shard_map/convert_element_type | solution.py:12
  61.4 2.5 %dynamic-slice_bitcast_fusion.1 = (f32[15,16,512]{2,1,0:T(8,128)S(1)}, f32[15,16,512]{2,1,0:T(8,128)}) fusion(f32[8,15,16,512]{3,2,1,0:T(8,128)} %get-tuple-element.15, s32[]{:T(128)S(6)} %select_n.109, s32[]{:T(128)S(6)} %add.228), kind=kLoop, calls=%fused_computation.86 | loop fusion | bytes 1966088 | tf_op jit(solution)/shard_map/squeeze | solution.py:83
  64.0 2.3 %broadcast_select_fusion.3 = (bf16[4,16,4096]{2,1,0:T(8,128)(2,1)}, bf16[4,16,4096]{2,1,0:T(8,128)(2,1)}) fusion(bf16[4,16,4096]{2,1,0:T(8,128)(2,1)S(1)} %bitcast.151, bf16[4,16,4096]{2,1,0:T(8,128)(2,1)} %bitcast.58, pred[]{:T(512)S(6)} %eq.5), kind=kLoop, calls=%fused_computation.84 | loop fusion | flops 524288 | bytes 2097153 | tf_op jit(solution)/shard_map/jit(_where)/select_n | solution.py:74
  66.3 5.3 %broadcast_select_fusion.1 = (bf16[4096,512]{1,0:T(8,128)(2,1)}, bf16[4096,512]{1,0:T(8,128)(2,1)}) fusion(bf16[4096,512]{1,0:T(8,128)(2,1)S(1)} %copy-done.4, bf16[4096,512]{1,0:T(8,128)(2,1)} %collective-permute-done.1, pred[]{:T(512)S(6)} %eq.5), kind=kLoop, calls=%fused_computation.14 | loop fusion | flops 4194304 | bytes 16777216 | tf_op jit(solution)/shard_map/jit(_where)/select_n | solution.py:74
  71.6 8.1 %pad_maximum_fusion = bf16[4096,1024]{1,0:T(8,128)(2,1)} fusion(bf16[4096,512]{1,0:T(8,128)(2,1)} %get-tuple-element.8, bf16[4096,512]{1,0:T(8,128)(2,1)} %get-tuple-element.7), kind=kLoop, calls=%fused_computation.7 | loop fusion | flops 16777216 | bytes 16777216 | tf_op jit(solution)/shard_map/concatenate | solution.py:74
  79.7 7.5 %divide_convert_fusion.1 = (bf16[15,16,1024]{2,1,0:T(8,128)(2,1)}, f32[15,16,1024]{2,1,0:T(8,128)}) fusion(f32[16,1024]{1,0:T(8,128)} %maximum_convert_fusion, f32[15,16]{1,0:T(8,128)S(1)} %fusion.77, f32[15,1024]{1,0:T(8,128)} %get-tuple-element.26, bf16[15,16,512]{2,1,0:T(8,128)(2,1)S(1)} %copy-done.9, bf16[15,16,512]{2,1,0:T(8,128)(2,1)S(1)} %get-tuple-element.11, ...), kind=kOutput, calls=%fused_computation.72 | convolution fusion | flops 2017443840 | bytes 13435840 | tf_op jit(solution)/shard_map/jrk,jkn->rn/dot_general | solution.py:88
  89.8 2.5 %fusion.9 = f32[15,16,1024]{2,1,0:T(8,128)S(1)} fusion(bf16[15,16,1024]{2,1,0:T(8,128)(2,1)} %get-tuple-element.49, s32[]{:T(128)S(6)} %select_n.117, bf16[4096,512]{1,0:T(8,128)(2,1)} %get-tuple-element.7, bf16[4096,512]{1,0:T(8,128)(2,1)} %get-tuple-element.8), kind=kOutput, calls=%fused_computation.28 | convolution fusion | flops 507510784 | bytes 9863172 | tf_op jit(solution)/shard_map/dot_general | solution.py:105
  92.3 7.6 %collective-permute-done.2 = bf16[240,1024]{1,0:T(8,128)(2,1)S(1)} collective-permute-done((bf16[240,1024]{1,0:T(8,128)(2,1)}, bf16[240,1024]{1,0:T(8,128)(2,1)S(1)}, u32[]{:S(2)}, u32[]{:S(2)}) %collective-permute-start.2) | collective-permute-done | bytes 491552 | tf_op jit(solution)/shard_map/ppermute | solution.py:16
  110.7 3.7 %collective-permute-done.5 = bf16[240,512]{1,0:T(8,128)(2,1)} collective-permute-done((bf16[240,512]{1,0:T(8,128)(2,1)}, bf16[240,512]{1,0:T(8,128)(2,1)}, u32[]{:S(2)}, u32[]{:S(2)}) %collective-permute-start.5) | collective-permute-done | bytes 245792 | tf_op jit(solution)/shard_map/ppermute | solution.py:16
  115.3 3.3 %fusion.19 = f32[240,1024]{1,0:T(8,128)} fusion(bf16[240,1024]{1,0:T(8,128)(2,1)S(1)} %constant_dynamic-update-slice_fusion, s32[]{:T(128)S(6)} %select_n.120, bf16[4096,512]{1,0:T(8,128)(2,1)} %get-tuple-element.7, bf16[4096,512]{1,0:T(8,128)(2,1)} %get-tuple-element.8), kind=kOutput, calls=%fused_computation.37 | convolution fusion | flops 507510784 | bytes 9863172 | tf_op jit(solution)/shard_map/dot_general | solution.py:105
  120.4 3.1 %fusion.38 = f32[16]{0:T(128)S(1)} fusion(bf16[15,16,1024]{2,1,0:T(8,128)(2,1)} %get-tuple-element.49, f32[15,16,1024]{2,1,0:T(8,128)} %bitcast.150, f32[15,16,1024]{2,1,0:T(8,128)S(1)} %bitcast.149, f32[15,16,1024]{2,1,0:T(8,128)S(1)} %bitcast.148, f32[15,16,1024]{2,1,0:T(8,128)S(1)} %fusion.9, f32[1024]{0:T(1024)S(1)} %bitcast.164, ...), kind=kLoop, calls=%fused_computation.58 | loop fusion | flops 7864304 | bytes 7079872 | tf_op jit(solution)/shard_map/reduce_sum | solution.py:112
  124.8 4.9 %all-to-all-start.2 = ((f32[32,2,16]{2,1,0:T(2,128)}), f32[32,2,16]{2,1,0:T(2,128)S(1)}, u32[]{:S(2)}, u32[]{:S(2)}) async-start(f32[32,2,16]{2,1,0:T(2,128)} %broadcast_in_dim.30), calls=%async_computation.2 | async-start | bytes 65536 | tf_op jit(solution)/shard_map/all_to_all | solution.py:116
  131.0 6.0 %all-to-all-done.2 = f32[32,2,16]{2,1,0:T(2,128)S(1)} async-done(((f32[32,2,16]{2,1,0:T(2,128)}), f32[32,2,16]{2,1,0:T(2,128)S(1)}, u32[]{:S(2)}, u32[]{:S(2)}) %all-to-all-start.2) | async-done | bytes 4128 | tf_op jit(solution)/shard_map/all_to_all | solution.py:116
  139.6 3.3 %convolution_convert_fusion = bf16[4096,512]{1,0:T(8,128)(2,1)} fusion(bf16[128,4096]{1,0:T(8,128)(2,1)S(1)} %bitcast.156, bf16[128,512]{1,0:T(8,128)(2,1)S(1)} %get-tuple-element.32, bf16[128,512]{1,0:T(8,128)(2,1)S(1)} %get-tuple-element.31), kind=kOutput, calls=%fused_computation.12 | convolution fusion | flops 1080557568 | bytes 5505024 | tf_op jit(solution)/shard_map/dot_general | solution.py:128
  (140 shorter events, 40.1 us)
Async XLA Ops:
  2.3 10.6 %copy-start.16 = (f32[512]{0:T(512)S(1)}, f32[512]{0:T(512)}, u32[]{:S(2)}) copy-start(f32[512]{0:T(512)} %param.14) | copy-start | bytes 6148
  2.3 10.6 %copy-start.17 = (f32[512]{0:T(512)S(1)}, f32[512]{0:T(512)}, u32[]{:S(2)}) copy-start(f32[512]{0:T(512)} %param.16) | copy-start | bytes 6148
  2.3 18.7 %collective-permute-start.10 = (bf16[32,512]{1,0:T(8,128)(2,1)S(1)}, bf16[32,512]{1,0:T(8,128)(2,1)S(1)}, u32[]{:S(2)}, u32[]{:S(2)}) collective-permute-start(bf16[32,512]{1,0:T(8,128)(2,1)S(1)} %broadcast_select_fusion.6), channel_id=1, source_target_pairs={{0,8},{8,0},{16,24},{24,16},{1,9},{9,1},{17,25},{25,17},{2,10},{10... | collective-permute-start | bytes 98312 | tf_op jit(solution)/shard_map/ppermute | solution.py:16
  5.4 15.6 %collective-permute-start.11 = (bf16[32,512]{1,0:T(8,128)(2,1)S(1)}, bf16[32,512]{1,0:T(8,128)(2,1)S(1)}, u32[]{:S(2)}, u32[]{:S(2)}) collective-permute-start(bf16[32,512]{1,0:T(8,128)(2,1)S(1)} %broadcast_select_fusion.6), channel_id=1, source_target_pairs={{0,16},{8,24},{16,0},{24,8},{1,17},{9,25},{17,1},{25,9},{2,18},{10... | collective-permute-start | bytes 98312 | tf_op jit(solution)/shard_map/ppermute | solution.py:16
  8.0 13.0 %collective-permute-start.12 = (bf16[32,512]{1,0:T(8,128)(2,1)S(1)}, bf16[32,512]{1,0:T(8,128)(2,1)S(1)}, u32[]{:S(2)}, u32[]{:S(2)}) collective-permute-start(bf16[32,512]{1,0:T(8,128)(2,1)S(1)} %broadcast_select_fusion.6), channel_id=1, source_target_pairs={{0,24},{8,16},{16,8},{24,0},{1,25},{9,17},{17,9},{25,1},{2,26},{10... | collective-permute-start | bytes 98312 | tf_op jit(solution)/shard_map/ppermute | solution.py:16
  9.9 10.6 %copy-start.20 = (s32[32]{0:T(128)S(1)}, s32[32]{0:T(128)}, u32[]{:S(2)}) copy-start(s32[32]{0:T(128)} %param.19) | copy-start | bytes 388
  13.0 8.7 %collective-permute-start = (f32[62,512]{1,0:T(8,128)S(1)}, f32[62,512]{1,0:T(8,128)S(1)}, u32[]{:S(2)}, u32[]{:S(2)}) collective-permute-start(f32[62,512]{1,0:T(8,128)S(1)} %pad_maximum_fusion.4), channel_id=1, source_target_pairs={{0,1},{1,0},{2,3},{3,2},{4,5},{5,4},{6,7},{7,6},{8,9},{9,8},{10,11... | collective-permute-start | bytes 380936 | tf_op jit(solution)/shard_map/ppermute | solution.py:16
  15.2 12.4 %all-to-all-start = ((bf16[8,48,512]{2,1,0:T(8,128)(2,1)}), bf16[8,48,512]{2,1,0:T(8,128)(2,1)S(1)}, u32[]{:S(2)}, u32[]{:S(2)}) async-start(bf16[8,48,512]{2,1,0:T(8,128)(2,1)} %bitcast.4), calls=%async_computation | async-start | bytes 786432 | tf_op jit(solution)/shard_map/all_to_all | solution.py:60
  19.2 47.0 %collective-permute-start.1 = (bf16[4096,512]{1,0:T(8,128)(2,1)}, bf16[4096,512]{1,0:T(8,128)(2,1)}, u32[]{:S(2)}, u32[]{:S(2)}) collective-permute-start(bf16[4096,512]{1,0:T(8,128)(2,1)} %param.13), channel_id=1, source_target_pairs={{0,1},{1,0},{2,3},{3,2},{4,5},{5,4},{6,7},{7,6},{8,9},{9,8},{10,11... | collective-permute-start | bytes 12582920 | tf_op jit(solution)/shard_map/ppermute | solution.py:16
  27.7 13.9 %collective-permute-start.7 = (bf16[8,16,512]{2,1,0:T(8,128)(2,1)S(1)}, bf16[8,16,512]{2,1,0:T(8,128)(2,1)S(1)}, u32[]{:S(2)}, u32[]{:S(2)}) collective-permute-start(bf16[8,16,512]{2,1,0:T(8,128)(2,1)S(1)} %get-tuple-element.24), channel_id=1, source_target_pairs={{0,16},{8,24},{16,0},{24,8},{1,17},{9,25},{17,1},{25,9},{2,18},{10... | collective-permute-start | bytes 393224 | tf_op jit(solution)/shard_map/ppermute | solution.py:16
  29.4 12.1 %collective-permute-start.6 = (bf16[8,16,512]{2,1,0:T(8,128)(2,1)S(1)}, bf16[8,16,512]{2,1,0:T(8,128)(2,1)S(1)}, u32[]{:S(2)}, u32[]{:S(2)}) collective-permute-start(bf16[8,16,512]{2,1,0:T(8,128)(2,1)S(1)} %get-tuple-element.24), channel_id=1, source_target_pairs={{0,8},{8,0},{16,24},{24,16},{1,9},{9,1},{17,25},{25,17},{2,10},{10... | collective-permute-start | bytes 393224 | tf_op jit(solution)/shard_map/ppermute | solution.py:16
  31.9 9.7 %collective-permute-start.8 = (bf16[8,16,512]{2,1,0:T(8,128)(2,1)S(1)}, bf16[8,16,512]{2,1,0:T(8,128)(2,1)S(1)}, u32[]{:S(2)}, u32[]{:S(2)}) collective-permute-start(bf16[8,16,512]{2,1,0:T(8,128)(2,1)S(1)} %get-tuple-element.24), channel_id=1, source_target_pairs={{0,24},{8,16},{16,8},{24,0},{1,25},{9,17},{17,9},{25,1},{2,26},{10... | collective-permute-start | bytes 393224 | tf_op jit(solution)/shard_map/ppermute | solution.py:16
  35.7 10.3 %all-to-all-start.1 = ((f32[8,15,512]{2,1,0:T(8,128)}), f32[8,15,512]{2,1,0:T(8,128)S(1)}, u32[]{:S(2)}, u32[]{:S(2)}) async-start(f32[8,15,512]{2,1,0:T(8,128)} %broadcast_in_dim.29), calls=%async_computation.1 | async-start | bytes 524288 | tf_op jit(solution)/shard_map/all_to_all | solution.py:65
  43.0 20.9 %collective-permute-start.9 = (bf16[64,4096]{1,0:T(8,128)(2,1)}, bf16[64,4096]{1,0:T(8,128)(2,1)}, u32[]{:S(2)}, u32[]{:S(2)}) collective-permute-start(bf16[64,4096]{1,0:T(8,128)(2,1)} %bitcast.75), channel_id=1, source_target_pairs={{0,1},{1,0},{2,3},{3,2},{4,5},{5,4},{6,7},{7,6},{8,9},{9,8},{10,11... | collective-permute-start | bytes 1572872 | tf_op jit(solution)/shard_map/ppermute | solution.py:16
  63.9 15.7 %copy-start.6 = (f32[15,16,512]{2,1,0:T(8,128)}, f32[15,16,512]{2,1,0:T(8,128)S(1)}, u32[]{:S(2)}) copy-start(f32[15,16,512]{2,1,0:T(8,128)S(1)} %get-tuple-element.9) | copy-start | bytes 1474564
  79.7 8.6 %copy-start.15 = (bf16[16,1024,1]{1,0,2:T(8,128)(2,1)S(1)}, bf16[16,1024,1]{1,0,2:T(8,128)(2,1)}, u32[]{:S(2)}) copy-start(bf16[16,1024,1]{1,0,2:T(8,128)(2,1)} %get-tuple-element.35) | copy-start | bytes 98308
  87.1 15.8 %collective-permute-start.3 = (bf16[240,1024]{1,0:T(8,128)(2,1)}, bf16[240,1024]{1,0:T(8,128)(2,1)}, u32[]{:S(2)}, u32[]{:S(2)}) collective-permute-start(bf16[240,1024]{1,0:T(8,128)(2,1)} %bitcast.32), channel_id=1, source_target_pairs={{0,4},{1,5},{2,6},{3,7},{4,0},{5,1},{6,2},{7,3},{8,12},{9,13},{10,... | collective-permute-start | bytes 1474568 | tf_op jit(solution)/shard_map/ppermute | solution.py:16
  87.7 12.2 %collective-permute-start.2 = (bf16[240,1024]{1,0:T(8,128)(2,1)}, bf16[240,1024]{1,0:T(8,128)(2,1)S(1)}, u32[]{:S(2)}, u32[]{:S(2)}) collective-permute-start(bf16[240,1024]{1,0:T(8,128)(2,1)} %bitcast.32), channel_id=1, source_target_pairs={{0,2},{1,3},{2,0},{3,1},{4,6},{5,7},{6,4},{7,5},{8,10},{9,11},{10,... | collective-permute-start | bytes 1474568 | tf_op jit(solution)/shard_map/ppermute | solution.py:16
  89.8 12.4 %copy-start.2 = (bf16[4096,512]{1,0:T(8,128)(2,1)S(1)}, bf16[4096,512]{1,0:T(8,128)(2,1)}, u32[]{:S(2)}) copy-start(bf16[4096,512]{1,0:T(8,128)(2,1)} %get-tuple-element.7) | copy-start | bytes 12582916
  89.8 12.4 %copy-start.3 = (bf16[4096,512]{1,0:T(8,128)(2,1)S(1)}, bf16[4096,512]{1,0:T(8,128)(2,1)}, u32[]{:S(2)}) copy-start(bf16[4096,512]{1,0:T(8,128)(2,1)} %get-tuple-element.8) | copy-start | bytes 12582916
  100.7 9.9 %collective-permute-start.4 = (bf16[240,512]{1,0:T(8,128)(2,1)}, bf16[240,512]{1,0:T(8,128)(2,1)S(1)}, u32[]{:S(2)}, u32[]{:S(2)}) collective-permute-start(bf16[240,512]{1,0:T(8,128)(2,1)} %slice.131), channel_id=1, source_target_pairs={{0,4},{1,5},{2,6},{3,7},{4,0},{5,1},{6,2},{7,3},{8,12},{9,13},{10,... | collective-permute-start | bytes 737288 | tf_op jit(solution)/shard_map/ppermute | solution.py:16
  107.8 6.5 %collective-permute-start.5 = (bf16[240,512]{1,0:T(8,128)(2,1)}, bf16[240,512]{1,0:T(8,128)(2,1)}, u32[]{:S(2)}, u32[]{:S(2)}) collective-permute-start(bf16[240,512]{1,0:T(8,128)(2,1)} %slice.132), channel_id=1, source_target_pairs={{0,2},{1,3},{2,0},{3,1},{4,6},{5,7},{6,4},{7,5},{8,10},{9,11},{10,... | collective-permute-start | bytes 737288 | tf_op jit(solution)/shard_map/ppermute | solution.py:16
  120.4 18.0 %copy-start.18 = (pred[4]{0:T(512)(128)(4,1)S(1)}, pred[4]{0:T(512)(128)(4,1)}, u32[]{:S(2)}) copy-start(pred[4]{0:T(512)(128)(4,1)} %compare_and_fusion.2) | copy-start | bytes 16
  124.8 12.1 %all-to-all-start.2 = ((f32[32,2,16]{2,1,0:T(2,128)}), f32[32,2,16]{2,1,0:T(2,128)S(1)}, u32[]{:S(2)}, u32[]{:S(2)}) async-start(f32[32,2,16]{2,1,0:T(2,128)} %broadcast_in_dim.30), calls=%async_computation.2 | async-start | bytes 65536 | tf_op jit(solution)/shard_map/all_to_all | solution.py:116
  (13 other events, 62.3 us)

commit v2 on v0

v2 whole, which is shorter than its diff:
```python
import functools

import jax
import jax.numpy as jnp
from jax import lax
from jax.experimental import pallas as pl
from jax.experimental.pallas import tpu as pltpu
from jax.sharding import PartitionSpec as P

sigma_scale = 0.01
f32 = jnp.float32
bf16 = jnp.bfloat16
i32 = jnp.int32
EP = 16
VMEM_LIMIT = 24 * 2**20


def spike(membrane):
    return (0.5 + 0.5 * jnp.tanh(2.0 * (membrane - 1.0))).astype(bf16)


def dot(a, b):
    return jnp.dot(a, b, preferred_element_type=f32)


def fold(x):
    parts = [x[:, i : i + 128] for i in range(0, x.shape[1], 128)]
    return functools.reduce(jnp.add, parts)


def params(cost_flops, cost_bytes):
    return dict(
        compiler_params=pltpu.CompilerParams(vmem_limit_bytes=VMEM_LIMIT, dimension_semantics=("arbitrary",)),
        cost_estimate=pl.CostEstimate(flops=cost_flops, bytes_accessed=cost_bytes, transcendentals=0),
    )


def whole(shape):
    return pl.BlockSpec(shape, lambda *_: (0,) * len(shape))


def drive_kernel(spk_ref, win_ref, bias_ref, leak_ref, read_ref, table_ref, idx_ref, side_ref, load_ref, post_ref, acc_ref):
    k = pl.program_id(0)
    steps, epis, depth = spk_ref.shape
    tp = load_ref.shape[0]

    @pl.when(k == 0)
    def _():
        acc_ref[...] = jnp.zeros_like(acc_ref)
        count = idx_ref.shape[0]
        at = lax.broadcasted_iota(i32, (count, table_ref.shape[0]), 1)
        pre_hot = jnp.where(at == idx_ref[:, 0:1], 1.0, 0.0).astype(bf16)
        post_hot = jnp.where(at == idx_ref[:, 1:2], 1.0, 0.0).astype(bf16)
        pre = dot(pre_hot, table_ref[...]).astype(bf16)
        post = dot(post_hot, table_ref[...]).astype(bf16)
        for j in range(tp):
            c = j % 2
            load_ref[j, EP : 2 * EP, :] = pre[c * EP : (c + 1) * EP]
            load_ref[j, 2 * EP : 3 * EP, :] = post[c * EP : (c + 1) * EP]
        for c in range(2):
            post_ref[c] = post[c * EP : (c + 1) * EP]

    blank = jnp.zeros((EP - epis, depth), i32)
    rows = [jnp.concatenate([spk_ref[t], blank], 0).astype(f32).astype(bf16) for t in range(steps)]
    acc_ref[...] += dot(jnp.concatenate(rows, 0), win_ref[...])

    @pl.when(k == pl.num_programs(0) - 1)
    def _():
        drive = acc_ref[...] + bias_ref[...]
        side_ref[: steps * EP, :] = drive
        row = lax.broadcasted_iota(i32, (8, drive.shape[1]), 0)
        side_ref[steps * EP :, :] = jnp.where(row == 0, leak_ref[...], read_ref[...])
        s0 = spike(drive[:EP]).astype(f32)
        here = lax.broadcasted_iota(i32, s0.shape, 0) < epis
        s0 = jnp.where(here, s0, 0.0).astype(bf16)
        for j in range(tp):
            load_ref[j, 0:EP, :] = s0


def drive_call(in_spikes, w_in, bias, leak, read, table, idx, tp):
    steps, epis, inputs = in_spikes.shape
    width = w_in.shape[1]
    depth = min(1024, inputs)
    members = idx.shape[0]
    rows = steps * EP
    return pl.pallas_call(
        drive_kernel,
        grid=(inputs // depth,),
        in_specs=[
            pl.BlockSpec((steps, epis, depth), lambda k: (0, 0, k)),
            pl.BlockSpec((depth, width), lambda k: (k, 0)),
            whole((1, width)),
            whole((1, width)),
            whole((1, width)),
            whole(table.shape),
            whole((members, 2)),
        ],
        out_specs=[whole((rows + 8, width)), whole((tp, 3 * EP, width)), whole((2, EP, width))],
        out_shape=[
            jax.ShapeDtypeStruct((rows + 8, width), f32),
            jax.ShapeDtypeStruct((tp, 3 * EP, width), bf16),
            jax.ShapeDtypeStruct((2, EP, width), bf16),
        ],
        scratch_shapes=[pltpu.VMEM((rows, width), f32)],
        name="drive",
        **params(2 * rows * inputs * width, inputs * width * 2 + steps * 16 * inputs * 4),
    )(in_spikes, w_in, bias, leak, read, table, idx)


def base_kernel(s0_ref, pre_ref, w_ref, side_ref, out_ref, proj_ref, acc_ref):
    j = pl.program_id(0)
    steps_rows = side_ref.shape[0] - 8

    @pl.when(j == 0)
    def _():
        acc_ref[...] = jnp.zeros_like(acc_ref)
        proj_ref[...] = jnp.zeros_like(proj_ref)

    s0 = s0_ref[0]
    acc_ref[...] += dot(s0, w_ref[...])
    proj_ref[...] += lax.dot_general(pre_ref[0], s0, (((1,), (1,)), ((), ())), preferred_element_type=f32)

    @pl.when(j == pl.num_programs(0) - 1)
    def _():
        mem0 = side_ref[0:EP, :]
        leak = side_ref[steps_rows : steps_rows + 1, :]
        base = leak * (mem0 - spike(mem0).astype(f32)) + side_ref[EP : 2 * EP, :] + acc_ref[...]
        for i in range(out_ref.shape[0]):
            out_ref[i] = base


def base_call(got, w_rec, side):
    tp, _, width = got.shape
    return pl.pallas_call(
        base_kernel,
        grid=(tp,),
        in_specs=[
            pl.BlockSpec((1, EP, width), lambda j: (j, 0, 0)),
            pl.BlockSpec((1, EP, width), lambda j: (j, 1, 0)),
            pl.BlockSpec((width, width), lambda j: (j, 0)),
            whole(side.shape),
        ],
        out_specs=[whole((tp, EP, width)), whole((EP, EP))],
        out_shape=[jax.ShapeDtypeStruct((tp, EP, width), f32), jax.ShapeDtypeStruct((EP, EP), f32)],
        scratch_shapes=[pltpu.VMEM((EP, width), f32)],
        name="base",
        **params(2 * EP * tp * width * width, tp * width * width * 2),
    )(got, got, w_rec, side)


def step2_kernel(
    me_ref, base_ref, s0_ref, pre_ref, post_ref, wo_ref, ws_ref, proj1_ref, so_ref, ss_ref,
    s2o_ref, s2s_ref, nexto_ref, nexts_ref, postc_ref, read_ref,
    s1_ref, acco_ref, accs_ref, carry_ref, p2_ref, rs_ref, *, epis,
):
    j = pl.program_id(0)
    width = base_ref.shape[2]
    lead = so_ref.shape[0] - 8

    def membrane1(e):
        c = sigma_scale * proj1_ref[:, e : e + 1]
        return base_ref[0, e : e + 1, :] + c * post_ref[0].astype(f32)

    @pl.when(j == 0)
    def _():
        acco_ref[...] = jnp.zeros_like(acco_ref)
        accs_ref[...] = jnp.zeros_like(accs_ref)
        p2_ref[...] = jnp.zeros_like(p2_ref)
        rs_ref[...] = jnp.zeros_like(rs_ref)

    pre = pre_ref[0].astype(f32)
    for e in range(epis):
        at = slice(e * EP, (e + 1) * EP)
        s1 = spike(membrane1(e))
        s1_ref[at, :] = s1
        p2_ref[at, :] += fold(s1.astype(f32) * pre)

    def chip_part(h, side_ref):
        leak, read = side_ref[lead : lead + 1, :], side_ref[lead + 1 : lead + 2, :]
        postc_ref[h] = post_ref[0]
        s0 = s0_ref[0].astype(f32)
        total = jnp.broadcast_to(jnp.sum(s0, 0, keepdims=True), (EP, width))
        for e in range(epis):
            at = slice(e * EP, (e + 1) * EP)
            s1 = s1_ref[at, :].astype(f32)
            total += s1
            carry_ref[h, at, :] = leak * (membrane1(e) - s1) + side_ref[2 * EP + e : 2 * EP + e + 1, :]
        rs_ref[...] += fold(total * read)

    @pl.when(j == 0)
    def _():
        chip_part(0, so_ref)

    @pl.when(j == 1)
    def _():
        chip_part(1, ss_ref)

    acco_ref[...] += dot(s1_ref[...], wo_ref[...])
    accs_ref[...] += dot(s1_ref[...], ws_ref[...])

    @pl.when(j == pl.num_programs(0) - 1)
    def _():
        proj2 = sigma_scale * jnp.sum(p2_ref[...], axis=1, keepdims=True)
        for h, side_ref, acc_ref, s2_ref, next_ref in (
            (0, so_ref, acco_ref, s2o_ref, nexto_ref),
            (1, ss_ref, accs_ref, s2s_ref, nexts_ref),
        ):
            leak, read = side_ref[lead : lead + 1, :], side_ref[lead + 1 : lead + 2, :]
            post = postc_ref[h].astype(f32)
            total = jnp.zeros((EP, width), f32)
            for e in range(epis):
                at = slice(e * EP, (e + 1) * EP)
                mem = carry_ref[h, at, :] + acc_ref[at, :] + proj2[at, :] * post
                s2 = spike(mem)
                s2_ref[at, :] = s2
                s2 = s2.astype(f32)
                total += s2
                next_ref[at, :] = leak * (mem - s2) + side_ref[3 * EP + e : 3 * EP + e + 1, :]
            rs_ref[...] += fold(total * read)
        read_ref[...] = rs_ref[...]


def step2_call(me, base, got, w_rec, w_sib, proj1, side, side_sib, epis):
    tp, _, width = got.shape
    rows = epis * EP
    far = lambda block: pl.BlockSpec((1, EP, width), lambda j, me: (j ^ me[0], block, 0))
    weight = pl.BlockSpec((width, width), lambda j, me: (j ^ me[0], 0))
    spec = pltpu.PrefetchScalarGridSpec(
        num_scalar_prefetch=1,
        grid=(tp,),
        in_specs=[far(0), far(0), far(1), far(2), weight, weight, whole((EP, EP)), whole(side.shape), whole(side.shape)],
        out_specs=[whole((rows, width))] * 4 + [whole((2, EP, width)), whole((EP, 128))],
        scratch_shapes=[
            pltpu.VMEM((rows, width), bf16),
            pltpu.VMEM((rows, width), f32),
            pltpu.VMEM((rows, width), f32),
            pltpu.VMEM((2, rows, width), f32),
            pltpu.VMEM((rows, 128), f32),
            pltpu.VMEM((EP, 128), f32),
        ],
    )
    sds = jax.ShapeDtypeStruct
    return pl.pallas_call(
        functools.partial(step2_kernel, epis=epis),
        grid_spec=spec,
        out_shape=[
            sds((rows, width), bf16), sds((rows, width), bf16), sds((rows, width), f32), sds((rows, width), f32),
            sds((2, EP, width), bf16), sds((EP, 128), f32),
        ],
        name="step2",
        **params(4 * rows * tp * width * width, 4 * tp * width * width),
    )(me, base, got, got, got, w_rec, w_sib, proj1, side, side_sib)


def accumulate(j, blocks, wo_ref, ws_ref, pre_ref, acco_ref, accs_ref, p_ref):
    for n, block_ref in enumerate(blocks):

        @pl.when(j == n)
        def _(block_ref=block_ref):
            acco_ref[...] += dot(block_ref[...], wo_ref[...])
            accs_ref[...] += dot(block_ref[...], ws_ref[...])
            pre = pre_ref[0].astype(f32)
            for r in range(0, block_ref.shape[0], EP):
                p_ref[r : r + EP, :] += fold(block_ref[r : r + EP, :].astype(f32) * pre)


def part_kernel(me_ref, *refs, count, first, packs):
    blocks, refs = refs[:count], refs[count:]
    wo_ref, ws_ref, pre_ref, acco_in, accs_in, p_in = refs[:6]
    rest = refs[6:]
    j = pl.program_id(0)
    if packs:
        got_ref, post_ref, acco_ref, accs_ref, p_ref, pack_ref = rest
    else:
        acco_ref, accs_ref, p_ref = rest

    @pl.when(j == 0)
    def _():
        acco_ref[...] = acco_in[...]
        accs_ref[...] = accs_in[...]
        p_ref[...] = jnp.zeros_like(p_ref) if first else p_in[...]
        if packs:
            tp = got_ref.shape[0]
            for i in range(tp):
                pack_ref[i] = got_ref[i]
            for c in range(2):
                pack_ref[tp + c] = post_ref[c]

    accumulate(j, blocks, wo_ref, ws_ref, pre_ref, acco_ref, accs_ref, p_ref)


def table_index(order):
    def of(j):
        at = jnp.int32(order[0])
        for n, v in enumerate(order[1:], 1):
            at = jnp.where(j == n, jnp.int32(v), at)
        return at

    return of


def part_specs(blocks, order, got, shapes):
    rows, width = blocks[0].shape
    at = table_index(order)
    weight = pl.BlockSpec((width, width), lambda j, me: (at(j) ^ me[0], 0))
    return [whole((rows, width)) for _ in blocks] + [
        weight,
        weight,
        pl.BlockSpec((1, EP, width), lambda j, me: (at(j) ^ me[0], 1, 0)),
    ] + [whole(s) for s in shapes]


def part_call(me, blocks, order, w_rec, w_sib, got, acco, accs, proj, post_loc=None):
    rows, width = blocks[0].shape
    tp = got.shape[0]
    first = proj is None
    packs = post_loc is not None
    if first:
        proj = jnp.zeros((EP, 128), f32)
    ins = part_specs(blocks, order, got, [(rows, width), (rows, width), proj.shape])
    sds = jax.ShapeDtypeStruct
    outs = [sds((rows, width), f32), sds((rows, width), f32), sds((rows, 128), f32)]
    args = [me, *blocks, w_rec, w_sib, got, acco, accs, proj]
    if packs:
        ins += [pl.BlockSpec((tp, EP, width), lambda j, me: (0, 1, 0)), whole(post_loc.shape)]
        outs += [sds((tp + 2, EP, width), bf16)]
        args += [got, post_loc]
    spec = pltpu.PrefetchScalarGridSpec(
        num_scalar_prefetch=1,
        grid=(len(blocks),),
        in_specs=ins,
        out_specs=[whole(o.shape) for o in outs],
    )
    n = len(blocks)
    return pl.pallas_call(
        functools.partial(part_kernel, count=n, first=first, packs=packs),
        grid_spec=spec,
        out_shape=outs,
        name="part",
        **params(4 * rows * n * width * width, 4 * n * width * width + 16 * rows * width),
    )(*args)


def last_kernel(me_ref, *refs, count, epis, copies):
    blocks, refs = refs[:count], refs[count:]
    wo_ref, ws_ref, pre_ref, acco_in, accs_in, p_in, so_ref, ss_ref, postc_ref, read_ref, ranks_ref = refs[:11]
    note_ref, acco_ref, accs_ref, p_ref = refs[11:]
    j = pl.program_id(0)
    lead = so_ref.shape[0] - 8

    @pl.when(j == 0)
    def _():
        acco_ref[...] = acco_in[...]
        accs_ref[...] = accs_in[...]
        p_ref[...] = p_in[...]

    accumulate(j, blocks, wo_ref, ws_ref, pre_ref, acco_ref, accs_ref, p_ref)

    @pl.when(j == pl.num_programs(0) - 1)
    def _():
        proj = sigma_scale * jnp.sum(p_ref[...], axis=1, keepdims=True)
        sums = read_ref[...]
        for h, side_ref, acc_ref in ((0, so_ref, acco_ref), (1, ss_ref, accs_ref)):
            read = side_ref[lead + 1 : lead + 2, :]
            post = postc_ref[h].astype(f32)
            total = jnp.zeros(post.shape, f32)
            for e in range(epis):
                at = slice(e * EP, (e + 1) * EP)
                total += spike(acc_ref[at, :] + proj[at, :] * post).astype(f32)
            sums += fold(total * read)
        sums = jnp.sum(sums, axis=1, keepdims=True)
        row = lax.broadcasted_iota(i32, (EP, 128), 0)
        lane = lax.broadcasted_iota(i32, (EP, 128), 1) & (EP - 1)
        flat = jnp.sum(jnp.where(row == lane, sums, 0.0), axis=0, keepdims=True)
        core = me_ref[0] & 1
        ranks = ranks_ref[...].astype(f32)
        mine = jnp.where(core == 0, ranks[:EP], ranks[EP:])
        rank = jnp.sum(jnp.where(row == lane, mine, 0.0), axis=0, keepdims=True)
        odd = (lax.broadcasted_iota(i32, (2 * copies, 128), 0) & 1) == 1
        note_ref[...] = jnp.where(odd, rank, flat)


def last_call(me, blocks, order, w_rec, w_sib, got, acco, accs, proj, side, side_sib, postc, read, ranks, epis, copies):
    rows, width = blocks[0].shape
    ins = part_specs(
        blocks, order, got,
        [(rows, width), (rows, width), proj.shape, side.shape, side.shape, postc.shape, read.shape, ranks.shape],
    )
    spec = pltpu.PrefetchScalarGridSpec(
        num_scalar_prefetch=1,
        grid=(len(blocks),),
        in_specs=ins,
        out_specs=whole((2 * copies, 128)),
        scratch_shapes=[
            pltpu.VMEM((rows, width), f32),
            pltpu.VMEM((rows, width), f32),
            pltpu.VMEM((rows, 128), f32),
        ],
    )
    n = len(blocks)
    return pl.pallas_call(
        functools.partial(last_kernel, count=n, epis=epis, copies=copies),
        grid_spec=spec,
        out_shape=jax.ShapeDtypeStruct((2 * copies, 128), f32),
        name="last",
        **params(4 * rows * n * width * width, 4 * n * width * width + 16 * rows * width),
    )(me, *blocks, w_rec, w_sib, got, acco, accs, proj, side, side_sib, postc, read, ranks)


def prep_kernel(*refs, pop):
    packs, (pret_ref, post_ref) = refs[: 2 * pop], refs[2 * pop :]
    tp = packs[0].shape[0] - 2
    width = packs[0].shape[2]
    own = packs[:pop]
    for b in range(tp):
        cols = jnp.concatenate([p[b] for p in packs], 0)
        pret_ref[b * width : (b + 1) * width, :] = cols.astype(f32).T.astype(bf16)
    return own, post_ref


def prep_full_kernel(core_ref, *refs, pop):
    own, post_ref = prep_kernel(*refs, pop=pop)
    tp = own[0].shape[0] - 2
    core = core_ref[0]
    for d in range(2):
        for s in range(pop):
            at = (d * pop + s) * EP
            low, high = own[s][tp + d], own[s][tp + 1 - d]
            post_ref[at : at + EP, :] = jnp.where(core == 0, low.astype(f32), high.astype(f32)).astype(bf16)


def prep_call(core, packs, pop):
    blocks, _, width = packs[0].shape
    count = 2 * pop * EP
    sds = jax.ShapeDtypeStruct
    outs = [sds(((blocks - 2) * width, count), bf16), sds((count, width), bf16)]
    return pl.pallas_call(
        functools.partial(prep_full_kernel, pop=pop),
        grid_spec=pltpu.PrefetchScalarGridSpec(
            num_scalar_prefetch=1,
            grid=(1,),
            in_specs=[whole(p.shape) for p in packs],
            out_specs=[whole(o.shape) for o in outs],
        ),
        out_shape=outs,
        name="prep",
        **params(count * blocks * width, 4 * count * blocks * width),
    )(core, *packs)


def grad_kernel(place_ref, note_ref, pret_ref, post_ref, grad_ref, ret_ref, both_ref, *, tp, pop, plays):
    count = post_ref.shape[0]
    plane, core = place_ref[0], place_ref[1]

    @pl.when(pl.program_id(0) == 0)
    def _():
        notes = note_ref[...]
        wide = jnp.concatenate([notes] * (count // 128), 1) if count > 128 else notes
        row = lax.broadcasted_iota(i32, wide.shape, 0)
        lane = lax.broadcasted_iota(i32, wide.shape, 1)
        source = row >> 1
        kind = row & 1
        place = source // tp if tp & (tp - 1) else source >> (tp.bit_length() - 1)
        unit = source & 1
        group = lane >> 4
        want_plane = plane ^ (group & (pop - 1))
        want_core = core ^ (group >> (pop.bit_length() - 1))
        match = (place == want_plane) & (unit == want_core)
        total = jnp.sum(jnp.where(match & (kind == 0), wide, 0.0), 0, keepdims=True)
        lead = (source & (tp - 1)) < 2
        rank = jnp.sum(jnp.where(match & (kind == 1) & lead, wide, 0.0), 0, keepdims=True)
        fitness = rank / (count - 1) - 0.5 + total / plays
        fitness = fitness * ((12.0 / count) ** 0.5)
        diag = lax.broadcasted_iota(i32, (count, count), 0) == lax.broadcasted_iota(i32, (count, count), 1)
        column = jnp.sum(jnp.where(diag, fitness, 0.0), 1, keepdims=True)
        weighted = post_ref[...].astype(f32) * column
        high = weighted.astype(bf16)
        both_ref[:count, :] = high
        both_ref[count:, :] = (weighted - high.astype(f32)).astype(bf16)
        row = lax.broadcasted_iota(i32, notes.shape, 0)
        lane = lax.broadcasted_iota(i32, notes.shape, 1)
        source = row >> 1
        place = source >> (tp.bit_length() - 1)
        mine = (place == plane) & ((source & 1) == (lane >> 4)) & ((row & 1) == 0)
        ret_ref[...] = jnp.sum(jnp.where(mine, notes, 0.0), 0, keepdims=True) / plays

    pret = pret_ref[...]
    grad_ref[...] = dot(jnp.concatenate([pret, pret], 1), both_ref[...]).astype(bf16)


def grad_call(place, notes, pret, post, tp, pop, plays):
    inputs, count = pret.shape
    width = post.shape[1]
    block = min(512, inputs)
    return pl.pallas_call(
        functools.partial(grad_kernel, tp=tp, pop=pop, plays=plays),
        grid_spec=pltpu.PrefetchScalarGridSpec(
            num_scalar_prefetch=1,
            grid=(inputs // block,),
            in_specs=[whole(notes.shape), pl.BlockSpec((block, count), lambda i, _: (i, 0)), whole(post.shape)],
            out_specs=[pl.BlockSpec((block, width), lambda i, _: (i, 0)), whole((1, 128))],
            scratch_shapes=[pltpu.VMEM((2 * count, width), bf16)],
        ),
        out_shape=[jax.ShapeDtypeStruct((inputs, width), bf16), jax.ShapeDtypeStruct((1, 128), f32)],
        name="grad",
        **params(4 * inputs * count * width, 2 * inputs * (count + width)),
    )(place, notes, pret, post)


def swap(x, axis, mask):
    return lax.ppermute(x, axis, [(i, i ^ mask) for i in range(lax.axis_size(axis))])


def shards(
    in_spikes, w_in, w_rec, leak_rate, neuron_bias, readout, pert_table, pert_idx, member_ranks
):
    steps, epis, inputs = in_spikes.shape
    members = pert_idx.shape[0]
    tp, pop = lax.axis_size("tp"), lax.axis_size("pop")
    assert steps == 4 and epis < EP and members == 2 * EP
    me, plane = lax.axis_index("tp"), lax.axis_index("pop")
    at = me[None].astype(i32)
    place = jnp.stack([plane, me & 1]).astype(i32)

    w_sib = swap(w_rec, "tp", 1)
    side, load, post_loc = drive_call(
        in_spikes, w_in, neuron_bias[None], leak_rate[None], readout[None], pert_table, pert_idx, tp
    )
    side_sib = swap(side, "tp", 1)
    got = lax.all_to_all(load, "tp", 0, 0)
    base_out, proj1 = base_call(got, w_rec, side)
    base = lax.all_to_all(base_out, "tp", 0, 0)
    s2o, s2s, acco, accs, postc, read = step2_call(at, base, got, w_rec, w_sib, proj1, side, side_sib, epis)

    far, order = [], []
    if tp == 8:
        xa, yb = swap(s2o, "tp", 2), swap(s2s, "tp", 4)
        xb, ya = swap(s2s, "tp", 2), swap(s2o, "tp", 4)
        far, order = [xa, yb, xb, ya], [2, 5, 3, 4]
        end, end_order = [swap(xa, "tp", 4), swap(yb, "tp", 2)], [6, 7]
    else:
        for mask in range(2, tp, 2):
            far += [swap(s2o, "tp", mask), swap(s2s, "tp", mask)]
            order += [mask, mask + 1]
        far, end, order, end_order = far[:-2], far[-2:], order[:-2], order[-2:]
    acco, accs, proj, pack = part_call(at, [s2o, s2s], [0, 1], w_rec, w_sib, got, acco, accs, None, post_loc)
    packs = [pack] + [swap(pack, "pop", s) for s in range(1, pop)]
    packs += [swap(p, "tp", 1) for p in packs]
    acco, accs, proj = part_call(at, far, order, w_rec, w_sib, got, acco, accs, proj)
    notes = last_call(
        at, end, end_order, w_rec, w_sib, got, acco, accs, proj, side, side_sib, postc, read,
        member_ranks[:, None], epis, pop * tp,
    )
    notes = lax.all_to_all(notes, ("pop", "tp"), 0, 0, tiled=True)
    pret, post_all = prep_call(place[1:], packs, pop)
    grad, returns = grad_call(place, notes, pret, post_all, tp, pop, epis * steps)
    return (returns[0, :members], grad)


def solution(mesh):
    placed = (
        P(),
        P(None, "tp"),
        P(None, "tp"),
        P("tp"),
        P("tp"),
        P("tp"),
        P(None, "tp"),
        P("pop", None),
        P("pop"),
    )
    return jax.shard_map(
        shards, mesh=mesh, in_specs=placed, out_specs=(P("pop"), P(None, "tp")), check_vma=False
    )
```

time: 499 us -> 102 us (0.20)
  waiting for transfers between devices: 339 us -> 18.8 us
  blocking collectives: 87 us -> 13 us
  matrix products: 34 us -> 0 us
  Pallas kernels: 0 us -> 28.9 us
  starting transfers between devices: 0.38 us -> 22.3 us
  other arithmetic: 13.3 us -> 0.08 us
  between operations: 14 us -> 0.79 us
  local copies, waits for them, and re-layouts: 11 us -> 17 us
    psum x1 -> x0, waiting for transfers between devices: 291 us -> none  [shards(): grad_total = lax.psum(partial_grad, 'pop')]
    psum x4 -> x0, blocking collectives: 87 us -> none  [the longest x3 73.9 us: shards(): projection = lax.psum(partial_proj, 'tp')]
    all_gather x4 -> x0, waiting for transfers between devices: 47.1 us -> none  [the longest x3 24.8 us: shards(): lax.all_gather(flat_spikes, 'tp', axis=1, tiled=True)]
    dot_general x12 -> x0, matrix products: 34 us -> none  [the longest x3 21.4 us: shards(): jnp.dot(lax.all_gather(flat_spikes, 'tp', axis=1, tiled=True), w_rec, pre...]
    pallas_call x0 -> x8, Pallas kernels: none -> 28.9 us  [the longest x1 8.83 us: step2_call(): pl.pallas_call(functools.partial(step2_kernel, epis=epis), grid_spec=spec...]
    unnamed x12 -> x40, local copies, waits for them, and re-layouts: 0.03 us -> 15.2 us
    ppermute x0 -> x15, starting transfers between devices: none -> 13.9 us  [swap(): lax.ppermute(x, axis, [(i, i ^ mask) for i in range(lax.axis_size(axis))])]
    all_to_all x0 -> x1, blocking collectives: none -> 13 us  [shards(): got = lax.all_to_all(load, 'tp', 0, 0)]
  transfers between devices with their start and end apart: 5 -> 17, of which waited for: 5 -> 6; matrix products, arithmetic and copies ran while one was open for 4% -> 4% of each run, Pallas kernels for 0% -> 15%
where the time goes in v2:
time: 102 us; the launch traced here: 101 us
  Pallas kernels  28.9 us (28%)
  starting transfers between devices  22.3 us (22%)
  waiting for transfers between devices  18.8 us (18%)
  local copies, waits for them, and re-layouts  17 us (17%)
  blocking collectives  13 us (13%)
    unnamed x40, local copies, waits for them, and re-layouts  15.2 us
    ppermute x15, starting transfers between devices, swap(): lax.ppermute(x, axis, [(i, i ^ mask) for i in range(lax.axis_size(axis))])  13.9 us
    all_to_all x1, blocking collectives, shards(): got = lax.all_to_all(load, 'tp', 0, 0)  13 us
    pallas_call x1, Pallas kernels, step2_call(): pl.pallas_call(functools.partial(step2_kernel, epis=epis), grid_spec=spec...  8.83 us
    ppermute x15, waiting for transfers between devices, swap(): lax.ppermute(x, axis, [(i, i ^ mask) for i in range(lax.axis_size(axis))])  7.84 us
    pallas_call x2, Pallas kernels, part_call(): pl.pallas_call(functools.partial(part_kernel, count=n, first=first, packs...  6.26 us
    all_to_all x1, waiting for transfers between devices, shards(): notes = lax.all_to_all(notes, ('pop', 'tp'), 0, 0, tiled=True)  5.52 us
    all_to_all x1, waiting for transfers between devices, shards(): base = lax.all_to_all(base_out, 'tp', 0, 0)  5.43 us
  transfers between devices with their start and end apart: 17, of which 6 were waited for; matrix products, arithmetic and copies ran while one was open for 4% of the time, Pallas kernels for 15%

profile of v2, /device:TPU:0, one launch (start us, length us, event | category | flops | bytes accessed | tf_op | source)
XLA Modules:
  0.0 100.9 jit_solution(2100160324481955797)
XLA Ops:
  1.1 1.8 %copy.11.spk_ref = s32[4,15,4096]{2,1,0:T(8,128)S(1)} copy(s32[4,15,4096]{2,0,1:T(4,128)} %param.9) | data formatting | bytes 1966080 | tf_op args[0]
  3.7 2.3 %copy-done.5 = bf16[4096,512]{1,0:T(8,128)(2,1)S(1)} copy-done((bf16[4096,512]{1,0:T(8,128)(2,1)S(1)}, bf16[4096,512]{1,0:T(8,128)(2,1)}, u32[]{:S(2)}) %copy-start.5) | copy-done | bytes 4194328
  9.2 1.6 %drive.1 = (f32[72,512]{1,0:T(8,128)S(1)}, bf16[8,48,512]{2,1,0:T(8,128)(2,1)S(1)}, bf16[2,16,512]{2,1,0:T(8,128)(2,1)S(1)}) custom-call(s32[4,15,4096]{2,1,0:T(8,128)S(1)} %copy.11.spk_ref, bf16[4096,512]{1,0:T(8,128)(2,1)S(1)} %copy-done.5, f32[1,512]{1,0:T(1,128)S(1)} %bitcast.12, f32[1,512]{1,0:T(1,128)S(1)} %bitcast.13, f32[1,512]{1,0:T(1,128)S(1)} %bitcast.14, ...), custom_call_target="tpu_custom_call" | custom-call | flops 268435456 | bytes 5242880 | tf_op jit(solution)/shard_map/drive/pallas_call | solution.py:86
  10.8 13.0 %all_to_all.21.s0_ref.pre_ref.post_ref.refs_4_.refs_8_.refs_6_ = bf16[8,48,512]{2,1,0:T(8,128)(2,1)S(1)} all-to-all(bf16[8,48,512]{2,1,0:T(8,128)(2,1)S(1)} %get-tuple-element.24), channel_id=1, replica_groups=mesh['pop'=4,'tp'=8] {'tp'}, dimensions={0} | all-to-all | bytes 786432 | tf_op jit(solution)/shard_map/all_to_all | solution.py:530
  23.8 2.3 %base.1 = (f32[8,16,512]{2,1,0:T(8,128)}, f32[16,16]{1,0:T(8,128)S(1)}) custom-call(bf16[8,48,512]{2,1,0:T(8,128)(2,1)S(1)} %all_to_all.21.s0_ref.pre_ref.post_ref.refs_4_.refs_8_.refs_6_, bf16[8,48,512]{2,1,0:T(8,128)(2,1)S(1)} %all_to_all.21.s0_ref.pre_ref.post_ref.refs_4_.refs_8_.refs_6_, bf16[4096,512]{1,0:T(8,128)(2,1)S(1)} %copy-done, ...), custom_call_target="tpu_custom_call" | custom-call | flops 67108864 | bytes 4194304 | tf_op jit(solution)/shard_map/base/pallas_call | solution.py:134
  26.1 3.4 %all-to-all-start.1 = ((f32[8,16,512]{2,1,0:T(8,128)}), f32[8,16,512]{2,1,0:T(8,128)S(1)}, u32[]{:S(2)}, u32[]{:S(2)}) async-start(f32[8,16,512]{2,1,0:T(8,128)} %get-tuple-element.26), calls=%async_computation.1 | async-start | bytes 524288 | tf_op jit(solution)/shard_map/all_to_all | solution.py:532
  30.9 5.4 %all-to-all-done.1.base_ref = f32[8,16,512]{2,1,0:T(8,128)S(1)} async-done(((f32[8,16,512]{2,1,0:T(8,128)}), f32[8,16,512]{2,1,0:T(8,128)S(1)}, u32[]{:S(2)}, u32[]{:S(2)}) %all-to-all-start.1) | async-done | bytes 262176 | tf_op jit(solution)/shard_map/all_to_all | solution.py:532
  36.4 2.2 %copy-done.1 = bf16[4096,512]{1,0:T(8,128)(2,1)S(1)} copy-done((bf16[4096,512]{1,0:T(8,128)(2,1)S(1)}, bf16[4096,512]{1,0:T(8,128)(2,1)}, u32[]{:S(2)}) %copy-start.1) | copy-done | bytes 4194328
  38.5 8.8 %step2.1 = (bf16[240,512]{1,0:T(8,128)(2,1)S(1)}, bf16[240,512]{1,0:T(8,128)(2,1)S(1)}, f32[240,512]{1,0:T(8,128)S(1)}, f32[240,512]{1,0:T(8,128)S(1)}, bf16[2,1...) custom-call(s32[1]{0:T(128)} %bitcast.2.me_ref, f32[8,16,512]{2,1,0:T(8,128)S(1)} %all-to-all-done.1.base_ref, ...), custom_call_target="tpu_custom_call" | custom-call | flops 2013265920 | bytes 8388608 | tf_op jit(solution)/shard_map/step2/pallas_call | solution.py:243
  49.1 2.6 %part.2 = (f32[240,512]{1,0:T(8,128)S(1)}, f32[240,512]{1,0:T(8,128)S(1)}, f32[240,128]{1,0:T(8,128)S(1)}, bf16[10,16,512]{2,1,0:T(8,128)(2,1)}) custom-call(s32[1]{0:T(128)} %bitcast.2.me_ref, bf16[240,512]{1,0:T(8,128)(2,1)S(1)} %get-tuple-element.28.refs_0_, bf16[240,512]{1,0:T(8,128)(2,1)S(1)} %get-tuple-element.29.refs_1_, ...), custom_call_target="tpu_custom_call" | custom-call | flops 503316480 | bytes 4063232 | tf_op jit(solution)/shard_map/part/pallas_call | solution.py:335
  52.4 1.6 %collective-permute-start.8 = (bf16[10,16,512]{2,1,0:T(8,128)(2,1)}, bf16[10,16,512]{2,1,0:T(8,128)(2,1)S(1)}, u32[]{:S(2)}, u32[]{:S(2)}) collective-permute-start(bf16[10,16,512]{2,1,0:T(8,128)(2,1)} %get-tuple-element.41.refs_0_), channel_id=1, source_target_pairs={{0,8},{8,0},{16,24},{24,16},{1,9},{9,1},{17,25},{25,17},{2,10},{10... | collective-permute-start | bytes 491528 | tf_op jit(solution)/shard_map/ppermute | solution.py:511
  54.5 2.6 %collective-permute-start.9 = (bf16[10,16,512]{2,1,0:T(8,128)(2,1)}, bf16[10,16,512]{2,1,0:T(8,128)(2,1)S(1)}, u32[]{:S(2)}, u32[]{:S(2)}) collective-permute-start(bf16[10,16,512]{2,1,0:T(8,128)(2,1)} %get-tuple-element.41.refs_0_), channel_id=1, source_target_pairs={{0,16},{8,24},{16,0},{24,8},{1,17},{9,25},{17,1},{25,9},{2,18},{10... | collective-permute-start | bytes 491528 | tf_op jit(solution)/shard_map/ppermute | solution.py:511
  57.1 1.4 %collective-permute-start.6 = (bf16[240,512]{1,0:T(8,128)(2,1)S(1)}, bf16[240,512]{1,0:T(8,128)(2,1)S(1)}, u32[]{:S(2)}, u32[]{:S(2)}) collective-permute-start(bf16[240,512]{1,0:T(8,128)(2,1)S(1)} %get-tuple-element.29.refs_1_), channel_id=1, source_target_pairs={{0,2},{1,3},{2,0},{3,1},{4,6},{5,7},{6,4},{7,5},{8,10},{9,11},{10,... | collective-permute-start | bytes 737288 | tf_op jit(solution)/shard_map/ppermute | solution.py:511
  58.6 2.4 %collective-permute-done.8.refs_1_ = bf16[10,16,512]{2,1,0:T(8,128)(2,1)S(1)} collective-permute-done((bf16[10,16,512]{2,1,0:T(8,128)(2,1)}, bf16[10,16,512]{2,1,0:T(8,128)(2,1)S(1)}, u32[]{:S(2)}, u32[]{:S(2)}) %collective-permute-start.8) | collective-permute-done | bytes 163872 | tf_op jit(solution)/shard_map/ppermute | solution.py:511
  61.0 2.0 %collective-permute-start.3 = (bf16[240,512]{1,0:T(8,128)(2,1)S(1)}, bf16[240,512]{1,0:T(8,128)(2,1)S(1)}, u32[]{:S(2)}, u32[]{:S(2)}) collective-permute-start(bf16[240,512]{1,0:T(8,128)(2,1)S(1)} %collective-permute-done.2.refs_0_), channel_id=1, source_target_pairs={{0,4},{1,5},{2,6},{3,7},{4,0},{5,1},{6,2},{7,3},{8,12},{9,13},{10,... | collective-permute-start | bytes 737288 | tf_op jit(solution)/shard_map/ppermute | solution.py:511
  64.4 2.3 %collective-permute-start.10 = (bf16[10,16,512]{2,1,0:T(8,128)(2,1)}, bf16[10,16,512]{2,1,0:T(8,128)(2,1)}, u32[]{:S(2)}, u32[]{:S(2)}) collective-permute-start(bf16[10,16,512]{2,1,0:T(8,128)(2,1)} %get-tuple-element.41.refs_0_), channel_id=1, source_target_pairs={{0,24},{8,16},{16,8},{24,0},{1,25},{9,17},{17,9},{25,1},{2,26},{10... | collective-permute-start | bytes 491528 | tf_op jit(solution)/shard_map/ppermute | solution.py:511
  68.9 3.0 %collective-permute-done.10.refs_3_ = bf16[10,16,512]{2,1,0:T(8,128)(2,1)} collective-permute-done((bf16[10,16,512]{2,1,0:T(8,128)(2,1)}, bf16[10,16,512]{2,1,0:T(8,128)(2,1)}, u32[]{:S(2)}, u32[]{:S(2)}) %collective-permute-start.10) | collective-permute-done | bytes 163872 | tf_op jit(solution)/shard_map/ppermute | solution.py:511
  72.9 2.2 %copy-done.3 = bf16[4096,512]{1,0:T(8,128)(2,1)S(1)} copy-done((bf16[4096,512]{1,0:T(8,128)(2,1)S(1)}, bf16[4096,512]{1,0:T(8,128)(2,1)}, u32[]{:S(2)}) %copy-start.3) | copy-done | bytes 4194328
  76.0 3.7 %part.3 = (f32[240,512]{1,0:T(8,128)S(1)}, f32[240,512]{1,0:T(8,128)S(1)}, f32[240,128]{1,0:T(8,128)S(1)}) custom-call(s32[1]{0:T(128)} %bitcast.2.me_ref, bf16[240,512]{1,0:T(8,128)(2,1)S(1)} %collective-permute-done.2.refs_0_, bf16[240,512]{1,0:T(8,128)(2,1)S(1)} %collective-permute-done.4.refs_1_, bf16[240,512]{1,0:T(8,128)(2,1)S(1)} %collective-permute-done.6.refs_2_, ...), custom_call_target="tpu_custom_call" | custom-call | flops 1006632960 | bytes 6160384 | tf_op jit(solution)/shard_map/part/pallas_call | solution.py:335
  79.8 3.0 %last.1 = f32[64,128]{1,0:T(8,128)} custom-call(s32[1]{0:T(128)} %bitcast.2.me_ref, bf16[240,512]{1,0:T(8,128)(2,1)S(1)} %collective-permute-done.3.refs_0_, bf16[240,512]{1,0:T(8,128)(2,1)} %collective-permute-done.5.refs_1_, bf16[4096,512]{1,0:T(8,128)(2,1)S(1)} %copy-done.4, bf16[4096,512]{1,0:T(8,128)(2,1)} %collective-permute-done.ws_ref.refs_3_.refs_5_, ...), custom_call_target="tpu_custom_call" | custom-call | flops 503316480 | bytes 4063232 | tf_op jit(solution)/shard_map/last/pallas_call | solution.py:401
  82.7 5.0 %all-to-all-start.2 = ((f32[32,2,128]{2,1,0:T(2,128)}), f32[32,2,128]{2,1,0:T(2,128)S(1)}, u32[]{:S(2)}, u32[]{:S(2)}) async-start(f32[32,2,128]{2,1,0:T(2,128)} %bitcast.7), calls=%async_computation.2 | async-start | bytes 65536 | tf_op jit(solution)/shard_map/all_to_all | solution.py:554
  87.9 1.6 %prep.1 = (bf16[4096,128]{1,0:T(8,128)(2,1)S(1)}, bf16[128,512]{1,0:T(8,128)(2,1)S(1)}) custom-call(s32[1]{0:T(128)} %bitcast.1.core_ref, bf16[10,16,512]{2,1,0:T(8,128)(2,1)} %get-tuple-element.41.refs_0_, bf16[10,16,512]{2,1,0:T(8,128)(2,1)S(1)} %collective-permute-done.8.refs_1_, bf16[10,16,512]{2,1,0:T(8,128)(2,1)S(1)} %copy-done.8, ...), custom_call_target="tpu_custom_call" | custom-call | flops 655360 | bytes 2621440 | tf_op jit(solution)/shard_map/prep/pallas_call | solution.py:437
  89.5 5.5 %all-to-all-done.2 = f32[32,2,128]{2,1,0:T(2,128)S(1)} async-done(((f32[32,2,128]{2,1,0:T(2,128)}), f32[32,2,128]{2,1,0:T(2,128)S(1)}, u32[]{:S(2)}, u32[]{:S(2)}) %all-to-all-start.2) | async-done | bytes 32800 | tf_op jit(solution)/shard_map/all_to_all | solution.py:554
  95.0 5.4 %grad.1 = (bf16[4096,512]{1,0:T(8,128)(2,1)}, f32[1,128]{1,0:T(1,128)S(1)}) custom-call(s32[2]{0:T(128)S(1)} %pad_add_fusion.place_ref, f32[64,128]{1,0:T(8,128)S(1)} %bitcast.11, bf16[4096,128]{1,0:T(8,128)(2,1)S(1)} %get-tuple-element.42.pret_ref, bf16[128,512]{1,0:T(8,128)(2,1)S(1)} %get-tuple-element.43.post_ref), custom_call_target="tpu_custom_call" | custom-call | flops 1073741824 | bytes 5242880 | tf_op jit(solution)/shard_map/grad/pallas_call | solution.py:495
  (63 shorter events, 15.0 us)
Async XLA Ops:
  0.6 35.7 %collective-permute-start = (bf16[4096,512]{1,0:T(8,128)(2,1)}, bf16[4096,512]{1,0:T(8,128)(2,1)}, u32[]{:S(2)}, u32[]{:S(2)}) collective-permute-start(bf16[4096,512]{1,0:T(8,128)(2,1)} %refs_2_.3), channel_id=1, source_target_pairs={{0,1},{1,0},{2,3},{3,2},{4,5},{5,4},{6,7},{7,6},{8,9},{9,8},{10,11... | collective-permute-start | bytes 12582920 | tf_op jit(solution)/shard_map/ppermute | solution.py:511
  3.7 20.1 %copy-start = (bf16[4096,512]{1,0:T(8,128)(2,1)S(1)}, bf16[4096,512]{1,0:T(8,128)(2,1)}, u32[]{:S(2)}) copy-start(bf16[4096,512]{1,0:T(8,128)(2,1)} %refs_2_.3) | copy-start | bytes 12582916
  26.1 10.3 %all-to-all-start.1 = ((f32[8,16,512]{2,1,0:T(8,128)}), f32[8,16,512]{2,1,0:T(8,128)S(1)}, u32[]{:S(2)}, u32[]{:S(2)}) async-start(f32[8,16,512]{2,1,0:T(8,128)} %get-tuple-element.26), calls=%async_computation.1 | async-start | bytes 524288 | tf_op jit(solution)/shard_map/all_to_all | solution.py:532
  29.5 1.4 %collective-permute-start.1 = (f32[72,512]{1,0:T(8,128)S(1)}, f32[72,512]{1,0:T(8,128)S(1)}, u32[]{:S(2)}, u32[]{:S(2)}) collective-permute-start(f32[72,512]{1,0:T(8,128)S(1)} %get-tuple-element.25.side_ref.so_ref.refs_8_), channel_id=1, source_target_pairs={{0,1},{1,0},{2,3},{3,2},{4,5},{5,4},{6,7},{7,6},{8,9},{9,8},{10,11... | collective-permute-start | bytes 442376 | tf_op jit(solution)/shard_map/ppermute | solution.py:511
  38.5 10.6 %copy-start.2 = (bf16[4096,512]{1,0:T(8,128)(2,1)S(1)}, bf16[4096,512]{1,0:T(8,128)(2,1)}, u32[]{:S(2)}) copy-start(bf16[4096,512]{1,0:T(8,128)(2,1)} %refs_2_.3) | copy-start | bytes 12582916
  48.6 12.4 %collective-permute-start.2 = (bf16[240,512]{1,0:T(8,128)(2,1)S(1)}, bf16[240,512]{1,0:T(8,128)(2,1)S(1)}, u32[]{:S(2)}, u32[]{:S(2)}) collective-permute-start(bf16[240,512]{1,0:T(8,128)(2,1)S(1)} %get-tuple-element.28.refs_0_), channel_id=1, source_target_pairs={{0,2},{1,3},{2,0},{3,1},{4,6},{5,7},{6,4},{7,5},{8,10},{9,11},{10,... | collective-permute-start | bytes 737288 | tf_op jit(solution)/shard_map/ppermute | solution.py:511
  52.4 8.6 %collective-permute-start.8 = (bf16[10,16,512]{2,1,0:T(8,128)(2,1)}, bf16[10,16,512]{2,1,0:T(8,128)(2,1)S(1)}, u32[]{:S(2)}, u32[]{:S(2)}) collective-permute-start(bf16[10,16,512]{2,1,0:T(8,128)(2,1)} %get-tuple-element.41.refs_0_), channel_id=1, source_target_pairs={{0,8},{8,0},{16,24},{24,16},{1,9},{9,1},{17,25},{25,17},{2,10},{10... | collective-permute-start | bytes 491528 | tf_op jit(solution)/shard_map/ppermute | solution.py:511
  54.0 12.7 %collective-permute-start.4 = (bf16[240,512]{1,0:T(8,128)(2,1)S(1)}, bf16[240,512]{1,0:T(8,128)(2,1)S(1)}, u32[]{:S(2)}, u32[]{:S(2)}) collective-permute-start(bf16[240,512]{1,0:T(8,128)(2,1)S(1)} %get-tuple-element.29.refs_1_), channel_id=1, source_target_pairs={{0,4},{1,5},{2,6},{3,7},{4,0},{5,1},{6,2},{7,3},{8,12},{9,13},{10,... | collective-permute-start | bytes 737288 | tf_op jit(solution)/shard_map/ppermute | solution.py:511
  54.5 9.8 %collective-permute-start.9 = (bf16[10,16,512]{2,1,0:T(8,128)(2,1)}, bf16[10,16,512]{2,1,0:T(8,128)(2,1)S(1)}, u32[]{:S(2)}, u32[]{:S(2)}) collective-permute-start(bf16[10,16,512]{2,1,0:T(8,128)(2,1)} %get-tuple-element.41.refs_0_), channel_id=1, source_target_pairs={{0,16},{8,24},{16,0},{24,8},{1,17},{9,25},{17,1},{25,9},{2,18},{10... | collective-permute-start | bytes 491528 | tf_op jit(solution)/shard_map/ppermute | solution.py:511
  57.1 14.8 %collective-permute-start.6 = (bf16[240,512]{1,0:T(8,128)(2,1)S(1)}, bf16[240,512]{1,0:T(8,128)(2,1)S(1)}, u32[]{:S(2)}, u32[]{:S(2)}) collective-permute-start(bf16[240,512]{1,0:T(8,128)(2,1)S(1)} %get-tuple-element.29.refs_1_), channel_id=1, source_target_pairs={{0,2},{1,3},{2,0},{3,1},{4,6},{5,7},{6,4},{7,5},{8,10},{9,11},{10,... | collective-permute-start | bytes 737288 | tf_op jit(solution)/shard_map/ppermute | solution.py:511
  61.0 11.4 %collective-permute-start.7 = (bf16[240,512]{1,0:T(8,128)(2,1)S(1)}, bf16[240,512]{1,0:T(8,128)(2,1)S(1)}, u32[]{:S(2)}, u32[]{:S(2)}) collective-permute-start(bf16[240,512]{1,0:T(8,128)(2,1)S(1)} %get-tuple-element.28.refs_0_), channel_id=1, source_target_pairs={{0,4},{1,5},{2,6},{3,7},{4,0},{5,1},{6,2},{7,3},{8,12},{9,13},{10,... | collective-permute-start | bytes 737288 | tf_op jit(solution)/shard_map/ppermute | solution.py:511
  61.0 11.5 %collective-permute-start.3 = (bf16[240,512]{1,0:T(8,128)(2,1)S(1)}, bf16[240,512]{1,0:T(8,128)(2,1)S(1)}, u32[]{:S(2)}, u32[]{:S(2)}) collective-permute-start(bf16[240,512]{1,0:T(8,128)(2,1)S(1)} %collective-permute-done.2.refs_0_), channel_id=1, source_target_pairs={{0,4},{1,5},{2,6},{3,7},{4,0},{5,1},{6,2},{7,3},{8,12},{9,13},{10,... | collective-permute-start | bytes 737288 | tf_op jit(solution)/shard_map/ppermute | solution.py:511
  64.4 7.5 %collective-permute-start.10 = (bf16[10,16,512]{2,1,0:T(8,128)(2,1)}, bf16[10,16,512]{2,1,0:T(8,128)(2,1)}, u32[]{:S(2)}, u32[]{:S(2)}) collective-permute-start(bf16[10,16,512]{2,1,0:T(8,128)(2,1)} %get-tuple-element.41.refs_0_), channel_id=1, source_target_pairs={{0,24},{8,16},{16,8},{24,0},{1,25},{9,17},{17,9},{25,1},{2,26},{10... | collective-permute-start | bytes 491528 | tf_op jit(solution)/shard_map/ppermute | solution.py:511
  66.7 13.0 %collective-permute-start.5 = (bf16[240,512]{1,0:T(8,128)(2,1)S(1)}, bf16[240,512]{1,0:T(8,128)(2,1)}, u32[]{:S(2)}, u32[]{:S(2)}) collective-permute-start(bf16[240,512]{1,0:T(8,128)(2,1)S(1)} %collective-permute-done.4.refs_1_), channel_id=1, source_target_pairs={{0,2},{1,3},{2,0},{3,1},{4,6},{5,7},{6,4},{7,5},{8,10},{9,11},{10,... | collective-permute-start | bytes 737288 | tf_op jit(solution)/shard_map/ppermute | solution.py:511
  71.9 15.9 %collective-permute-start.11 = (bf16[10,16,512]{2,1,0:T(8,128)(2,1)}, bf16[10,16,512]{2,1,0:T(8,128)(2,1)}, u32[]{:S(2)}, u32[]{:S(2)}) collective-permute-start(bf16[10,16,512]{2,1,0:T(8,128)(2,1)} %get-tuple-element.41.refs_0_), channel_id=1, source_target_pairs={{0,1},{1,0},{2,3},{3,2},{4,5},{5,4},{6,7},{7,6},{8,9},{9,8},{10,11... | collective-permute-start | bytes 491528 | tf_op jit(solution)/shard_map/ppermute | solution.py:511
  71.9 15.9 %collective-permute-start.12 = (bf16[10,16,512]{2,1,0:T(8,128)(2,1)S(1)}, bf16[10,16,512]{2,1,0:T(8,128)(2,1)S(1)}, u32[]{:S(2)}, u32[]{:S(2)}) collective-permute-start(bf16[10,16,512]{2,1,0:T(8,128)(2,1)S(1)} %collective-permute-done.8.refs_1_), channel_id=1, source_target_pairs={{0,1},{1,0},{2,3},{3,2},{4,5},{5,4},{6,7},{7,6},{8,9},{9,8},{10,11... | collective-permute-start | bytes 491528 | tf_op jit(solution)/shard_map/ppermute | solution.py:511
  72.4 15.4 %collective-permute-start.13 = (bf16[10,16,512]{2,1,0:T(8,128)(2,1)}, bf16[10,16,512]{2,1,0:T(8,128)(2,1)}, u32[]{:S(2)}, u32[]{:S(2)}) collective-permute-start(bf16[10,16,512]{2,1,0:T(8,128)(2,1)} %copy-done.7), channel_id=1, source_target_pairs={{0,1},{1,0},{2,3},{3,2},{4,5},{5,4},{6,7},{7,6},{8,9},{9,8},{10,11... | collective-permute-start | bytes 491528 | tf_op jit(solution)/shard_map/ppermute | solution.py:511
  72.5 15.3 %collective-permute-start.14 = (bf16[10,16,512]{2,1,0:T(8,128)(2,1)}, bf16[10,16,512]{2,1,0:T(8,128)(2,1)}, u32[]{:S(2)}, u32[]{:S(2)}) collective-permute-start(bf16[10,16,512]{2,1,0:T(8,128)(2,1)} %collective-permute-done.10.refs_3_), channel_id=1, source_target_pairs={{0,1},{1,0},{2,3},{3,2},{4,5},{5,4},{6,7},{7,6},{8,9},{9,8},{10,11... | collective-permute-start | bytes 491528 | tf_op jit(solution)/shard_map/ppermute | solution.py:511
  76.0 3.7 %copy-start.4 = (bf16[4096,512]{1,0:T(8,128)(2,1)S(1)}, bf16[4096,512]{1,0:T(8,128)(2,1)}, u32[]{:S(2)}) copy-start(bf16[4096,512]{1,0:T(8,128)(2,1)} %refs_2_.3) | copy-start | bytes 12582916
  76.0 3.7 %copy-start.11 = (s32[32,1]{1,0:T(8,128)S(1)}, s32[32,1]{1,0:T(8,128)}, u32[]{:S(2)}) copy-start(s32[32,1]{1,0:T(8,128)} %copy.13.refs_12_) | copy-start | bytes 388
  76.0 3.7 %copy-start.13 = (bf16[2,16,512]{2,1,0:T(8,128)(2,1)S(1)}, bf16[2,16,512]{2,1,0:T(8,128)(2,1)}, u32[]{:S(2)}) copy-start(bf16[2,16,512]{2,1,0:T(8,128)(2,1)} %copy-done.12) | copy-start | bytes 98308
  76.0 3.7 %copy-start.15 = (f32[16,128]{1,0:T(8,128)S(1)}, f32[16,128]{1,0:T(8,128)}, u32[]{:S(2)}) copy-start(f32[16,128]{1,0:T(8,128)} %copy-done.14) | copy-start | bytes 24580
  79.8 8.1 %copy-start.8 = (bf16[10,16,512]{2,1,0:T(8,128)(2,1)S(1)}, bf16[10,16,512]{2,1,0:T(8,128)(2,1)}, u32[]{:S(2)}) copy-start(bf16[10,16,512]{2,1,0:T(8,128)(2,1)} %copy-done.7) | copy-start | bytes 491524
  82.7 12.3 %all-to-all-start.2 = ((f32[32,2,128]{2,1,0:T(2,128)}), f32[32,2,128]{2,1,0:T(2,128)S(1)}, u32[]{:S(2)}, u32[]{:S(2)}) async-start(f32[32,2,128]{2,1,0:T(2,128)} %bitcast.7), calls=%async_computation.2 | async-start | bytes 65536 | tf_op jit(solution)/shard_map/all_to_all | solution.py:554
  (12 other events, 15.0 us)

commit v3 on v0

v3 whole, which is shorter than its diff:
```python
import functools

import jax
import jax.numpy as jnp
from jax import lax
from jax.experimental import pallas as pl
from jax.experimental.pallas import tpu as pltpu
from jax.sharding import PartitionSpec as P

sigma_scale = 0.01
f32 = jnp.float32
bf16 = jnp.bfloat16
i32 = jnp.int32
L_BASE = 48
L_STEP2 = 32
L_PART = 24
L_DRIVE = 58
L_LAST = 24
EP = 16


def spike(membrane):
    return (0.5 + 0.5 * jnp.tanh(2.0 * (membrane - 1.0))).astype(bf16)


def dot(a, b):
    return jnp.dot(a, b, preferred_element_type=f32)


def fold(x):
    parts = [x[:, i : i + 128] for i in range(0, x.shape[1], 128)]
    return functools.reduce(jnp.add, parts)


def params(mib, flops, nbytes):
    return dict(
        compiler_params=pltpu.CompilerParams(vmem_limit_bytes=mib * 2**20),
        cost_estimate=pl.CostEstimate(flops=flops, bytes_accessed=nbytes, transcendentals=0),
    )


VM = pl.BlockSpec(memory_space=pltpu.VMEM)
SM = pl.BlockSpec(memory_space=pltpu.SMEM)
HB = pl.BlockSpec(memory_space=pltpu.HBM)
sds = jax.ShapeDtypeStruct


def block_rows(b, width):
    return pl.ds(pl.multiple_of(b * width, width), width)


def drive_kernel(
    spk_hbm, win_hbm, bias_hbm, leak_hbm, read_hbm, table_hbm, idx_hbm,
    side_ref, load_ref, post_ref,
    spk, win, bias, leak, read, table, idx, acc_ref, sems,
):
    epis, steps, inputs = spk.shape
    tp = load_ref.shape[0]
    parts = 4
    depth = inputs // parts
    copies = []
    for k in range(parts):
        at = pl.ds(k * depth, depth)
        copies.append((spk_hbm.at[:, :, at], spk.at[:, :, at]))
        copies.append((win_hbm.at[at], win.at[at]))
    copies += [(table_hbm, table), (idx_hbm, idx), (bias_hbm, bias), (leak_hbm, leak), (read_hbm, read)]
    copies = [pltpu.make_async_copy(a, b, sems.at[n]) for n, (a, b) in enumerate(copies)]
    for copy in copies:
        copy.start()
    for k in range(parts):
        copies[2 * k].wait()
        copies[2 * k + 1].wait()
        at = slice(k * depth, (k + 1) * depth)
        x = spk[:, :, at].reshape(epis * steps, depth).astype(f32).astype(bf16)
        part = dot(x, win[at, :])
        total = part if k == 0 else total + part
    for copy in copies[2 * parts :]:
        copy.wait()
    total = total + bias[...]
    lanes = range(acc_ref.shape[0])
    for c in lanes:
        acc_ref[c] = total[:, c * 128 : (c + 1) * 128]
    blank = jnp.zeros((EP - epis, total.shape[1]), f32)
    for t in range(steps):
        drive = jnp.concatenate([acc_ref[c, pl.ds(t, epis, stride=steps), :] for c in lanes], 1)
        drive = jnp.concatenate([drive, blank], 0)
        side_ref[t * EP : (t + 1) * EP, :] = drive
        if t == 0:
            s0 = spike(drive).astype(f32)
            here = lax.broadcasted_iota(i32, s0.shape, 0) < epis
            s0 = jnp.where(here, s0, 0.0).astype(bf16)
            for j in range(tp):
                load_ref[j, :EP, :] = s0
    row = lax.broadcasted_iota(i32, (8, total.shape[1]), 0)
    side_ref[steps * EP :, :] = jnp.where(row == 0, leak[...], read[...])
    at = lax.broadcasted_iota(i32, (table.shape[0], idx.shape[1]), 0)
    pick = (((0,), (0,)), ((), ()))
    pre, post = (
        lax.dot_general(
            jnp.where(at == idx[n : n + 1, :], 1.0, 0.0).astype(bf16), table[...], pick, preferred_element_type=f32
        ).astype(bf16)
        for n in range(2)
    )
    for j in range(tp):
        own = slice((j % 2) * EP, (j % 2 + 1) * EP)
        load_ref[j, EP : 2 * EP, :] = pre[own]
        load_ref[j, 2 * EP :, :] = post[own]
    for c in range(2):
        post_ref[c] = post[c * EP : (c + 1) * EP]


def drive_call(in_spikes, w_in, bias, leak, read, table, idx, tp):
    steps, epis, inputs = in_spikes.shape
    width = w_in.shape[1]
    members = idx.shape[0]
    ins = [in_spikes.transpose(1, 0, 2), w_in, bias[None], leak[None], read[None], table, idx.T]
    return pl.pallas_call(
        drive_kernel,
        in_specs=[HB] * 7,
        out_specs=[VM] * 3,
        out_shape=[
            sds((steps * EP + 8, width), f32),
            sds((tp, 3 * EP, width), bf16),
            sds((2, EP, width), bf16),
        ],
        scratch_shapes=[pltpu.VMEM(x.shape, x.dtype) for x in ins]
        + [pltpu.VMEM((width // 128, steps * epis, 128), f32), pltpu.SemaphoreType.DMA((13,))],
        name="drive",
        **params(L_DRIVE, 2 * steps * EP * inputs * width, inputs * width * 2 + steps * EP * inputs * 4),
    )(*ins)


def base_kernel(got_ref, w_hbm, side_ref, out_ref, w_ref, sems):
    tp, _, width = got_ref.shape
    lead = side_ref.shape[0] - 8
    parts = 4
    depth = w_ref.shape[0] // parts
    copies = []
    for k in range(parts):
        at = pl.ds(k * depth, depth)
        copies.append(pltpu.make_async_copy(w_hbm.at[at], w_ref.at[at], sems.at[k]))
    for copy in copies:
        copy.start()
    mem0 = side_ref[0:EP, :]
    leak = side_ref[lead : lead + 1, :]
    base = leak * (mem0 - spike(mem0).astype(f32)) + side_ref[EP : 2 * EP, :]
    for k in range(parts):
        copies[k].wait()
        for j in range(k * tp // parts, (k + 1) * tp // parts):
            base += dot(got_ref[j, :EP, :], w_ref[j * width : (j + 1) * width, :])
    for i in range(tp):
        out_ref[i] = base


def base_call(got, w_rec, side):
    tp, _, width = got.shape
    return pl.pallas_call(
        base_kernel,
        in_specs=[VM, HB, VM],
        out_specs=VM,
        out_shape=sds((tp, EP, width), f32),
        scratch_shapes=[pltpu.VMEM(w_rec.shape, bf16), pltpu.SemaphoreType.DMA((4,))],
        name="base",
        **params(L_BASE, 2 * EP * tp * width * width, tp * width * width * 2),
    )(got, w_rec, side)


def proj_kernel(got_ref, post_ref, proj_ref, pack_ref):
    tp = got_ref.shape[0]
    proj = jnp.zeros((EP, EP), f32)
    for j in range(tp):
        pre = got_ref[j, EP : 2 * EP, :]
        proj += lax.dot_general(pre, got_ref[j, :EP, :], (((1,), (1,)), ((), ())), preferred_element_type=f32)
        pack_ref[j] = pre
    proj_ref[...] = sigma_scale * proj
    for c in range(2):
        pack_ref[tp + c] = post_ref[c]


def proj_call(got, post_loc):
    tp, _, width = got.shape
    return pl.pallas_call(
        proj_kernel,
        in_specs=[VM] * 2,
        out_specs=[VM] * 2,
        out_shape=[sds((EP, EP), f32), sds((tp + 2, EP, width), bf16)],
        name="proj",
        **params(8, 2 * EP * EP * tp * width, 4 * tp * EP * width),
    )(got, post_loc)


def step2_kernel(
    me_ref, base_ref, rows_ref, wo_hbm, ws_hbm, proj1_ref, so_ref, ss_ref, near_ref,
    s2o_ref, s2s_ref, memo_ref, mems_ref, s1c_ref,
    s1_ref, wo_ref, ws_ref, acco_ref, accs_ref, p2_ref, sems, *, epis,
):
    tp, _, width = base_ref.shape
    lead = so_ref.shape[0] - 8
    me = me_ref[0]

    def fetch(j):
        at = block_rows(j ^ me, width)
        return (
            pltpu.make_async_copy(wo_hbm.at[at], wo_ref.at[at], sems.at[0, j]),
            pltpu.make_async_copy(ws_hbm.at[at], ws_ref.at[at], sems.at[1, j]),
        )

    for j in range(tp):
        for copy in fetch(j):
            copy.start()

    def membrane1(b, e, post):
        return base_ref[b, e : e + 1, :] + proj1_ref[:, e : e + 1] * post

    p2_ref[...] = jnp.zeros_like(p2_ref)
    acco_ref[...] = jnp.zeros_like(acco_ref)
    accs_ref[...] = jnp.zeros_like(accs_ref)

    def rebuild(j):
        b = j ^ me
        pre = rows_ref[b, EP : 2 * EP, :].astype(f32)
        post = rows_ref[b, 2 * EP :, :].astype(f32)
        for e in range(epis):
            at = slice(e * EP, (e + 1) * EP)
            s1 = spike(membrane1(b, e, post))
            s1_ref[j, at, :] = s1
            p2_ref[at, :] += fold(s1.astype(f32) * pre)

    def multiply(j):
        for copy in fetch(j):
            copy.wait()
        at = block_rows(j ^ me, width)
        s1 = s1_ref[j]
        acco_ref[...] += dot(s1, wo_ref[at, :])
        accs_ref[...] += dot(s1, ws_ref[at, :])

    rebuild(0)

    def body(j, _):
        multiply(j)
        rebuild(j + 1)
        return 0

    lax.fori_loop(0, tp - 1, body, 0)
    multiply(tp - 1)
    proj2 = sigma_scale * jnp.sum(p2_ref[...], axis=1, keepdims=True)
    for h, side_ref, acc_ref, s2_ref, mem_ref in (
        (0, so_ref, acco_ref, s2o_ref, memo_ref),
        (1, ss_ref, accs_ref, s2s_ref, mems_ref),
    ):
        leak = side_ref[lead : lead + 1, :]
        post = rows_ref[h ^ me, 2 * EP :, :].astype(f32)
        for e in range(epis):
            at = slice(e * EP, (e + 1) * EP)
            s1 = s1_ref[h, at, :]
            s1c_ref[h, at, :] = s1
            mem = leak * (membrane1(h ^ me, e, post) - s1.astype(f32)) + side_ref[2 * EP + e : 2 * EP + e + 1, :]
            mem = mem + acc_ref[at, :] + proj2[at, :] * post
            mem_ref[at, :] = mem
            s2_ref[at, :] = spike(mem)


def step2_call(me, base, got, w_rec, w_sib, proj1, side, side_sib, near, epis):
    tp, _, width = base.shape
    n = epis * EP
    return pl.pallas_call(
        functools.partial(step2_kernel, epis=epis),
        in_specs=[SM, VM, VM, HB, HB, VM, VM, VM, HB],
        out_specs=[VM] * 5,
        out_shape=[
            sds((n, width), bf16), sds((n, width), bf16), sds((n, width), f32), sds((n, width), f32),
            sds((2, n, width), bf16),
        ],
        scratch_shapes=[
            pltpu.VMEM((tp, n, width), bf16),
            pltpu.VMEM(w_sib.shape, bf16),
            pltpu.VMEM(w_sib.shape, bf16),
            pltpu.VMEM((n, width), f32),
            pltpu.VMEM((n, width), f32),
            pltpu.VMEM((n, 128), f32),
            pltpu.SemaphoreType.DMA((2, tp)),
        ],
        name="step2",
        **params(L_STEP2, 4 * n * tp * width * width, 4 * tp * width * width),
    )(me, base, got, w_rec, w_sib, proj1, side, side_sib, near)


def fetch_blocks(order, me, wo_hbm, ws_hbm, w_ref, sems):
    copies = []
    for n, v in enumerate(order):
        at = block_rows(v ^ me, wo_hbm.shape[1])
        for h, hbm in ((0, wo_hbm), (1, ws_hbm)):
            copies.append(pltpu.make_async_copy(hbm.at[at], w_ref.at[h, n], sems.at[h, n]))
    for copy in copies:
        copy.start()
    return copies


def add_blocks(order, me, blocks, copies, w_ref, rows_ref, acco_ref, accs_ref, p_ref):
    for n, v in enumerate(order):
        copies[2 * n].wait()
        copies[2 * n + 1].wait()
        block = blocks[n][...]
        acco_ref[...] += dot(block, w_ref[0, n])
        accs_ref[...] += dot(block, w_ref[1, n])
        pre = rows_ref[v ^ me, EP : 2 * EP, :].astype(f32)
        for r in range(0, block.shape[0], EP):
            p_ref[r : r + EP, :] += fold(block[r : r + EP, :].astype(f32) * pre)


def own_kernel(
    me_ref, s2o_ref, s2s_ref, wo_hbm, ws_hbm, rows_ref, s1c_ref, memo_ref, mems_ref, so_ref, ss_ref, pack_ref, near_ref,
    acco_ref, accs_ref, p_ref, read_ref, pair_ref, w_ref, sems, *, epis,
):
    blocks = (s2o_ref, s2s_ref)
    width = wo_hbm.shape[1]
    lead = so_ref.shape[0] - 8
    me = me_ref[0]
    copies = fetch_blocks([0, 1], me, wo_hbm, ws_hbm, w_ref, sems)
    pair_ref[0] = pack_ref[...]
    pair_ref[1] = near_ref[...]
    p_ref[...] = jnp.zeros_like(p_ref)
    sums = jnp.zeros((EP, 128), f32)
    for h, side_ref, mem_ref, acc_ref in ((0, so_ref, memo_ref, acco_ref), (1, ss_ref, mems_ref, accs_ref)):
        leak, read = side_ref[lead : lead + 1, :], side_ref[lead + 1 : lead + 2, :]
        s0 = rows_ref[h ^ me, :EP, :].astype(f32)
        total = jnp.broadcast_to(jnp.sum(s0, 0, keepdims=True), (EP, width))
        for e in range(epis):
            at = slice(e * EP, (e + 1) * EP)
            s2 = blocks[h][at, :].astype(f32)
            total += s1c_ref[h, at, :].astype(f32) + s2
            acc_ref[at, :] = leak * (mem_ref[at, :] - s2) + side_ref[3 * EP + e : 3 * EP + e + 1, :]
        sums += fold(total * read)
    read_ref[...] = sums
    add_blocks([0, 1], me, blocks, copies, w_ref, rows_ref, acco_ref, accs_ref, p_ref)


def own_call(me, s2o, s2s, w_rec, w_sib, rows, s1c, memo, mems, side, side_sib, pack, near, epis):
    n, width = s2o.shape
    return pl.pallas_call(
        functools.partial(own_kernel, epis=epis),
        in_specs=[SM, VM, VM, HB, HB] + [VM] * 8,
        out_specs=[VM] * 5,
        out_shape=[
            sds((n, width), f32), sds((n, width), f32), sds((n, 128), f32), sds((EP, 128), f32),
            sds((2,) + pack.shape, bf16),
        ],
        scratch_shapes=[pltpu.VMEM((2, 2, width, width), bf16), pltpu.SemaphoreType.DMA((2, 2))],
        name="own",
        **params(L_PART, 8 * n * width * width, 8 * width * width),
    )(me, s2o, s2s, w_rec, w_sib, rows, s1c, memo, mems, side, side_sib, pack, near)


def part_kernel(me_ref, *refs, order):
    blocks, refs = refs[: len(order)], refs[len(order) :]
    wo_hbm, ws_hbm, rows_ref, acco_in, accs_in, p_in, acco_ref, accs_ref, p_ref, w_ref, sems = refs
    me = me_ref[0]
    copies = fetch_blocks(order, me, wo_hbm, ws_hbm, w_ref, sems)
    acco_ref[...] = acco_in[...]
    accs_ref[...] = accs_in[...]
    p_ref[...] = p_in[...]
    add_blocks(order, me, blocks, copies, w_ref, rows_ref, acco_ref, accs_ref, p_ref)


def part_call(me, blocks, order, w_rec, w_sib, rows, acco, accs, proj):
    n, width = blocks[0].shape
    count = len(order)
    return pl.pallas_call(
        functools.partial(part_kernel, order=order),
        in_specs=[SM] + [VM] * count + [HB, HB] + [VM] * 4,
        out_specs=[VM] * 3,
        out_shape=[sds((n, width), f32), sds((n, width), f32), sds((n, 128), f32)],
        scratch_shapes=[pltpu.VMEM((2, count, width, width), bf16), pltpu.SemaphoreType.DMA((2, count))],
        name="part",
        **params(L_PART, 4 * n * count * width * width, 4 * count * width * width),
    )(me, *blocks, w_rec, w_sib, rows, acco, accs, proj)


def last_kernel(me_ref, *refs, order, epis, copies):
    blocks, refs = refs[: len(order)], refs[len(order) :]
    wo_hbm, ws_hbm, rows_ref, acco_in, accs_in, p_in, so_ref, ss_ref, read_ref, ranks_ref = refs[:10]
    note_ref, w_ref, acco_ref, accs_ref, p_ref, sems = refs[10:]
    lead = so_ref.shape[0] - 8
    me = me_ref[0]
    fetched = fetch_blocks(order, me, wo_hbm, ws_hbm, w_ref, sems)
    acco_ref[...] = acco_in[...]
    accs_ref[...] = accs_in[...]
    p_ref[...] = p_in[...]
    add_blocks(order, me, blocks, fetched, w_ref, rows_ref, acco_ref, accs_ref, p_ref)
    proj = sigma_scale * jnp.sum(p_ref[...], axis=1, keepdims=True)
    sums = read_ref[...]
    for h, side_ref, acc_ref in ((0, so_ref, acco_ref), (1, ss_ref, accs_ref)):
        read = side_ref[lead + 1 : lead + 2, :]
        post = rows_ref[h ^ me, 2 * EP :, :].astype(f32)
        total = jnp.zeros(post.shape, f32)
        for e in range(epis):
            at = slice(e * EP, (e + 1) * EP)
            total += spike(acc_ref[at, :] + proj[at, :] * post).astype(f32)
        sums += fold(total * read)
    sums = jnp.sum(sums, axis=1, keepdims=True)
    row = lax.broadcasted_iota(i32, (EP, 128), 0)
    lane = lax.broadcasted_iota(i32, (EP, 128), 1) & (EP - 1)
    flat = jnp.sum(jnp.where(row == lane, sums, 0.0), axis=0, keepdims=True)
    ranks = ranks_ref[...].astype(f32)
    wide = lax.broadcasted_iota(i32, (EP, 2 * EP), 1)
    chosen = wide == lax.broadcasted_iota(i32, (EP, 2 * EP), 0) + (me & 1) * EP
    mine = jnp.sum(jnp.where(chosen, ranks, 0.0), axis=1, keepdims=True)
    rank = jnp.sum(jnp.where(row == lane, mine, 0.0), axis=0, keepdims=True)
    odd = (lax.broadcasted_iota(i32, (2 * copies, 128), 0) & 1) == 1
    note_ref[...] = jnp.where(odd, rank, flat)


def last_call(me, blocks, order, w_rec, w_sib, rows, acco, accs, proj, side, side_sib, read, ranks, epis, copies):
    n, width = blocks[0].shape
    count = len(order)
    return pl.pallas_call(
        functools.partial(last_kernel, order=order, epis=epis, copies=copies),
        in_specs=[SM] + [VM] * count + [HB, HB] + [VM] * 8,
        out_specs=VM,
        out_shape=sds((2 * copies, 128), f32),
        scratch_shapes=[
            pltpu.VMEM((2, count, width, width), bf16),
            pltpu.VMEM((n, width), f32),
            pltpu.VMEM((n, width), f32),
            pltpu.VMEM((n, 128), f32),
            pltpu.SemaphoreType.DMA((2, count)),
        ],
        name="last",
        **params(L_LAST, 0, 0),
    )(me, *blocks, w_rec, w_sib, rows, acco, accs, proj, side, side_sib, read, ranks)


def tie_kernel(x_ref, after_ref, out_ref):
    pass


def tie_call(x, after):
    return pl.pallas_call(
        tie_kernel,
        in_specs=[HB, HB],
        out_specs=HB,
        out_shape=sds(x.shape, x.dtype),
        input_output_aliases={0: 0},
        name="tie",
        **params(8, 0, 1024),
    )(x, after)


def hand_kernel(x_ref, after_ref, out_ref):
    out_ref[...] = x_ref[...]


def hand_call(x, after):
    return pl.pallas_call(
        hand_kernel,
        in_specs=[VM, HB],
        out_specs=VM,
        out_shape=sds(x.shape, x.dtype),
        name="hand",
        **params(8, 0, 1024),
    )(x, after)


def prep_kernel(core_ref, *refs, pop):
    groups, (pret_ref, post_ref) = refs[:pop], refs[pop:]
    tp = groups[0].shape[1] - 2
    width = groups[0].shape[3]
    for b in range(tp):
        cols = jnp.concatenate([g[i, b] for g in groups for i in range(2)], 0)
        pret_ref[b * width : (b + 1) * width, :] = cols.astype(f32).T.astype(bf16)
    for d in range(2):
        for s in range(pop):
            at = (d * pop + s) * EP
            post_ref[at : at + EP, :] = groups[s // 2][s % 2, tp + (d ^ core_ref[0])]


def prep_call(core, groups, pop):
    _, blocks, _, width = groups[0].shape
    count = 2 * pop * EP
    return pl.pallas_call(
        functools.partial(prep_kernel, pop=pop),
        in_specs=[SM] + [VM] * len(groups),
        out_specs=[VM] * 2,
        out_shape=[sds(((blocks - 2) * width, count), bf16), sds((count, width), bf16)],
        name="prep",
        **params(16, count * blocks * width, 4 * count * blocks * width),
    )(core, *groups)


def grad_kernel(place_ref, note_ref, pret_ref, post_ref, grad_hbm, ret_ref, both_ref, grad_ref, sems, *, tp, pop, plays):
    count = post_ref.shape[0]
    plane, core = place_ref[0], place_ref[1]
    shift = tp.bit_length() - 1
    notes = note_ref[...]

    def where_from(shape):
        row = lax.broadcasted_iota(i32, shape, 0)
        return (row >> 1) >> shift, (row >> 1) & (tp - 1), row & 1, lax.broadcasted_iota(i32, shape, 1) >> 4

    wide = jnp.concatenate([notes] * (count // 128), 1) if count > 128 else notes
    place, unit, kind, group = where_from(wide.shape)
    match = (place == (plane ^ (group & (pop - 1)))) & ((unit & 1) == (core ^ (group >> (pop.bit_length() - 1))))
    total = jnp.sum(jnp.where(match & (kind == 0), wide, 0.0), 0, keepdims=True)
    rank = jnp.sum(jnp.where(match & (kind == 1) & (unit < 2), wide, 0.0), 0, keepdims=True)
    fitness = rank / (count - 1) - 0.5 + total / plays
    fitness = fitness * ((12.0 / count) ** 0.5)
    diag = lax.broadcasted_iota(i32, (count, count), 0) == lax.broadcasted_iota(i32, (count, count), 1)
    column = jnp.sum(jnp.where(diag, fitness, 0.0), 1, keepdims=True)
    weighted = post_ref[...].astype(f32) * column
    high = weighted.astype(bf16)
    both_ref[:count, :] = high
    both_ref[count:, :] = (weighted - high.astype(f32)).astype(bf16)

    inputs = pret_ref.shape[0]
    block = min(512, inputs)

    def out(i):
        at = block_rows(i, block)
        return pltpu.make_async_copy(grad_ref.at[at], grad_hbm.at[at], sems.at[i])

    def body(i, _):
        at = block_rows(i, block)
        pret = pret_ref[at, :]
        grad_ref[at, :] = dot(jnp.concatenate([pret, pret], 1), both_ref[...]).astype(bf16)
        out(i).start()
        return 0

    lax.fori_loop(0, inputs // block, body, 0)
    place, unit, kind, group = where_from(notes.shape)
    mine = (place == plane) & ((unit & 1) == group) & (kind == 0)
    ret_ref[...] = (jnp.sum(jnp.where(mine, notes, 0.0), 0, keepdims=True) / plays)[0, : ret_ref.shape[0]]
    lax.fori_loop(0, inputs // block, lambda i, _: (out(i).wait(), 0)[1], 0)


def grad_call(place, notes, pret, post, tp, pop, plays, members):
    inputs, count = pret.shape
    width = post.shape[1]
    return pl.pallas_call(
        functools.partial(grad_kernel, tp=tp, pop=pop, plays=plays),
        in_specs=[SM] + [VM] * 3,
        out_specs=[HB, VM],
        out_shape=[sds((inputs, width), bf16), sds((members,), f32)],
        scratch_shapes=[
            pltpu.VMEM((2 * count, width), bf16),
            pltpu.VMEM((inputs, width), bf16),
            pltpu.SemaphoreType.DMA((inputs // min(512, inputs),)),
        ],
        name="grad",
        **params(16, 4 * inputs * count * width, 2 * inputs * (count + width)),
    )(place, notes, pret, post)


def swap(x, axis, mask):
    return lax.ppermute(x, axis, [(i, i ^ mask) for i in range(lax.axis_size(axis))])


def shards(
    in_spikes, w_in, w_rec, leak_rate, neuron_bias, readout, pert_table, pert_idx, member_ranks
):
    steps, epis, inputs = in_spikes.shape
    members = pert_idx.shape[0]
    tp, pop = lax.axis_size("tp"), lax.axis_size("pop")
    assert steps == 4 and epis < EP and members == 2 * EP
    me, plane = lax.axis_index("tp"), lax.axis_index("pop")
    at = me[None].astype(i32)
    place = jnp.stack([plane, me & 1]).astype(i32)

    w_sib = swap(w_rec, "tp", 1)
    side, load, post_loc = drive_call(
        in_spikes, w_in, neuron_bias, leak_rate, readout, pert_table, pert_idx, tp
    )
    got = lax.all_to_all(load, "tp", 0, 0)
    w_sib = tie_call(w_sib, got)
    w_own = swap(w_sib, "tp", 1)
    side_sib = swap(side, "tp", 1)
    base = lax.all_to_all(base_call(got, w_rec, side), "tp", 0, 0)
    proj1, pack = proj_call(got, post_loc)
    near = swap(pack, "pop", 1)
    s2o, s2s, memo, mems, s1c = step2_call(at, base, got, w_own, w_sib, proj1, side, side_sib, near, epis)
    far, order = [], []
    if tp == 8:
        xa, yb = swap(s2o, "tp", 2), swap(s2s, "tp", 4)
        xb, ya = swap(s2s, "tp", 2), swap(s2o, "tp", 4)
    else:
        for mask in range(2, tp, 2):
            far += [swap(s2o, "tp", mask), swap(s2s, "tp", mask)]
            order += [mask, mask + 1]
    acco, accs, proj, read, pair = own_call(
        at, s2o, s2s, w_own, w_sib, got, s1c, memo, mems, side, side_sib, pack, near, epis
    )
    if tp == 8:
        xa, yb = tie_call(xa, pair), tie_call(yb, pair)
        far, order = [xa, yb], [2, 5]
        end, ends = [xb, ya, swap(xa, "tp", 4), swap(yb, "tp", 2)], [3, 4, 6, 7]
    else:
        far, end, order, ends = far[:-2], far[-2:], order[:-2], order[-2:]
    acco, accs, proj = part_call(at, far, order, w_own, w_sib, got, acco, accs, proj)
    notes = last_call(
        at, end, ends, w_own, w_sib, got, acco, accs, proj, side, side_sib, read, member_ranks[None], epis, pop * tp
    )
    groups, mask = [pair], 2
    while mask < pop:
        groups += [swap(g, "pop", mask) for g in groups]
        mask *= 2
    groups += [swap(g, "tp", 1) for g in groups[:1]] + [swap(hand_call(g, notes), "tp", 1) for g in groups[1:]]
    notes = lax.all_to_all(notes, ("pop", "tp"), 0, 0, tiled=True)
    pret, post_all = prep_call(place[1:], groups, pop)
    grad, returns = grad_call(place, notes, pret, post_all, tp, pop, epis * steps, members)
    return (returns, grad)


def solution(mesh):
    placed = (
        P(),
        P(None, "tp"),
        P(None, "tp"),
        P("tp"),
        P("tp"),
        P("tp"),
        P(None, "tp"),
        P("pop", None),
        P("pop"),
    )
    return jax.shard_map(
        shards, mesh=mesh, in_specs=placed, out_specs=(P("pop"), P(None, "tp")), check_vma=False
    )
```

time: 499 us -> 77.8 us (0.16)
  waiting for transfers between devices: 339 us -> 17.6 us
  blocking collectives: 87 us -> 13.2 us
  matrix products: 34 us -> 0 us
  Pallas kernels: 0 us -> 23.7 us
  starting transfers between devices: 0.38 us -> 20 us
  other arithmetic: 13.3 us -> 0.08 us
  between operations: 14 us -> 0.78 us
  local copies, waits for them, and re-layouts: 11 us -> 2.1 us
    psum x1 -> x0, waiting for transfers between devices: 291 us -> none  [shards(): grad_total = lax.psum(partial_grad, 'pop')]
    psum x4 -> x0, blocking collectives: 87 us -> none  [the longest x3 73.9 us: shards(): projection = lax.psum(partial_proj, 'tp')]
    all_gather x4 -> x0, waiting for transfers between devices: 47.1 us -> none  [the longest x3 24.8 us: shards(): lax.all_gather(flat_spikes, 'tp', axis=1, tiled=True)]
    dot_general x12 -> x0, matrix products: 34 us -> none  [the longest x3 21.4 us: shards(): jnp.dot(lax.all_gather(flat_spikes, 'tp', axis=1, tiled=True), w_rec, pre...]
    pallas_call x0 -> x13, Pallas kernels: none -> 23.7 us  [the longest x1 5.53 us: step2_call(): pl.pallas_call(functools.partial(step2_kernel, epis=epis), in_specs=[SM,...]
    all_to_all x0 -> x1, blocking collectives: none -> 13.2 us  [shards(): got = lax.all_to_all(load, 'tp', 0, 0)]
    ppermute x0 -> x13, starting transfers between devices: none -> 12.2 us  [swap(): lax.ppermute(x, axis, [(i, i ^ mask) for i in range(lax.axis_size(axis))])]
    convert_element_type x7 -> x0, other arithmetic: 12 us -> none  [the longest x1 6.58 us: shards(): grad_rec = (grad_total * jnp.sqrt(12.0 / member_count)).astype(jnp.bfloat16)]
  transfers between devices with their start and end apart: 5 -> 15, of which waited for: 5 -> 8; matrix products, arithmetic and copies ran while one was open for 4% -> 0% of each run, Pallas kernels for 0% -> 18%
where the time goes in v3:
time: 77.8 us; the launch traced here: 77.4 us
  Pallas kernels  23.7 us (30%)
  starting transfers between devices  20 us (26%)
  waiting for transfers between devices  17.6 us (23%)
  blocking collectives  13.2 us (17%)
  local copies, waits for them, and re-layouts  2.1 us (3%)
  between operations  0.78 us (1%)
    all_to_all x1, blocking collectives, shards(): got = lax.all_to_all(load, 'tp', 0, 0)  13.2 us
    ppermute x13, starting transfers between devices, swap(): lax.ppermute(x, axis, [(i, i ^ mask) for i in range(lax.axis_size(axis))])  12.2 us
    ppermute x13, waiting for transfers between devices, swap(): lax.ppermute(x, axis, [(i, i ^ mask) for i in range(lax.axis_size(axis))])  10.6 us
    all_to_all x1, waiting for transfers between devices, shards(): notes = lax.all_to_all(notes, ('pop', 'tp'), 0, 0, tiled=True)  6.82 us
    pallas_call x1, Pallas kernels, step2_call(): pl.pallas_call(functools.partial(step2_kernel, epis=epis), in_specs=[SM,...  5.53 us
    pallas_call x1, Pallas kernels, grad_call(): pl.pallas_call(functools.partial(grad_kernel, tp=tp, pop=pop, plays=plays...  4.43 us
    all_to_all x1, starting transfers between devices, shards(): notes = lax.all_to_all(notes, ('pop', 'tp'), 0, 0, tiled=True)  4.38 us
    pallas_call x1, Pallas kernels, drive_call(): pl.pallas_call(drive_kernel, in_specs=[HB] * 7, out_specs=[VM] * 3, out_s...  3.95 us
  transfers between devices with their start and end apart: 15, of which 8 were waited for; matrix products, arithmetic and copies ran while one was open for 0% of the time, Pallas kernels for 18%

profile of v3, /device:TPU:0, one launch (start us, length us, event | category | flops | bytes accessed | tf_op | source)
XLA Modules:
  0.0 77.4 jit_solution(3082256750937474724)
XLA Ops:
  0.6 0.5 collective-permute-start
  1.1 4.0 %drive.1 = (f32[72,512]{1,0:T(8,128)}, bf16[8,48,512]{2,1,0:T(8,128)(2,1)}, bf16[2,16,512]{2,1,0:T(8,128)(2,1)}) custom-call(s32[15,4,4096]{2,1,0:T(4,128)} %bitcast.13, bf16[4096,512]{1,0:T(8,128)(2,1)} %win_hbm.1, f32[1,512]{1,0:T(1,128)} %bitcast.14, f32[1,512]{1,0:T(1,128)} %bitcast.15, f32[1,512]{1,0:T(1,128)} %bitcast.16, bf16[256,512]{1,0:T(8,128)(2,1)} %table_hbm.1, ...), custom_call_target="tpu_custom_call" | custom-call | flops 268435456 | bytes 5242880 | tf_op jit(solution)/shard_map/drive/pallas_call | solution.py:117
  5.1 13.2 %all_to_all.21.got_ref.after_ref.rows_ref.refs_4_.refs_6_ = bf16[8,48,512]{2,1,0:T(8,128)(2,1)S(1)} all-to-all(bf16[8,48,512]{2,1,0:T(8,128)(2,1)} %get-tuple-element.24), channel_id=1, replica_groups=mesh['pop'=4,'tp'=8] {'tp'}, dimensions={0} | all-to-all | bytes 786432 | tf_op jit(solution)/shard_map/all_to_all | solution.py:572
  18.4 2.1 %copy-done = bf16[4096,512]{1,0:T(8,128)(2,1)S(1)} copy-done((bf16[4096,512]{1,0:T(8,128)(2,1)S(1)}, bf16[4096,512]{1,0:T(8,128)(2,1)}, u32[]{:S(2)}) %copy-start) | copy-done | bytes 4194328
  20.5 1.7 %base.1 = f32[8,16,512]{2,1,0:T(8,128)} custom-call(bf16[8,48,512]{2,1,0:T(8,128)(2,1)S(1)} %all_to_all.21.got_ref.after_ref.rows_ref.refs_4_.refs_6_, bf16[4096,512]{1,0:T(8,128)(2,1)S(1)} %copy-done, f32[72,512]{1,0:T(8,128)S(1)} %copy-done.1), custom_call_target="tpu_custom_call" | custom-call | flops 67108864 | bytes 4194304 | tf_op jit(solution)/shard_map/base/pallas_call | solution.py:157
  22.2 3.4 %all-to-all-start.1 = ((f32[8,16,512]{2,1,0:T(8,128)}), f32[8,16,512]{2,1,0:T(8,128)S(1)}, u32[]{:S(2)}, u32[]{:S(2)}) async-start(f32[8,16,512]{2,1,0:T(8,128)} %base.1), calls=%async_computation.1 | async-start | bytes 524288 | tf_op jit(solution)/shard_map/all_to_all | solution.py:576
  25.8 1.6 %collective-permute-start.3 = (bf16[10,16,512]{2,1,0:T(8,128)(2,1)S(1)}, bf16[10,16,512]{2,1,0:T(8,128)(2,1)S(1)}, u32[]{:S(2)}, u32[]{:S(2)}) collective-permute-start(bf16[10,16,512]{2,1,0:T(8,128)(2,1)S(1)} %get-tuple-element.28.pack_ref), channel_id=1, source_target_pairs={{0,8},{8,0},{16,24},{24,16},{1,9},{9,1},{17,25},{25,17},{2,10},{10... | collective-permute-start | bytes 491528 | tf_op jit(solution)/shard_map/ppermute | solution.py:554
  27.6 1.2 %collective-permute-done.2.ss_ref.refs_11_ = f32[72,512]{1,0:T(8,128)S(1)} collective-permute-done((f32[72,512]{1,0:T(8,128)S(1)}, f32[72,512]{1,0:T(8,128)S(1)}, u32[]{:S(2)}, u32[]{:S(2)}) %collective-permute-start.2) | collective-permute-done | bytes 147488 | tf_op jit(solution)/shard_map/ppermute | solution.py:554
  28.8 3.6 %collective-permute-done.3.near_ref = bf16[10,16,512]{2,1,0:T(8,128)(2,1)S(1)} collective-permute-done((bf16[10,16,512]{2,1,0:T(8,128)(2,1)S(1)}, bf16[10,16,512]{2,1,0:T(8,128)(2,1)S(1)}, u32[]{:S(2)}, u32[]{:S(2)}) %collective-permute-start.3) | collective-permute-done | bytes 163872 | tf_op jit(solution)/shard_map/ppermute | solution.py:554
  32.5 5.5 %step2.1 = (bf16[240,512]{1,0:T(8,128)(2,1)S(1)}, bf16[240,512]{1,0:T(8,128)(2,1)S(1)}, f32[240,512]{1,0:T(8,128)S(1)}, f32[240,512]{1,0:T(8,128)S(1)}, bf16[2,240,512]{2,1,0:T(8,128)(2,1)S(1)}) custom-call(s32[1]{0:T(128)} %bitcast.2.me_ref, f32[8,16,512]{2,1,0:T(8,128)S(1)} %all-to-all-done.1.base_ref, ...), custom_call_target="tpu_custom_call" | custom-call | flops 2013265920 | bytes 8388608 | tf_op jit(solution)/shard_map/step2/pallas_call | solution.py:266
  38.0 1.6 %collective-permute-start.8 = (bf16[240,512]{1,0:T(8,128)(2,1)S(1)}, bf16[240,512]{1,0:T(8,128)(2,1)S(1)}, u32[]{:S(2)}, u32[]{:S(2)}) collective-permute-start(bf16[240,512]{1,0:T(8,128)(2,1)S(1)} %get-tuple-element.29.s2s_ref), channel_id=1, source_target_pairs={{0,4},{1,5},{2,6},{3,7},{4,0},{5,1},{6,2},{7,3},{8,12},{9,13},{10,... | collective-permute-start | bytes 737288 | tf_op jit(solution)/shard_map/ppermute | solution.py:554
  39.6 1.5 %collective-permute-start.6 = (bf16[240,512]{1,0:T(8,128)(2,1)S(1)}, bf16[240,512]{1,0:T(8,128)(2,1)S(1)}, u32[]{:S(2)}, u32[]{:S(2)}) collective-permute-start(bf16[240,512]{1,0:T(8,128)(2,1)S(1)} %get-tuple-element.30.s2o_ref), channel_id=1, source_target_pairs={{0,2},{1,3},{2,0},{3,1},{4,6},{5,7},{6,4},{7,5},{8,10},{9,11},{10,... | collective-permute-start | bytes 737288 | tf_op jit(solution)/shard_map/ppermute | solution.py:554
  41.1 2.0 %own.1 = (f32[240,512]{1,0:T(8,128)S(1)}, f32[240,512]{1,0:T(8,128)S(1)}, f32[240,128]{1,0:T(8,128)S(1)}, f32[16,128]{1,0:T(8,128)S(1)}, bf16[2,10,16,512]{3,2,1,0:T(8,128)(2,1)S(1)}) custom-call(s32[1]{0:T(128)} %bitcast.2.me_ref, bf16[240,512]{1,0:T(8,128)(2,1)S(1)} %get-tuple-element.30.s2o_ref, bf16[240,512]{1,0:T(8,128)(2,1)S(1)} %get-tuple-element.29.s2s_ref, ...), custom_call_target="tpu_custom_call" | custom-call | flops 503316480 | bytes 2097152 | tf_op jit(solution)/shard_map/own/pallas_call | solution.py:340
  43.1 2.7 %collective-permute-start.10 = (bf16[2,10,16,512]{3,2,1,0:T(8,128)(2,1)S(1)}, bf16[2,10,16,512]{3,2,1,0:T(8,128)(2,1)S(1)}, u32[]{:S(2)}, u32[]{:S(2)}) collective-permute-start(bf16[2,10,16,512]{3,2,1,0:T(8,128)(2,1)S(1)} %get-tuple-element.34.after_ref.refs_0_), channel_id=1, source_target_pairs={{0,16},{8,24},{16,0},{24,8},{1,17},{9,25},{17,1},{25,9},{2,18},{10... | collective-permute-start | bytes 983048 | tf_op jit(solution)/shard_map/ppermute | solution.py:554
  45.8 0.5 collective-permute-start.4
  46.8 1.5 %collective-permute-start.9 = (bf16[240,512]{1,0:T(8,128)(2,1)S(1)}, bf16[240,512]{1,0:T(8,128)(2,1)S(1)}, u32[]{:S(2)}, u32[]{:S(2)}) collective-permute-start(bf16[240,512]{1,0:T(8,128)(2,1)S(1)} %tie.5.refs_1_), channel_id=1, source_target_pairs={{0,2},{1,3},{2,0},{3,1},{4,6},{5,7},{6,4},{7,5},{8,10},{9,11},{10,... | collective-permute-start | bytes 737288 | tf_op jit(solution)/shard_map/ppermute | solution.py:554
  48.3 1.5 %collective-permute-start.7 = (bf16[240,512]{1,0:T(8,128)(2,1)S(1)}, bf16[240,512]{1,0:T(8,128)(2,1)S(1)}, u32[]{:S(2)}, u32[]{:S(2)}) collective-permute-start(bf16[240,512]{1,0:T(8,128)(2,1)S(1)} %tie.4.refs_0_), channel_id=1, source_target_pairs={{0,4},{1,5},{2,6},{3,7},{4,0},{5,1},{6,2},{7,3},{8,12},{9,13},{10,... | collective-permute-start | bytes 737288 | tf_op jit(solution)/shard_map/ppermute | solution.py:554
  49.8 2.0 %part.1 = (f32[240,512]{1,0:T(8,128)S(1)}, f32[240,512]{1,0:T(8,128)S(1)}, f32[240,128]{1,0:T(8,128)S(1)}) custom-call(s32[1]{0:T(128)} %bitcast.2.me_ref, bf16[240,512]{1,0:T(8,128)(2,1)S(1)} %tie.4.refs_0_, bf16[240,512]{1,0:T(8,128)(2,1)S(1)} %tie.5.refs_1_, bf16[4096,512]{1,0:T(8,128)(2,1)} %collective-permute-done.1.wo_hbm.refs_2_.refs_4_, ...), custom_call_target="tpu_custom_call" | custom-call | flops 503316480 | bytes 2097152 | tf_op jit(solution)/shard_map/part/pallas_call | solution.py:368
  51.9 2.8 %collective-permute-done.4.refs_0_ = bf16[240,512]{1,0:T(8,128)(2,1)S(1)} collective-permute-done((bf16[240,512]{1,0:T(8,128)(2,1)S(1)}, bf16[240,512]{1,0:T(8,128)(2,1)S(1)}, u32[]{:S(2)}, u32[]{:S(2)}) %collective-permute-start.4) | collective-permute-done | bytes 245792 | tf_op jit(solution)/shard_map/ppermute | solution.py:554
  55.0 2.4 %collective-permute-done.9.refs_3_ = bf16[240,512]{1,0:T(8,128)(2,1)S(1)} collective-permute-done((bf16[240,512]{1,0:T(8,128)(2,1)S(1)}, bf16[240,512]{1,0:T(8,128)(2,1)S(1)}, u32[]{:S(2)}, u32[]{:S(2)}) %collective-permute-start.9) | collective-permute-done | bytes 245792 | tf_op jit(solution)/shard_map/ppermute | solution.py:554
  57.7 3.6 %last.1.after_ref = f32[64,128]{1,0:T(8,128)} custom-call(s32[1]{0:T(128)} %bitcast.2.me_ref, bf16[240,512]{1,0:T(8,128)(2,1)S(1)} %collective-permute-done.4.refs_0_, bf16[240,512]{1,0:T(8,128)(2,1)S(1)} %collective-permute-done.5.refs_1_, bf16[240,512]{1,0:T(8,128)(2,1)S(1)} %collective-permute-done.7.refs_2_, ...), custom_call_target="tpu_custom_call" | custom-call | tf_op jit(solution)/shard_map/last/pallas_call | solution.py:416
  61.3 4.4 %all-to-all-start.2 = ((f32[32,2,128]{2,1,0:T(2,128)}), f32[32,2,128]{2,1,0:T(2,128)S(1)}, u32[]{:S(2)}, u32[]{:S(2)}) async-start(f32[32,2,128]{2,1,0:T(2,128)} %bitcast.9), calls=%async_computation.2 | async-start | bytes 65536 | tf_op jit(solution)/shard_map/all_to_all | solution.py:606
  66.2 6.8 %all-to-all-done.2 = f32[32,2,128]{2,1,0:T(2,128)S(1)} async-done(((f32[32,2,128]{2,1,0:T(2,128)}), f32[32,2,128]{2,1,0:T(2,128)S(1)}, u32[]{:S(2)}, u32[]{:S(2)}) %all-to-all-start.2) | async-done | bytes 32800 | tf_op jit(solution)/shard_map/all_to_all | solution.py:606
  73.0 4.4 %grad.1 = (bf16[4096,512]{1,0:T(8,128)(2,1)}, f32[32]{0:T(128)}) custom-call(s32[2]{0:T(128)S(1)} %pad_add_fusion.place_ref, f32[64,128]{1,0:T(8,128)S(1)} %bitcast.11, bf16[4096,128]{1,0:T(8,128)(2,1)S(1)} %get-tuple-element.42.pret_ref, bf16[128,512]{1,0:T(8,128)(2,1)S(1)} %get-tuple-element.43.post_ref), custom_call_target="tpu_custom_call" | custom-call | flops 1073741824 | bytes 5242880 | tf_op jit(solution)/shard_map/grad/pallas_call | solution.py:538
  (29 shorter events, 2.2 us)
Async XLA Ops:
  0.6 17.7 %collective-permute-start = (bf16[4096,512]{1,0:T(8,128)(2,1)}, bf16[4096,512]{1,0:T(8,128)(2,1)}, u32[]{:S(2)}, u32[]{:S(2)}) collective-permute-start(bf16[4096,512]{1,0:T(8,128)(2,1)} %w_hbm.1), channel_id=1, source_target_pairs={{0,1},{1,0},{2,3},{3,2},{4,5},{5,4},{6,7},{7,6},{8,9},{9,8},{10,11... | collective-permute-start | bytes 12582920 | tf_op jit(solution)/shard_map/ppermute | solution.py:554
  18.3 2.2 %copy-start = (bf16[4096,512]{1,0:T(8,128)(2,1)S(1)}, bf16[4096,512]{1,0:T(8,128)(2,1)}, u32[]{:S(2)}) copy-start(bf16[4096,512]{1,0:T(8,128)(2,1)} %w_hbm.1) | copy-start | bytes 12582916
  18.3 2.2 %copy-start.1 = (f32[72,512]{1,0:T(8,128)S(1)}, f32[72,512]{1,0:T(8,128)}, u32[]{:S(2)}) copy-start(f32[72,512]{1,0:T(8,128)} %get-tuple-element.25.side_ref.so_ref.refs_10_) | copy-start | bytes 442372
  18.3 7.3 %copy-start.2 = (bf16[2,16,512]{2,1,0:T(8,128)(2,1)S(1)}, bf16[2,16,512]{2,1,0:T(8,128)(2,1)}, u32[]{:S(2)}) copy-start(bf16[2,16,512]{2,1,0:T(8,128)(2,1)} %get-tuple-element.26.post_ref) | copy-start | bytes 98308
  18.3 14.2 %collective-permute-start.1 = (bf16[4096,512]{1,0:T(8,128)(2,1)}, bf16[4096,512]{1,0:T(8,128)(2,1)}, u32[]{:S(2)}, u32[]{:S(2)}) collective-permute-start(bf16[4096,512]{1,0:T(8,128)(2,1)} %tie.3.ws_hbm.refs_3_.refs_5_), channel_id=1, source_target_pairs={{0,1},{1,0},{2,3},{3,2},{4,5},{5,4},{6,7},{7,6},{8,9},{9,8},{10,11... | collective-permute-start | bytes 12582920 | tf_op jit(solution)/shard_map/ppermute | solution.py:554
  22.2 10.3 %all-to-all-start.1 = ((f32[8,16,512]{2,1,0:T(8,128)}), f32[8,16,512]{2,1,0:T(8,128)S(1)}, u32[]{:S(2)}, u32[]{:S(2)}) async-start(f32[8,16,512]{2,1,0:T(8,128)} %base.1), calls=%async_computation.1 | async-start | bytes 524288 | tf_op jit(solution)/shard_map/all_to_all | solution.py:576
  25.8 6.6 %collective-permute-start.3 = (bf16[10,16,512]{2,1,0:T(8,128)(2,1)S(1)}, bf16[10,16,512]{2,1,0:T(8,128)(2,1)S(1)}, u32[]{:S(2)}, u32[]{:S(2)}) collective-permute-start(bf16[10,16,512]{2,1,0:T(8,128)(2,1)S(1)} %get-tuple-element.28.pack_ref), channel_id=1, source_target_pairs={{0,8},{8,0},{16,24},{24,16},{1,9},{9,1},{17,25},{25,17},{2,10},{10... | collective-permute-start | bytes 491528 | tf_op jit(solution)/shard_map/ppermute | solution.py:554
  27.4 1.4 %collective-permute-start.2 = (f32[72,512]{1,0:T(8,128)S(1)}, f32[72,512]{1,0:T(8,128)S(1)}, u32[]{:S(2)}, u32[]{:S(2)}) collective-permute-start(f32[72,512]{1,0:T(8,128)S(1)} %copy-done.1), channel_id=1, source_target_pairs={{0,1},{1,0},{2,3},{3,2},{4,5},{5,4},{6,7},{7,6},{8,9},{9,8},{10,11... | collective-permute-start | bytes 442376 | tf_op jit(solution)/shard_map/ppermute | solution.py:554
  38.0 8.8 %collective-permute-start.8 = (bf16[240,512]{1,0:T(8,128)(2,1)S(1)}, bf16[240,512]{1,0:T(8,128)(2,1)S(1)}, u32[]{:S(2)}, u32[]{:S(2)}) collective-permute-start(bf16[240,512]{1,0:T(8,128)(2,1)S(1)} %get-tuple-element.29.s2s_ref), channel_id=1, source_target_pairs={{0,4},{1,5},{2,6},{3,7},{4,0},{5,1},{6,2},{7,3},{8,12},{9,13},{10,... | collective-permute-start | bytes 737288 | tf_op jit(solution)/shard_map/ppermute | solution.py:554
  39.6 8.7 %collective-permute-start.6 = (bf16[240,512]{1,0:T(8,128)(2,1)S(1)}, bf16[240,512]{1,0:T(8,128)(2,1)S(1)}, u32[]{:S(2)}, u32[]{:S(2)}) collective-permute-start(bf16[240,512]{1,0:T(8,128)(2,1)S(1)} %get-tuple-element.30.s2o_ref), channel_id=1, source_target_pairs={{0,2},{1,3},{2,0},{3,1},{4,6},{5,7},{6,4},{7,5},{8,10},{9,11},{10,... | collective-permute-start | bytes 737288 | tf_op jit(solution)/shard_map/ppermute | solution.py:554
  43.1 18.1 %collective-permute-start.10 = (bf16[2,10,16,512]{3,2,1,0:T(8,128)(2,1)S(1)}, bf16[2,10,16,512]{3,2,1,0:T(8,128)(2,1)S(1)}, u32[]{:S(2)}, u32[]{:S(2)}) collective-permute-start(bf16[2,10,16,512]{3,2,1,0:T(8,128)(2,1)S(1)} %get-tuple-element.34.after_ref.refs_0_), channel_id=1, source_target_pairs={{0,16},{8,24},{16,0},{24,8},{1,17},{9,25},{17,1},{25,9},{2,18},{10... | collective-permute-start | bytes 983048 | tf_op jit(solution)/shard_map/ppermute | solution.py:554
  45.8 8.9 %collective-permute-start.4 = (bf16[240,512]{1,0:T(8,128)(2,1)S(1)}, bf16[240,512]{1,0:T(8,128)(2,1)S(1)}, u32[]{:S(2)}, u32[]{:S(2)}) collective-permute-start(bf16[240,512]{1,0:T(8,128)(2,1)S(1)} %get-tuple-element.29.s2s_ref), channel_id=1, source_target_pairs={{0,2},{1,3},{2,0},{3,1},{4,6},{5,7},{6,4},{7,5},{8,10},{9,11},{10,... | collective-permute-start | bytes 737288 | tf_op jit(solution)/shard_map/ppermute | solution.py:554
  46.3 8.7 %collective-permute-start.5 = (bf16[240,512]{1,0:T(8,128)(2,1)S(1)}, bf16[240,512]{1,0:T(8,128)(2,1)S(1)}, u32[]{:S(2)}, u32[]{:S(2)}) collective-permute-start(bf16[240,512]{1,0:T(8,128)(2,1)S(1)} %get-tuple-element.30.s2o_ref), channel_id=1, source_target_pairs={{0,4},{1,5},{2,6},{3,7},{4,0},{5,1},{6,2},{7,3},{8,12},{9,13},{10,... | collective-permute-start | bytes 737288 | tf_op jit(solution)/shard_map/ppermute | solution.py:554
  46.8 10.5 %collective-permute-start.9 = (bf16[240,512]{1,0:T(8,128)(2,1)S(1)}, bf16[240,512]{1,0:T(8,128)(2,1)S(1)}, u32[]{:S(2)}, u32[]{:S(2)}) collective-permute-start(bf16[240,512]{1,0:T(8,128)(2,1)S(1)} %tie.5.refs_1_), channel_id=1, source_target_pairs={{0,2},{1,3},{2,0},{3,1},{4,6},{5,7},{6,4},{7,5},{8,10},{9,11},{10,... | collective-permute-start | bytes 737288 | tf_op jit(solution)/shard_map/ppermute | solution.py:554
  48.3 9.3 %collective-permute-start.7 = (bf16[240,512]{1,0:T(8,128)(2,1)S(1)}, bf16[240,512]{1,0:T(8,128)(2,1)S(1)}, u32[]{:S(2)}, u32[]{:S(2)}) collective-permute-start(bf16[240,512]{1,0:T(8,128)(2,1)S(1)} %tie.4.refs_0_), channel_id=1, source_target_pairs={{0,4},{1,5},{2,6},{3,7},{4,0},{5,1},{6,2},{7,3},{8,12},{9,13},{10,... | collective-permute-start | bytes 737288 | tf_op jit(solution)/shard_map/ppermute | solution.py:554
  49.8 7.8 %copy-start.3 = (s32[32]{0:T(128)S(1)}, s32[32]{0:T(128)}, u32[]{:S(2)}) copy-start(s32[32]{0:T(128)} %param.17) | copy-start | bytes 388
  54.7 11.1 %collective-permute-start.11 = (bf16[2,10,16,512]{3,2,1,0:T(8,128)(2,1)S(1)}, bf16[2,10,16,512]{3,2,1,0:T(8,128)(2,1)S(1)}, u32[]{:S(2)}, u32[]{:S(2)}) collective-permute-start(bf16[2,10,16,512]{3,2,1,0:T(8,128)(2,1)S(1)} %get-tuple-element.34.after_ref.refs_0_), channel_id=1, source_target_pairs={{0,1},{1,0},{2,3},{3,2},{4,5},{5,4},{6,7},{7,6},{8,9},{9,8},{10,11... | collective-permute-start | bytes 983048 | tf_op jit(solution)/shard_map/ppermute | solution.py:554
  61.3 4.6 %collective-permute-start.12 = (bf16[2,10,16,512]{3,2,1,0:T(8,128)(2,1)S(1)}, bf16[2,10,16,512]{3,2,1,0:T(8,128)(2,1)S(1)}, u32[]{:S(2)}, u32[]{:S(2)}) collective-permute-start(bf16[2,10,16,512]{3,2,1,0:T(8,128)(2,1)S(1)} %hand.1), channel_id=1, source_target_pairs={{0,1},{1,0},{2,3},{3,2},{4,5},{5,4},{6,7},{7,6},{8,9},{9,8},{10,11... | collective-permute-start | bytes 983048 | tf_op jit(solution)/shard_map/ppermute | solution.py:554
  61.3 11.6 %all-to-all-start.2 = ((f32[32,2,128]{2,1,0:T(2,128)}), f32[32,2,128]{2,1,0:T(2,128)S(1)}, u32[]{:S(2)}, u32[]{:S(2)}) async-start(f32[32,2,128]{2,1,0:T(2,128)} %bitcast.9), calls=%async_computation.2 | async-start | bytes 65536 | tf_op jit(solution)/shard_map/all_to_all | solution.py:606

commit v4 on v3

--- a/solution.py
+++ b/solution.py
@@ -241,7 +241,7 @@
         rebuild(j + 1)
         return 0
 
-    lax.fori_loop(0, tp - 1, body, 0)
+    lax.fori_loop(0, tp - 1, body, 0, unroll=True)
     multiply(tp - 1)
     proj2 = sigma_scale * jnp.sum(p2_ref[...], axis=1, keepdims=True)
     for h, side_ref, acc_ref, s2_ref, mem_ref in (
@@ -298,8 +298,8 @@
 
 def add_blocks(order, me, blocks, copies, w_ref, rows_ref, acco_ref, accs_ref, p_ref):
     for n, v in enumerate(order):
-        copies[2 * n].wait()
-        copies[2 * n + 1].wait()
+        for copy in copies[2 * n : 2 * n + 2]:
+            copy.wait()
         block = blocks[n][...]
         acco_ref[...] += dot(block, w_ref[0, n])
         accs_ref[...] += dot(block, w_ref[1, n])
@@ -351,26 +351,34 @@
     )(me, s2o, s2s, w_rec, w_sib, rows, s1c, memo, mems, side, side_sib, pack, near)
 
 
-def part_kernel(me_ref, *refs, order):
+def part_kernel(me_ref, *refs, order, tail):
     blocks, refs = refs[: len(order)], refs[len(order) :]
-    wo_hbm, ws_hbm, rows_ref, acco_in, accs_in, p_in, acco_ref, accs_ref, p_ref, w_ref, sems = refs
+    wo_hbm, ws_hbm, rows_ref, acco_in, accs_in, p_in, acco_ref, accs_ref, p_ref, *rest = refs
+    w_ref, sems = rest[-2:]
     me = me_ref[0]
     copies = fetch_blocks(order, me, wo_hbm, ws_hbm, w_ref, sems)
+    if tail:
+        later = fetch_blocks(tail, me, wo_hbm, ws_hbm, rest[0], rest[1])
     acco_ref[...] = acco_in[...]
     accs_ref[...] = accs_in[...]
     p_ref[...] = p_in[...]
     add_blocks(order, me, blocks, copies, w_ref, rows_ref, acco_ref, accs_ref, p_ref)
-
-
-def part_call(me, blocks, order, w_rec, w_sib, rows, acco, accs, proj):
+    if tail:
+        for copy in later:
+            copy.wait()
+
+
+def part_call(me, blocks, order, w_rec, w_sib, rows, acco, accs, proj, tail=()):
     n, width = blocks[0].shape
     count = len(order)
-    return pl.pallas_call(
-        functools.partial(part_kernel, order=order),
+    more = [sds((2, len(tail), width, width), bf16)] if tail else []
+    sems = [pltpu.SemaphoreType.DMA((2, len(tail)))] if tail else []
+    return pl.pallas_call(
+        functools.partial(part_kernel, order=order, tail=tail),
         in_specs=[SM] + [VM] * count + [HB, HB] + [VM] * 4,
-        out_specs=[VM] * 3,
-        out_shape=[sds((n, width), f32), sds((n, width), f32), sds((n, 128), f32)],
-        scratch_shapes=[pltpu.VMEM((2, count, width, width), bf16), pltpu.SemaphoreType.DMA((2, count))],
+        out_specs=[VM] * (3 + len(more)),
+        out_shape=[sds((n, width), f32), sds((n, width), f32), sds((n, 128), f32)] + more,
+        scratch_shapes=sems + [pltpu.VMEM((2, count, width, width), bf16), pltpu.SemaphoreType.DMA((2, count))],
         name="part",
         **params(L_PART, 4 * n * count * width * width, 4 * count * width * width),
     )(me, *blocks, w_rec, w_sib, rows, acco, accs, proj)
@@ -378,15 +386,14 @@
 
 def last_kernel(me_ref, *refs, order, epis, copies):
     blocks, refs = refs[: len(order)], refs[len(order) :]
-    wo_hbm, ws_hbm, rows_ref, acco_in, accs_in, p_in, so_ref, ss_ref, read_ref, ranks_ref = refs[:10]
-    note_ref, w_ref, acco_ref, accs_ref, p_ref, sems = refs[10:]
+    w_ref, rows_ref, acco_in, accs_in, p_in, so_ref, ss_ref, read_ref, ranks_ref = refs[:9]
+    note_ref, acco_ref, accs_ref, p_ref = refs[9:]
     lead = so_ref.shape[0] - 8
     me = me_ref[0]
-    fetched = fetch_blocks(order, me, wo_hbm, ws_hbm, w_ref, sems)
     acco_ref[...] = acco_in[...]
     accs_ref[...] = accs_in[...]
     p_ref[...] = p_in[...]
-    add_blocks(order, me, blocks, fetched, w_ref, rows_ref, acco_ref, accs_ref, p_ref)
+    add_blocks(order, me, blocks, [], w_ref, rows_ref, acco_ref, accs_ref, p_ref)
     proj = sigma_scale * jnp.sum(p_ref[...], axis=1, keepdims=True)
     sums = read_ref[...]
     for h, side_ref, acc_ref in ((0, so_ref, acco_ref), (1, ss_ref, accs_ref)):
@@ -410,24 +417,22 @@
     note_ref[...] = jnp.where(odd, rank, flat)
 
 
-def last_call(me, blocks, order, w_rec, w_sib, rows, acco, accs, proj, side, side_sib, read, ranks, epis, copies):
+def last_call(me, blocks, order, tail, rows, acco, accs, proj, side, side_sib, read, ranks, epis, copies):
     n, width = blocks[0].shape
     count = len(order)
     return pl.pallas_call(
         functools.partial(last_kernel, order=order, epis=epis, copies=copies),
-        in_specs=[SM] + [VM] * count + [HB, HB] + [VM] * 8,
+        in_specs=[SM] + [VM] * (count + 9),
         out_specs=VM,
         out_shape=sds((2 * copies, 128), f32),
         scratch_shapes=[
-            pltpu.VMEM((2, count, width, width), bf16),
             pltpu.VMEM((n, width), f32),
             pltpu.VMEM((n, width), f32),
             pltpu.VMEM((n, 128), f32),
-            pltpu.SemaphoreType.DMA((2, count)),
         ],
         name="last",
         **params(L_LAST, 0, 0),
-    )(me, *blocks, w_rec, w_sib, rows, acco, accs, proj, side, side_sib, read, ranks)
+    )(me, *blocks, tail, rows, acco, accs, proj, side, side_sib, read, ranks)
 
 
 def tie_kernel(x_ref, after_ref, out_ref):
@@ -525,7 +530,7 @@
         out(i).start()
         return 0
 
-    lax.fori_loop(0, inputs // block, body, 0)
+    lax.fori_loop(0, inputs // block, body, 0, unroll=True)
     place, unit, kind, group = where_from(notes.shape)
     mine = (place == plane) & ((unit & 1) == group) & (kind == 0)
     ret_ref[...] = (jnp.sum(jnp.where(mine, notes, 0.0), 0, keepdims=True) / plays)[0, : ret_ref.shape[0]]
@@ -591,12 +596,14 @@
     if tp == 8:
         xa, yb = tie_call(xa, pair), tie_call(yb, pair)
         far, order = [xa, yb], [2, 5]
-        end, ends = [xb, ya, swap(xa, "tp", 4), swap(yb, "tp", 2)], [3, 4, 6, 7]
+        end, ends = [swap(xa, "tp", 4), swap(yb, "tp", 2)], [6, 7]
     else:
         far, end, order, ends = far[:-2], far[-2:], order[:-2], order[-2:]
-    acco, accs, proj = part_call(at, far, order, w_own, w_sib, got, acco, accs, proj)
+    acco, accs, proj, tail = part_call(at, far, order, w_own, w_sib, got, acco, accs, proj, tuple(ends))
+    if tp == 8:
+        acco, accs, proj = part_call(at, [xb, ya], [3, 4], w_own, w_sib, got, acco, accs, proj)
     notes = last_call(
-        at, end, ends, w_own, w_sib, got, acco, accs, proj, side, side_sib, read, member_ranks[None], epis, pop * tp
+        at, end, ends, tail, got, acco, accs, proj, side, side_sib, read, member_ranks[None], epis, pop * tp
     )
     groups, mask = [pair], 2
     while mask < pop:

time: 77.8 us -> 74.1 us (0.952)
  waiting for transfers between devices: 17.6 us -> 15.3 us
  Pallas kernels: 23.7 us -> 22.5 us
    pallas_call x1 -> x2, Pallas kernels: 2.01 us -> 4.55 us  [part_call(): pl.pallas_call(functools.partial(part_kernel, order=order, tail=tail), in...]
    ppermute x13, waiting for transfers between devices: 10.6 us -> 8.34 us  [swap(): lax.ppermute(x, axis, [(i, i ^ mask) for i in range(lax.axis_size(axis))])]
    pallas_call x1, Pallas kernels: 3.56 us -> 1.56 us  [last_call(): pl.pallas_call(functools.partial(last_kernel, order=order, epis=epis, cop...]
    pallas_call x1, Pallas kernels: 5.53 us -> 4.63 us  [step2_call(): pl.pallas_call(functools.partial(step2_kernel, epis=epis), in_specs=[SM,...]
    pallas_call x1, Pallas kernels: 4.43 us -> 3.55 us  [grad_call(): pl.pallas_call(functools.partial(grad_kernel, tp=tp, pop=pop, plays=plays...]
  transfers between devices with their start and end apart: 15 -> 15, of which waited for: 8 -> 9; matrix products, arithmetic and copies ran while one was open for 0% -> 0% of each run, Pallas kernels for 18% -> 19%
where the time goes in v4:
time: 74.1 us; the launch traced here: 73.6 us
  Pallas kernels  22.5 us (30%)
  starting transfers between devices  19.7 us (27%)
  waiting for transfers between devices  15.3 us (21%)
  blocking collectives  13.2 us (18%)
  local copies, waits for them, and re-layouts  2.1 us (3%)
  between operations  0.77 us (1%)
    all_to_all x1, blocking collectives, shards(): got = lax.all_to_all(load, 'tp', 0, 0)  13.2 us
    ppermute x13, starting transfers between devices, swap(): lax.ppermute(x, axis, [(i, i ^ mask) for i in range(lax.axis_size(axis))])  12.2 us
    ppermute x13, waiting for transfers between devices, swap(): lax.ppermute(x, axis, [(i, i ^ mask) for i in range(lax.axis_size(axis))])  8.34 us
    all_to_all x1, waiting for transfers between devices, shards(): notes = lax.all_to_all(notes, ('pop', 'tp'), 0, 0, tiled=True)  6.82 us
    pallas_call x1, Pallas kernels, step2_call(): pl.pallas_call(functools.partial(step2_kernel, epis=epis), in_specs=[SM,...  4.63 us
    pallas_call x2, Pallas kernels, part_call(): pl.pallas_call(functools.partial(part_kernel, order=order, tail=tail), in...  4.55 us
    all_to_all x1, starting transfers between devices, shards(): notes = lax.all_to_all(notes, ('pop', 'tp'), 0, 0, tiled=True)  4.08 us
    pallas_call x1, Pallas kernels, drive_call(): pl.pallas_call(drive_kernel, in_specs=[HB] * 7, out_specs=[VM] * 3, out_s...  3.95 us
  transfers between devices with their start and end apart: 15, of which 9 were waited for; matrix products, arithmetic and copies ran while one was open for 0% of the time, Pallas kernels for 19%

profile of v4, /device:TPU:0, one launch (start us, length us, event | category | flops | bytes accessed | tf_op | source)
XLA Modules:
  0.0 73.6 jit_solution(9266327010309760788)
XLA Ops:
  0.6 0.5 collective-permute-start
  1.1 4.0 %drive.1 = (f32[72,512]{1,0:T(8,128)}, bf16[8,48,512]{2,1,0:T(8,128)(2,1)}, bf16[2,16,512]{2,1,0:T(8,128)(2,1)}) custom-call(s32[15,4,4096]{2,1,0:T(4,128)} %bitcast.13, bf16[4096,512]{1,0:T(8,128)(2,1)} %win_hbm.1, f32[1,512]{1,0:T(1,128)} %bitcast.14, f32[1,512]{1,0:T(1,128)} %bitcast.15, f32[1,512]{1,0:T(1,128)} %bitcast.16, bf16[256,512]{1,0:T(8,128)(2,1)} %table_hbm.1, ...), custom_call_target="tpu_custom_call" | custom-call | flops 268435456 | bytes 5242880 | tf_op jit(solution)/shard_map/drive/pallas_call | solution.py:117
  5.1 13.2 %all_to_all.21.got_ref.after_ref.rows_ref.refs_4_.refs_3_ = bf16[8,48,512]{2,1,0:T(8,128)(2,1)S(1)} all-to-all(bf16[8,48,512]{2,1,0:T(8,128)(2,1)} %get-tuple-element.28), channel_id=1, replica_groups=mesh['pop'=4,'tp'=8] {'tp'}, dimensions={0} | all-to-all | bytes 786432 | tf_op jit(solution)/shard_map/all_to_all | solution.py:577
  18.4 2.1 %copy-done = bf16[4096,512]{1,0:T(8,128)(2,1)S(1)} copy-done((bf16[4096,512]{1,0:T(8,128)(2,1)S(1)}, bf16[4096,512]{1,0:T(8,128)(2,1)}, u32[]{:S(2)}) %copy-start) | copy-done | bytes 4194328
  20.5 1.7 %base.1 = f32[8,16,512]{2,1,0:T(8,128)} custom-call(bf16[8,48,512]{2,1,0:T(8,128)(2,1)S(1)} %all_to_all.21.got_ref.after_ref.rows_ref.refs_4_.refs_3_, bf16[4096,512]{1,0:T(8,128)(2,1)S(1)} %copy-done, f32[72,512]{1,0:T(8,128)S(1)} %copy-done.1), custom_call_target="tpu_custom_call" | custom-call | flops 67108864 | bytes 4194304 | tf_op jit(solution)/shard_map/base/pallas_call | solution.py:157
  22.2 3.4 %all-to-all-start.1 = ((f32[8,16,512]{2,1,0:T(8,128)}), f32[8,16,512]{2,1,0:T(8,128)S(1)}, u32[]{:S(2)}, u32[]{:S(2)}) async-start(f32[8,16,512]{2,1,0:T(8,128)} %base.1), calls=%async_computation.1 | async-start | bytes 524288 | tf_op jit(solution)/shard_map/all_to_all | solution.py:581
  25.8 1.6 %collective-permute-start.3 = (bf16[10,16,512]{2,1,0:T(8,128)(2,1)S(1)}, bf16[10,16,512]{2,1,0:T(8,128)(2,1)S(1)}, u32[]{:S(2)}, u32[]{:S(2)}) collective-permute-start(bf16[10,16,512]{2,1,0:T(8,128)(2,1)S(1)} %get-tuple-element.32.pack_ref), channel_id=1, source_target_pairs={{0,8},{8,0},{16,24},{24,16},{1,9},{9,1},{17,25},{25,17},{2,10},{10... | collective-permute-start | bytes 491528 | tf_op jit(solution)/shard_map/ppermute | solution.py:559
  27.6 1.2 %collective-permute-done.2.ss_ref.refs_8_ = f32[72,512]{1,0:T(8,128)S(1)} collective-permute-done((f32[72,512]{1,0:T(8,128)S(1)}, f32[72,512]{1,0:T(8,128)S(1)}, u32[]{:S(2)}, u32[]{:S(2)}) %collective-permute-start.2) | collective-permute-done | bytes 147488 | tf_op jit(solution)/shard_map/ppermute | solution.py:559
  28.8 3.6 %collective-permute-done.3.near_ref = bf16[10,16,512]{2,1,0:T(8,128)(2,1)S(1)} collective-permute-done((bf16[10,16,512]{2,1,0:T(8,128)(2,1)S(1)}, bf16[10,16,512]{2,1,0:T(8,128)(2,1)S(1)}, u32[]{:S(2)}, u32[]{:S(2)}) %collective-permute-start.3) | collective-permute-done | bytes 163872 | tf_op jit(solution)/shard_map/ppermute | solution.py:559
  32.5 4.6 %step2.1 = (bf16[240,512]{1,0:T(8,128)(2,1)S(1)}, bf16[240,512]{1,0:T(8,128)(2,1)S(1)}, f32[240,512]{1,0:T(8,128)S(1)}, f32[240,512]{1,0:T(8,128)S(1)}, bf16[2,240,512]{2,1,0:T(8,128)(2,1)S(1)}) custom-call(s32[1]{0:T(128)} %bitcast.2.me_ref, f32[8,16,512]{2,1,0:T(8,128)S(1)} %all-to-all-done.1.base_ref, ...), custom_call_target="tpu_custom_call" | custom-call | flops 2013265920 | bytes 8388608 | tf_op jit(solution)/shard_map/step2/pallas_call | solution.py:266
  37.1 1.6 %collective-permute-start.6 = (bf16[240,512]{1,0:T(8,128)(2,1)S(1)}, bf16[240,512]{1,0:T(8,128)(2,1)S(1)}, u32[]{:S(2)}, u32[]{:S(2)}) collective-permute-start(bf16[240,512]{1,0:T(8,128)(2,1)S(1)} %get-tuple-element.34.s2s_ref), channel_id=1, source_target_pairs={{0,4},{1,5},{2,6},{3,7},{4,0},{5,1},{6,2},{7,3},{8,12},{9,13},{10,... | collective-permute-start | bytes 737288 | tf_op jit(solution)/shard_map/ppermute | solution.py:559
  38.7 1.5 %collective-permute-start.4 = (bf16[240,512]{1,0:T(8,128)(2,1)S(1)}, bf16[240,512]{1,0:T(8,128)(2,1)S(1)}, u32[]{:S(2)}, u32[]{:S(2)}) collective-permute-start(bf16[240,512]{1,0:T(8,128)(2,1)S(1)} %get-tuple-element.33.s2o_ref), channel_id=1, source_target_pairs={{0,2},{1,3},{2,0},{3,1},{4,6},{5,7},{6,4},{7,5},{8,10},{9,11},{10,... | collective-permute-start | bytes 737288 | tf_op jit(solution)/shard_map/ppermute | solution.py:559
  40.2 2.0 %own.1 = (f32[240,512]{1,0:T(8,128)S(1)}, f32[240,512]{1,0:T(8,128)S(1)}, f32[240,128]{1,0:T(8,128)S(1)}, f32[16,128]{1,0:T(8,128)S(1)}, bf16[2,10,16,512]{3,2,1,0:T(8,128)(2,1)S(1)}) custom-call(s32[1]{0:T(128)} %bitcast.2.me_ref, bf16[240,512]{1,0:T(8,128)(2,1)S(1)} %get-tuple-element.33.s2o_ref, bf16[240,512]{1,0:T(8,128)(2,1)S(1)} %get-tuple-element.34.s2s_ref, ...), custom_call_target="tpu_custom_call" | custom-call | flops 503316480 | bytes 2097152 | tf_op jit(solution)/shard_map/own/pallas_call | solution.py:340
  42.3 2.6 %collective-permute-start.10 = (bf16[2,10,16,512]{3,2,1,0:T(8,128)(2,1)S(1)}, bf16[2,10,16,512]{3,2,1,0:T(8,128)(2,1)S(1)}, u32[]{:S(2)}, u32[]{:S(2)}) collective-permute-start(bf16[2,10,16,512]{3,2,1,0:T(8,128)(2,1)S(1)} %get-tuple-element.38.after_ref.refs_0_), channel_id=1, source_target_pairs={{0,16},{8,24},{16,0},{24,8},{1,17},{9,25},{17,1},{25,9},{2,18},{10... | collective-permute-start | bytes 983048 | tf_op jit(solution)/shard_map/ppermute | solution.py:559
  44.9 0.5 collective-permute-start.8
  46.0 1.5 %collective-permute-start.7 = (bf16[240,512]{1,0:T(8,128)(2,1)S(1)}, bf16[240,512]{1,0:T(8,128)(2,1)S(1)}, u32[]{:S(2)}, u32[]{:S(2)}) collective-permute-start(bf16[240,512]{1,0:T(8,128)(2,1)S(1)} %tie.5.refs_1_), channel_id=1, source_target_pairs={{0,2},{1,3},{2,0},{3,1},{4,6},{5,7},{6,4},{7,5},{8,10},{9,11},{10,... | collective-permute-start | bytes 737288 | tf_op jit(solution)/shard_map/ppermute | solution.py:559
  47.5 1.5 %collective-permute-start.5 = (bf16[240,512]{1,0:T(8,128)(2,1)S(1)}, bf16[240,512]{1,0:T(8,128)(2,1)S(1)}, u32[]{:S(2)}, u32[]{:S(2)}) collective-permute-start(bf16[240,512]{1,0:T(8,128)(2,1)S(1)} %tie.4.refs_0_), channel_id=1, source_target_pairs={{0,4},{1,5},{2,6},{3,7},{4,0},{5,1},{6,2},{7,3},{8,12},{9,13},{10,... | collective-permute-start | bytes 737288 | tf_op jit(solution)/shard_map/ppermute | solution.py:559
  49.0 2.5 %part.2 = (f32[240,512]{1,0:T(8,128)S(1)}, f32[240,512]{1,0:T(8,128)S(1)}, f32[240,128]{1,0:T(8,128)S(1)}, bf16[2,2,512,512]{3,2,1,0:T(8,128)(2,1)S(1)}) custom-call(s32[1]{0:T(128)} %bitcast.2.me_ref, bf16[240,512]{1,0:T(8,128)(2,1)S(1)} %tie.4.refs_0_, bf16[240,512]{1,0:T(8,128)(2,1)S(1)} %tie.5.refs_1_, ...), custom_call_target="tpu_custom_call" | custom-call | flops 503316480 | bytes 2097152 | tf_op jit(solution)/shard_map/part/pallas_call | solution.py:376
  51.5 2.3 %collective-permute-done.8.refs_0_ = bf16[240,512]{1,0:T(8,128)(2,1)S(1)} collective-permute-done((bf16[240,512]{1,0:T(8,128)(2,1)S(1)}, bf16[240,512]{1,0:T(8,128)(2,1)S(1)}, u32[]{:S(2)}, u32[]{:S(2)}) %collective-permute-start.8) | collective-permute-done | bytes 245792 | tf_op jit(solution)/shard_map/ppermute | solution.py:559
  54.2 2.0 %part.3 = (f32[240,512]{1,0:T(8,128)S(1)}, f32[240,512]{1,0:T(8,128)S(1)}, f32[240,128]{1,0:T(8,128)S(1)}) custom-call(s32[1]{0:T(128)} %bitcast.2.me_ref, bf16[240,512]{1,0:T(8,128)(2,1)S(1)} %collective-permute-done.8.refs_0_, bf16[240,512]{1,0:T(8,128)(2,1)S(1)} %collective-permute-done.9.refs_1_, ...), custom_call_target="tpu_custom_call" | custom-call | flops 503316480 | bytes 2097152 | tf_op jit(solution)/shard_map/part/pallas_call | solution.py:376
  56.8 1.6 %last.1.after_ref = f32[64,128]{1,0:T(8,128)} custom-call(s32[1]{0:T(128)} %bitcast.2.me_ref, bf16[240,512]{1,0:T(8,128)(2,1)S(1)} %collective-permute-done.5.refs_0_, bf16[240,512]{1,0:T(8,128)(2,1)S(1)} %collective-permute-done.7.refs_1_, bf16[2,2,512,512]{3,2,1,0:T(8,128)(2,1)S(1)} %get-tuple-element.42.refs_2_, ...), custom_call_target="tpu_custom_call" | custom-call | tf_op jit(solution)/shard_map/last/pallas_call | solution.py:423
  58.7 4.1 %all-to-all-start.2 = ((f32[32,2,128]{2,1,0:T(2,128)}), f32[32,2,128]{2,1,0:T(2,128)S(1)}, u32[]{:S(2)}, u32[]{:S(2)}) async-start(f32[32,2,128]{2,1,0:T(2,128)} %bitcast.9), calls=%async_computation.2 | async-start | bytes 65536 | tf_op jit(solution)/shard_map/all_to_all | solution.py:613
  63.3 6.8 %all-to-all-done.2 = f32[32,2,128]{2,1,0:T(2,128)S(1)} async-done(((f32[32,2,128]{2,1,0:T(2,128)}), f32[32,2,128]{2,1,0:T(2,128)S(1)}, u32[]{:S(2)}, u32[]{:S(2)}) %all-to-all-start.2) | async-done | bytes 32800 | tf_op jit(solution)/shard_map/all_to_all | solution.py:613
  70.1 3.5 %grad.1 = (bf16[4096,512]{1,0:T(8,128)(2,1)}, f32[32]{0:T(128)}) custom-call(s32[2]{0:T(128)S(1)} %pad_add_fusion.place_ref, f32[64,128]{1,0:T(8,128)S(1)} %bitcast.11, bf16[4096,128]{1,0:T(8,128)(2,1)S(1)} %get-tuple-element.50.pret_ref, bf16[128,512]{1,0:T(8,128)(2,1)S(1)} %get-tuple-element.51.post_ref), custom_call_target="tpu_custom_call" | custom-call | flops 1073741824 | bytes 5242880 | tf_op jit(solution)/shard_map/grad/pallas_call | solution.py:543
  (30 shorter events, 2.8 us)
Async XLA Ops:
  0.6 17.7 %collective-permute-start = (bf16[4096,512]{1,0:T(8,128)(2,1)}, bf16[4096,512]{1,0:T(8,128)(2,1)}, u32[]{:S(2)}, u32[]{:S(2)}) collective-permute-start(bf16[4096,512]{1,0:T(8,128)(2,1)} %w_hbm.1), channel_id=1, source_target_pairs={{0,1},{1,0},{2,3},{3,2},{4,5},{5,4},{6,7},{7,6},{8,9},{9,8},{10,11... | collective-permute-start | bytes 12582920 | tf_op jit(solution)/shard_map/ppermute | solution.py:559
  18.3 2.2 %copy-start = (bf16[4096,512]{1,0:T(8,128)(2,1)S(1)}, bf16[4096,512]{1,0:T(8,128)(2,1)}, u32[]{:S(2)}) copy-start(bf16[4096,512]{1,0:T(8,128)(2,1)} %w_hbm.1) | copy-start | bytes 12582916
  18.3 2.2 %copy-start.1 = (f32[72,512]{1,0:T(8,128)S(1)}, f32[72,512]{1,0:T(8,128)}, u32[]{:S(2)}) copy-start(f32[72,512]{1,0:T(8,128)} %get-tuple-element.29.side_ref.so_ref.refs_7_) | copy-start | bytes 442372
  18.3 7.3 %copy-start.2 = (bf16[2,16,512]{2,1,0:T(8,128)(2,1)S(1)}, bf16[2,16,512]{2,1,0:T(8,128)(2,1)}, u32[]{:S(2)}) copy-start(bf16[2,16,512]{2,1,0:T(8,128)(2,1)} %get-tuple-element.30.post_ref) | copy-start | bytes 98308
  18.3 14.2 %collective-permute-start.1 = (bf16[4096,512]{1,0:T(8,128)(2,1)}, bf16[4096,512]{1,0:T(8,128)(2,1)}, u32[]{:S(2)}, u32[]{:S(2)}) collective-permute-start(bf16[4096,512]{1,0:T(8,128)(2,1)} %tie.3.ws_hbm.refs_3_), channel_id=1, source_target_pairs={{0,1},{1,0},{2,3},{3,2},{4,5},{5,4},{6,7},{7,6},{8,9},{9,8},{10,11... | collective-permute-start | bytes 12582920 | tf_op jit(solution)/shard_map/ppermute | solution.py:559
  22.2 10.3 %all-to-all-start.1 = ((f32[8,16,512]{2,1,0:T(8,128)}), f32[8,16,512]{2,1,0:T(8,128)S(1)}, u32[]{:S(2)}, u32[]{:S(2)}) async-start(f32[8,16,512]{2,1,0:T(8,128)} %base.1), calls=%async_computation.1 | async-start | bytes 524288 | tf_op jit(solution)/shard_map/all_to_all | solution.py:581
  25.8 6.6 %collective-permute-start.3 = (bf16[10,16,512]{2,1,0:T(8,128)(2,1)S(1)}, bf16[10,16,512]{2,1,0:T(8,128)(2,1)S(1)}, u32[]{:S(2)}, u32[]{:S(2)}) collective-permute-start(bf16[10,16,512]{2,1,0:T(8,128)(2,1)S(1)} %get-tuple-element.32.pack_ref), channel_id=1, source_target_pairs={{0,8},{8,0},{16,24},{24,16},{1,9},{9,1},{17,25},{25,17},{2,10},{10... | collective-permute-start | bytes 491528 | tf_op jit(solution)/shard_map/ppermute | solution.py:559
  27.4 1.4 %collective-permute-start.2 = (f32[72,512]{1,0:T(8,128)S(1)}, f32[72,512]{1,0:T(8,128)S(1)}, u32[]{:S(2)}, u32[]{:S(2)}) collective-permute-start(f32[72,512]{1,0:T(8,128)S(1)} %copy-done.1), channel_id=1, source_target_pairs={{0,1},{1,0},{2,3},{3,2},{4,5},{5,4},{6,7},{7,6},{8,9},{9,8},{10,11... | collective-permute-start | bytes 442376 | tf_op jit(solution)/shard_map/ppermute | solution.py:559
  37.1 8.8 %collective-permute-start.6 = (bf16[240,512]{1,0:T(8,128)(2,1)S(1)}, bf16[240,512]{1,0:T(8,128)(2,1)S(1)}, u32[]{:S(2)}, u32[]{:S(2)}) collective-permute-start(bf16[240,512]{1,0:T(8,128)(2,1)S(1)} %get-tuple-element.34.s2s_ref), channel_id=1, source_target_pairs={{0,4},{1,5},{2,6},{3,7},{4,0},{5,1},{6,2},{7,3},{8,12},{9,13},{10,... | collective-permute-start | bytes 737288 | tf_op jit(solution)/shard_map/ppermute | solution.py:559
  38.7 8.8 %collective-permute-start.4 = (bf16[240,512]{1,0:T(8,128)(2,1)S(1)}, bf16[240,512]{1,0:T(8,128)(2,1)S(1)}, u32[]{:S(2)}, u32[]{:S(2)}) collective-permute-start(bf16[240,512]{1,0:T(8,128)(2,1)S(1)} %get-tuple-element.33.s2o_ref), channel_id=1, source_target_pairs={{0,2},{1,3},{2,0},{3,1},{4,6},{5,7},{6,4},{7,5},{8,10},{9,11},{10,... | collective-permute-start | bytes 737288 | tf_op jit(solution)/shard_map/ppermute | solution.py:559
  42.3 16.4 %collective-permute-start.10 = (bf16[2,10,16,512]{3,2,1,0:T(8,128)(2,1)S(1)}, bf16[2,10,16,512]{3,2,1,0:T(8,128)(2,1)S(1)}, u32[]{:S(2)}, u32[]{:S(2)}) collective-permute-start(bf16[2,10,16,512]{3,2,1,0:T(8,128)(2,1)S(1)} %get-tuple-element.38.after_ref.refs_0_), channel_id=1, source_target_pairs={{0,16},{8,24},{16,0},{24,8},{1,17},{9,25},{17,1},{25,9},{2,18},{10... | collective-permute-start | bytes 983048 | tf_op jit(solution)/shard_map/ppermute | solution.py:559
  44.9 8.9 %collective-permute-start.8 = (bf16[240,512]{1,0:T(8,128)(2,1)S(1)}, bf16[240,512]{1,0:T(8,128)(2,1)S(1)}, u32[]{:S(2)}, u32[]{:S(2)}) collective-permute-start(bf16[240,512]{1,0:T(8,128)(2,1)S(1)} %get-tuple-element.34.s2s_ref), channel_id=1, source_target_pairs={{0,2},{1,3},{2,0},{3,1},{4,6},{5,7},{6,4},{7,5},{8,10},{9,11},{10,... | collective-permute-start | bytes 737288 | tf_op jit(solution)/shard_map/ppermute | solution.py:559
  45.5 8.7 %collective-permute-start.9 = (bf16[240,512]{1,0:T(8,128)(2,1)S(1)}, bf16[240,512]{1,0:T(8,128)(2,1)S(1)}, u32[]{:S(2)}, u32[]{:S(2)}) collective-permute-start(bf16[240,512]{1,0:T(8,128)(2,1)S(1)} %get-tuple-element.33.s2o_ref), channel_id=1, source_target_pairs={{0,4},{1,5},{2,6},{3,7},{4,0},{5,1},{6,2},{7,3},{8,12},{9,13},{10,... | collective-permute-start | bytes 737288 | tf_op jit(solution)/shard_map/ppermute | solution.py:559
  46.0 10.5 %collective-permute-start.7 = (bf16[240,512]{1,0:T(8,128)(2,1)S(1)}, bf16[240,512]{1,0:T(8,128)(2,1)S(1)}, u32[]{:S(2)}, u32[]{:S(2)}) collective-permute-start(bf16[240,512]{1,0:T(8,128)(2,1)S(1)} %tie.5.refs_1_), channel_id=1, source_target_pairs={{0,2},{1,3},{2,0},{3,1},{4,6},{5,7},{6,4},{7,5},{8,10},{9,11},{10,... | collective-permute-start | bytes 737288 | tf_op jit(solution)/shard_map/ppermute | solution.py:559
  47.5 9.3 %collective-permute-start.5 = (bf16[240,512]{1,0:T(8,128)(2,1)S(1)}, bf16[240,512]{1,0:T(8,128)(2,1)S(1)}, u32[]{:S(2)}, u32[]{:S(2)}) collective-permute-start(bf16[240,512]{1,0:T(8,128)(2,1)S(1)} %tie.4.refs_0_), channel_id=1, source_target_pairs={{0,4},{1,5},{2,6},{3,7},{4,0},{5,1},{6,2},{7,3},{8,12},{9,13},{10,... | collective-permute-start | bytes 737288 | tf_op jit(solution)/shard_map/ppermute | solution.py:559
  53.8 9.1 %collective-permute-start.11 = (bf16[2,10,16,512]{3,2,1,0:T(8,128)(2,1)S(1)}, bf16[2,10,16,512]{3,2,1,0:T(8,128)(2,1)S(1)}, u32[]{:S(2)}, u32[]{:S(2)}) collective-permute-start(bf16[2,10,16,512]{3,2,1,0:T(8,128)(2,1)S(1)} %get-tuple-element.38.after_ref.refs_0_), channel_id=1, source_target_pairs={{0,1},{1,0},{2,3},{3,2},{4,5},{5,4},{6,7},{7,6},{8,9},{9,8},{10,11... | collective-permute-start | bytes 983048 | tf_op jit(solution)/shard_map/ppermute | solution.py:559
  54.2 2.6 %copy-start.3 = (s32[32]{0:T(128)S(1)}, s32[32]{0:T(128)}, u32[]{:S(2)}) copy-start(s32[32]{0:T(128)} %param.17) | copy-start | bytes 388
  58.7 4.3 %collective-permute-start.12 = (bf16[2,10,16,512]{3,2,1,0:T(8,128)(2,1)S(1)}, bf16[2,10,16,512]{3,2,1,0:T(8,128)(2,1)S(1)}, u32[]{:S(2)}, u32[]{:S(2)}) collective-permute-start(bf16[2,10,16,512]{3,2,1,0:T(8,128)(2,1)S(1)} %hand.1), channel_id=1, source_target_pairs={{0,1},{1,0},{2,3},{3,2},{4,5},{5,4},{6,7},{7,6},{8,9},{9,8},{10,11... | collective-permute-start | bytes 983048 | tf_op jit(solution)/shard_map/ppermute | solution.py:559
  58.7 11.3 %all-to-all-start.2 = ((f32[32,2,128]{2,1,0:T(2,128)}), f32[32,2,128]{2,1,0:T(2,128)S(1)}, u32[]{:S(2)}, u32[]{:S(2)}) async-start(f32[32,2,128]{2,1,0:T(2,128)} %bitcast.9), calls=%async_computation.2 | async-start | bytes 65536 | tf_op jit(solution)/shard_map/all_to_all | solution.py:613

commit v5 on v4

--- a/solution.py
+++ b/solution.py
@@ -11,7 +11,7 @@
 f32 = jnp.float32
 bf16 = jnp.bfloat16
 i32 = jnp.int32
-L_BASE = 48
+L_BASE = 58
 L_STEP2 = 32
 L_PART = 24
 L_DRIVE = 58
@@ -40,7 +40,6 @@
 
 
 VM = pl.BlockSpec(memory_space=pltpu.VMEM)
-SM = pl.BlockSpec(memory_space=pltpu.SMEM)
 HB = pl.BlockSpec(memory_space=pltpu.HBM)
 sds = jax.ShapeDtypeStruct
 
@@ -56,7 +55,7 @@
 ):
     epis, steps, inputs = spk.shape
     tp = load_ref.shape[0]
-    parts = 4
+    parts = 8
     depth = inputs // parts
     copies = []
     for k in range(parts):
@@ -124,30 +123,32 @@
             sds((2, EP, width), bf16),
         ],
         scratch_shapes=[pltpu.VMEM(x.shape, x.dtype) for x in ins]
-        + [pltpu.VMEM((width // 128, steps * epis, 128), f32), pltpu.SemaphoreType.DMA((13,))],
+        + [pltpu.VMEM((width // 128, steps * epis, 128), f32), pltpu.SemaphoreType.DMA((21,))],
         name="drive",
         **params(L_DRIVE, 2 * steps * EP * inputs * width, inputs * width * 2 + steps * EP * inputs * 4),
     )(*ins)
 
 
-def base_kernel(got_ref, w_hbm, side_ref, out_ref, w_ref, sems):
+def base_kernel(got_hbm, w_hbm, side_hbm, out_ref, got_ref, w_ref, side_ref, sems):
     tp, _, width = got_ref.shape
     lead = side_ref.shape[0] - 8
-    parts = 4
-    depth = w_ref.shape[0] // parts
-    copies = []
-    for k in range(parts):
-        at = pl.ds(k * depth, depth)
-        copies.append(pltpu.make_async_copy(w_hbm.at[at], w_ref.at[at], sems.at[k]))
+    copies = [(got_hbm.at[:, pl.ds(0, EP)], got_ref)]
+    for j in range(tp):
+        at = pl.ds(j * width, width)
+        copies.append((w_hbm.at[at], w_ref.at[at]))
+    copies.append((side_hbm, side_ref))
+    copies = [pltpu.make_async_copy(a, b, sems.at[n]) for n, (a, b) in enumerate(copies)]
     for copy in copies:
         copy.start()
+    copies[0].wait()
+    base = jnp.zeros((EP, width), f32)
+    for j in range(tp):
+        copies[j + 1].wait()
+        base += dot(got_ref[j], w_ref[j * width : (j + 1) * width, :])
+    copies[-1].wait()
     mem0 = side_ref[0:EP, :]
     leak = side_ref[lead : lead + 1, :]
-    base = leak * (mem0 - spike(mem0).astype(f32)) + side_ref[EP : 2 * EP, :]
-    for k in range(parts):
-        copies[k].wait()
-        for j in range(k * tp // parts, (k + 1) * tp // parts):
-            base += dot(got_ref[j, :EP, :], w_ref[j * width : (j + 1) * width, :])
+    base += leak * (mem0 - spike(mem0).astype(f32)) + side_ref[EP : 2 * EP, :]
     for i in range(tp):
         out_ref[i] = base
 
@@ -156,10 +157,15 @@
     tp, _, width = got.shape
     return pl.pallas_call(
         base_kernel,
-        in_specs=[VM, HB, VM],
+        in_specs=[HB, HB, HB],
         out_specs=VM,
         out_shape=sds((tp, EP, width), f32),
-        scratch_shapes=[pltpu.VMEM(w_rec.shape, bf16), pltpu.SemaphoreType.DMA((4,))],
+        scratch_shapes=[
+            pltpu.VMEM((tp, EP, width), bf16),
+            pltpu.VMEM(w_rec.shape, bf16),
+            pltpu.VMEM(side.shape, f32),
+            pltpu.SemaphoreType.DMA((tp + 2,)),
+        ],
         name="base",
         **params(L_BASE, 2 * EP * tp * width * width, tp * width * width * 2),
     )(got, w_rec, side)
@@ -190,13 +196,13 @@
 
 
 def step2_kernel(
-    me_ref, base_ref, rows_ref, wo_hbm, ws_hbm, proj1_ref, so_ref, ss_ref, near_ref,
+    base_ref, rows_ref, wo_hbm, ws_hbm, proj1_ref, so_ref, ss_ref,
     s2o_ref, s2s_ref, memo_ref, mems_ref, s1c_ref,
     s1_ref, wo_ref, ws_ref, acco_ref, accs_ref, p2_ref, sems, *, epis,
 ):
     tp, _, width = base_ref.shape
     lead = so_ref.shape[0] - 8
-    me = me_ref[0]
+    me = lax.axis_index("tp")
 
     def fetch(j):
         at = block_rows(j ^ me, width)
@@ -260,12 +266,12 @@
             s2_ref[at, :] = spike(mem)
 
 
-def step2_call(me, base, got, w_rec, w_sib, proj1, side, side_sib, near, epis):
+def step2_call(base, got, w_rec, w_sib, proj1, side, side_sib, epis):
     tp, _, width = base.shape
     n = epis * EP
     return pl.pallas_call(
         functools.partial(step2_kernel, epis=epis),
-        in_specs=[SM, VM, VM, HB, HB, VM, VM, VM, HB],
+        in_specs=[VM, VM, HB, HB, VM, VM, VM],
         out_specs=[VM] * 5,
         out_shape=[
             sds((n, width), bf16), sds((n, width), bf16), sds((n, width), f32), sds((n, width), f32),
@@ -282,7 +288,7 @@
         ],
         name="step2",
         **params(L_STEP2, 4 * n * tp * width * width, 4 * tp * width * width),
-    )(me, base, got, w_rec, w_sib, proj1, side, side_sib, near)
+    )(base, got, w_rec, w_sib, proj1, side, side_sib)
 
 
 def fetch_blocks(order, me, wo_hbm, ws_hbm, w_ref, sems):
@@ -309,13 +315,13 @@
 
 
 def own_kernel(
-    me_ref, s2o_ref, s2s_ref, wo_hbm, ws_hbm, rows_ref, s1c_ref, memo_ref, mems_ref, so_ref, ss_ref, pack_ref, near_ref,
+    s2o_ref, s2s_ref, wo_hbm, ws_hbm, rows_ref, s1c_ref, memo_ref, mems_ref, so_ref, ss_ref, pack_ref, near_ref,
     acco_ref, accs_ref, p_ref, read_ref, pair_ref, w_ref, sems, *, epis,
 ):
     blocks = (s2o_ref, s2s_ref)
     width = wo_hbm.shape[1]
     lead = so_ref.shape[0] - 8
-    me = me_ref[0]
+    me = lax.axis_index("tp")
     copies = fetch_blocks([0, 1], me, wo_hbm, ws_hbm, w_ref, sems)
     pair_ref[0] = pack_ref[...]
     pair_ref[1] = near_ref[...]
@@ -335,11 +341,11 @@
     add_blocks([0, 1], me, blocks, copies, w_ref, rows_ref, acco_ref, accs_ref, p_ref)
 
 
-def own_call(me, s2o, s2s, w_rec, w_sib, rows, s1c, memo, mems, side, side_sib, pack, near, epis):
+def own_call(s2o, s2s, w_rec, w_sib, rows, s1c, memo, mems, side, side_sib, pack, near, epis):
     n, width = s2o.shape
     return pl.pallas_call(
         functools.partial(own_kernel, epis=epis),
-        in_specs=[SM, VM, VM, HB, HB] + [VM] * 8,
+        in_specs=[VM, VM, HB, HB] + [VM] * 8,
         out_specs=[VM] * 5,
         out_shape=[
             sds((n, width), f32), sds((n, width), f32), sds((n, 128), f32), sds((EP, 128), f32),
@@ -348,14 +354,14 @@
         scratch_shapes=[pltpu.VMEM((2, 2, width, width), bf16), pltpu.SemaphoreType.DMA((2, 2))],
         name="own",
         **params(L_PART, 8 * n * width * width, 8 * width * width),
-    )(me, s2o, s2s, w_rec, w_sib, rows, s1c, memo, mems, side, side_sib, pack, near)
-
-
-def part_kernel(me_ref, *refs, order, tail):
+    )(s2o, s2s, w_rec, w_sib, rows, s1c, memo, mems, side, side_sib, pack, near)
+
+
+def part_kernel(*refs, order, tail):
     blocks, refs = refs[: len(order)], refs[len(order) :]
     wo_hbm, ws_hbm, rows_ref, acco_in, accs_in, p_in, acco_ref, accs_ref, p_ref, *rest = refs
     w_ref, sems = rest[-2:]
-    me = me_ref[0]
+    me = lax.axis_index("tp")
     copies = fetch_blocks(order, me, wo_hbm, ws_hbm, w_ref, sems)
     if tail:
         later = fetch_blocks(tail, me, wo_hbm, ws_hbm, rest[0], rest[1])
@@ -368,28 +374,28 @@
             copy.wait()
 
 
-def part_call(me, blocks, order, w_rec, w_sib, rows, acco, accs, proj, tail=()):
+def part_call(blocks, order, w_rec, w_sib, rows, acco, accs, proj, tail=()):
     n, width = blocks[0].shape
     count = len(order)
     more = [sds((2, len(tail), width, width), bf16)] if tail else []
     sems = [pltpu.SemaphoreType.DMA((2, len(tail)))] if tail else []
     return pl.pallas_call(
         functools.partial(part_kernel, order=order, tail=tail),
-        in_specs=[SM] + [VM] * count + [HB, HB] + [VM] * 4,
+        in_specs=[VM] * count + [HB, HB] + [VM] * 4,
         out_specs=[VM] * (3 + len(more)),
         out_shape=[sds((n, width), f32), sds((n, width), f32), sds((n, 128), f32)] + more,
         scratch_shapes=sems + [pltpu.VMEM((2, count, width, width), bf16), pltpu.SemaphoreType.DMA((2, count))],
         name="part",
         **params(L_PART, 4 * n * count * width * width, 4 * count * width * width),
-    )(me, *blocks, w_rec, w_sib, rows, acco, accs, proj)
-
-
-def last_kernel(me_ref, *refs, order, epis, copies):
+    )(*blocks, w_rec, w_sib, rows, acco, accs, proj)
+
+
+def last_kernel(*refs, order, epis, copies):
     blocks, refs = refs[: len(order)], refs[len(order) :]
     w_ref, rows_ref, acco_in, accs_in, p_in, so_ref, ss_ref, read_ref, ranks_ref = refs[:9]
     note_ref, acco_ref, accs_ref, p_ref = refs[9:]
     lead = so_ref.shape[0] - 8
-    me = me_ref[0]
+    me = lax.axis_index("tp")
     acco_ref[...] = acco_in[...]
     accs_ref[...] = accs_in[...]
     p_ref[...] = p_in[...]
@@ -417,12 +423,12 @@
     note_ref[...] = jnp.where(odd, rank, flat)
 
 
-def last_call(me, blocks, order, tail, rows, acco, accs, proj, side, side_sib, read, ranks, epis, copies):
+def last_call(blocks, order, tail, rows, acco, accs, proj, side, side_sib, read, ranks, epis, copies):
     n, width = blocks[0].shape
     count = len(order)
     return pl.pallas_call(
         functools.partial(last_kernel, order=order, epis=epis, copies=copies),
-        in_specs=[SM] + [VM] * (count + 9),
+        in_specs=[VM] * (count + 9),
         out_specs=VM,
         out_shape=sds((2 * copies, 128), f32),
         scratch_shapes=[
@@ -432,7 +438,7 @@
         ],
         name="last",
         **params(L_LAST, 0, 0),
-    )(me, *blocks, tail, rows, acco, accs, proj, side, side_sib, read, ranks)
+    )(*blocks, tail, rows, acco, accs, proj, side, side_sib, read, ranks)
 
 
 def tie_kernel(x_ref, after_ref, out_ref):
@@ -466,7 +472,7 @@
     )(x, after)
 
 
-def prep_kernel(core_ref, *refs, pop):
+def prep_kernel(*refs, pop):
     groups, (pret_ref, post_ref) = refs[:pop], refs[pop:]
     tp = groups[0].shape[1] - 2
     width = groups[0].shape[3]
@@ -476,25 +482,25 @@
     for d in range(2):
         for s in range(pop):
             at = (d * pop + s) * EP
-            post_ref[at : at + EP, :] = groups[s // 2][s % 2, tp + (d ^ core_ref[0])]
-
-
-def prep_call(core, groups, pop):
+            post_ref[at : at + EP, :] = groups[s // 2][s % 2, tp + (d ^ (lax.axis_index("tp") & 1))]
+
+
+def prep_call(groups, pop):
     _, blocks, _, width = groups[0].shape
     count = 2 * pop * EP
     return pl.pallas_call(
         functools.partial(prep_kernel, pop=pop),
-        in_specs=[SM] + [VM] * len(groups),
+        in_specs=[VM] * len(groups),
         out_specs=[VM] * 2,
         out_shape=[sds(((blocks - 2) * width, count), bf16), sds((count, width), bf16)],
         name="prep",
         **params(16, count * blocks * width, 4 * count * blocks * width),
-    )(core, *groups)
-
-
-def grad_kernel(place_ref, note_ref, pret_ref, post_ref, grad_hbm, ret_ref, both_ref, grad_ref, sems, *, tp, pop, plays):
+    )(*groups)
+
+
+def grad_kernel(note_ref, pret_ref, post_ref, grad_hbm, ret_ref, both_ref, grad_ref, sems, *, tp, pop, plays):
     count = post_ref.shape[0]
-    plane, core = place_ref[0], place_ref[1]
+    plane, core = lax.axis_index("pop"), lax.axis_index("tp") & 1
     shift = tp.bit_length() - 1
     notes = note_ref[...]
 
@@ -537,12 +543,12 @@
     lax.fori_loop(0, inputs // block, lambda i, _: (out(i).wait(), 0)[1], 0)
 
 
-def grad_call(place, notes, pret, post, tp, pop, plays, members):
+def grad_call(notes, pret, post, tp, pop, plays, members):
     inputs, count = pret.shape
     width = post.shape[1]
     return pl.pallas_call(
         functools.partial(grad_kernel, tp=tp, pop=pop, plays=plays),
-        in_specs=[SM] + [VM] * 3,
+        in_specs=[VM] * 3,
         out_specs=[HB, VM],
         out_shape=[sds((inputs, width), bf16), sds((members,), f32)],
         scratch_shapes=[
@@ -552,7 +558,7 @@
         ],
         name="grad",
         **params(16, 4 * inputs * count * width, 2 * inputs * (count + width)),
-    )(place, notes, pret, post)
+    )(notes, pret, post)
 
 
 def swap(x, axis, mask):
@@ -566,22 +572,20 @@
     members = pert_idx.shape[0]
     tp, pop = lax.axis_size("tp"), lax.axis_size("pop")
     assert steps == 4 and epis < EP and members == 2 * EP
-    me, plane = lax.axis_index("tp"), lax.axis_index("pop")
-    at = me[None].astype(i32)
-    place = jnp.stack([plane, me & 1]).astype(i32)
 
     w_sib = swap(w_rec, "tp", 1)
     side, load, post_loc = drive_call(
         in_spikes, w_in, neuron_bias, leak_rate, readout, pert_table, pert_idx, tp
     )
     got = lax.all_to_all(load, "tp", 0, 0)
-    w_sib = tie_call(w_sib, got)
+    side_sib = swap(side, "tp", 1)
+    base = base_call(got, w_rec, side)
+    w_sib = tie_call(w_sib, base)
     w_own = swap(w_sib, "tp", 1)
-    side_sib = swap(side, "tp", 1)
-    base = lax.all_to_all(base_call(got, w_rec, side), "tp", 0, 0)
+    base = lax.all_to_all(base, "tp", 0, 0)
     proj1, pack = proj_call(got, post_loc)
     near = swap(pack, "pop", 1)
-    s2o, s2s, memo, mems, s1c = step2_call(at, base, got, w_own, w_sib, proj1, side, side_sib, near, epis)
+    s2o, s2s, memo, mems, s1c = step2_call(base, got, w_own, w_sib, proj1, side, side_sib, epis)
     far, order = [], []
     if tp == 8:
         xa, yb = swap(s2o, "tp", 2), swap(s2s, "tp", 4)
@@ -591,7 +595,7 @@
             far += [swap(s2o, "tp", mask), swap(s2s, "tp", mask)]
             order += [mask, mask + 1]
     acco, accs, proj, read, pair = own_call(
-        at, s2o, s2s, w_own, w_sib, got, s1c, memo, mems, side, side_sib, pack, near, epis
+        s2o, s2s, w_own, w_sib, got, s1c, memo, mems, side, side_sib, pack, near, epis
     )
     if tp == 8:
         xa, yb = tie_call(xa, pair), tie_call(yb, pair)
@@ -599,11 +603,11 @@
         end, ends = [swap(xa, "tp", 4), swap(yb, "tp", 2)], [6, 7]
     else:
         far, end, order, ends = far[:-2], far[-2:], order[:-2], order[-2:]
-    acco, accs, proj, tail = part_call(at, far, order, w_own, w_sib, got, acco, accs, proj, tuple(ends))
+    acco, accs, proj, tail = part_call(far, order, w_own, w_sib, got, acco, accs, proj, tuple(ends))
     if tp == 8:
-        acco, accs, proj = part_call(at, [xb, ya], [3, 4], w_own, w_sib, got, acco, accs, proj)
+        acco, accs, proj = part_call([xb, ya], [3, 4], w_own, w_sib, got, acco, accs, proj)
     notes = last_call(
-        at, end, ends, tail, got, acco, accs, proj, side, side_sib, read, member_ranks[None], epis, pop * tp
+        end, ends, tail, got, acco, accs, proj, side, side_sib, read, member_ranks[None], epis, pop * tp
     )
     groups, mask = [pair], 2
     while mask < pop:
@@ -611,8 +615,8 @@
         mask *= 2
     groups += [swap(g, "tp", 1) for g in groups[:1]] + [swap(hand_call(g, notes), "tp", 1) for g in groups[1:]]
     notes = lax.all_to_all(notes, ("pop", "tp"), 0, 0, tiled=True)
-    pret, post_all = prep_call(place[1:], groups, pop)
-    grad, returns = grad_call(place, notes, pret, post_all, tp, pop, epis * steps, members)
+    pret, post_all = prep_call(groups, pop)
+    grad, returns = grad_call(notes, pret, post_all, tp, pop, epis * steps, members)
     return (returns, grad)
 
 

time: 74.1 us -> 72.9 us (0.984)
  local copies, waits for them, and re-layouts: 2.1 us -> 0.02 us
  Pallas kernels: 22.5 us -> 23.4 us
    all_to_all x1, waiting for transfers between devices: 0.15 us -> 3.03 us  [shards(): base = lax.all_to_all(base, 'tp', 0, 0)]
    ppermute x13, waiting for transfers between devices: 8.34 us -> 5.62 us  [swap(): lax.ppermute(x, axis, [(i, i ^ mask) for i in range(lax.axis_size(axis))])]
    unnamed x8, local copies, waits for them, and re-layouts: 2.1 us -> 0.02 us
    pallas_call x4, Pallas kernels: 8.72 us -> 10.2 us  [the longest x1 4.64 us: step2_call(): pl.pallas_call(functools.partial(step2_kernel, epis=epis), in_specs=[VM,...]
    ppermute x13, starting transfers between devices: 12.2 us -> 10.8 us  [swap(): lax.ppermute(x, axis, [(i, i ^ mask) for i in range(lax.axis_size(axis))])]
    all_to_all x1, starting transfers between devices: 4.08 us -> 5.14 us  [shards(): notes = lax.all_to_all(notes, ('pop', 'tp'), 0, 0, tiled=True)]
  transfers between devices with their start and end apart: 15 -> 15, of which waited for: 9 -> 6; matrix products, arithmetic and copies ran while one was open for 0% -> 0% of each run, Pallas kernels for 19% -> 28%
where the time goes in v5:
time: 72.9 us; the launch traced here: 72.5 us
  Pallas kernels  23.4 us (32%)
  starting transfers between devices  19.5 us (27%)
  waiting for transfers between devices  15.5 us (21%)
  blocking collectives  13.3 us (18%)
  between operations  0.8 us (1%)
    all_to_all x1, blocking collectives, shards(): got = lax.all_to_all(load, 'tp', 0, 0)  13.3 us
    ppermute x13, starting transfers between devices, swap(): lax.ppermute(x, axis, [(i, i ^ mask) for i in range(lax.axis_size(axis))])  10.8 us
    all_to_all x1, waiting for transfers between devices, shards(): notes = lax.all_to_all(notes, ('pop', 'tp'), 0, 0, tiled=True)  6.88 us
    ppermute x13, waiting for transfers between devices, swap(): lax.ppermute(x, axis, [(i, i ^ mask) for i in range(lax.axis_size(axis))])  5.62 us
    all_to_all x1, starting transfers between devices, shards(): notes = lax.all_to_all(notes, ('pop', 'tp'), 0, 0, tiled=True)  5.14 us
    pallas_call x1, Pallas kernels, step2_call(): pl.pallas_call(functools.partial(step2_kernel, epis=epis), in_specs=[VM,...  4.64 us
    pallas_call x2, Pallas kernels, part_call(): pl.pallas_call(functools.partial(part_kernel, order=order, tail=tail), in...  4.51 us
    pallas_call x1, Pallas kernels, drive_call(): pl.pallas_call(drive_kernel, in_specs=[HB] * 7, out_specs=[VM] * 3, out_s...  3.88 us
  transfers between devices with their start and end apart: 15, of which 6 were waited for; matrix products, arithmetic and copies ran while one was open for 0% of the time, Pallas kernels for 28%

profile of v5, /device:TPU:0, one launch (start us, length us, event | category | flops | bytes accessed | tf_op | source)
XLA Modules:
  0.0 72.5 jit_solution(11014979532397229227)
XLA Ops:
  1.1 3.9 %drive.1 = (f32[72,512]{1,0:T(8,128)}, bf16[8,48,512]{2,1,0:T(8,128)(2,1)}, bf16[2,16,512]{2,1,0:T(8,128)(2,1)}) custom-call(s32[15,4,4096]{2,1,0:T(4,128)} %bitcast.10, bf16[4096,512]{1,0:T(8,128)(2,1)} %win_hbm.1, f32[1,512]{1,0:T(1,128)} %bitcast.11, f32[1,512]{1,0:T(1,128)} %bitcast.12, f32[1,512]{1,0:T(1,128)} %bitcast.13, bf16[256,512]{1,0:T(8,128)(2,1)} %table_hbm.1, ...), custom_call_target="tpu_custom_call" | custom-call | flops 268435456 | bytes 5242880 | tf_op jit(solution)/shard_map/drive/pallas_call | solution.py:116
  5.0 13.3 %all_to_all.21.got_hbm.got_ref.rows_ref.refs_4_.refs_3_ = bf16[8,48,512]{2,1,0:T(8,128)(2,1)} all-to-all(bf16[8,48,512]{2,1,0:T(8,128)(2,1)} %get-tuple-element.28), channel_id=1, replica_groups=mesh['pop'=4,'tp'=8] {'tp'}, dimensions={0} | all-to-all | bytes 786432 | tf_op jit(solution)/shard_map/all_to_all | solution.py:580
  18.4 3.2 %base.1.after_ref = f32[8,16,512]{2,1,0:T(8,128)} custom-call(bf16[8,48,512]{2,1,0:T(8,128)(2,1)} %all_to_all.21.got_hbm.got_ref.rows_ref.refs_4_.refs_3_, bf16[4096,512]{1,0:T(8,128)(2,1)} %w_hbm.1, f32[72,512]{1,0:T(8,128)} %get-tuple-element.29.side_hbm.so_ref.refs_7_), custom_call_target="tpu_custom_call" | custom-call | flops 67108864 | bytes 4194304 | tf_op jit(solution)/shard_map/base/pallas_call | solution.py:158
  21.7 3.6 %all-to-all-start.1 = ((f32[8,16,512]{2,1,0:T(8,128)}), f32[8,16,512]{2,1,0:T(8,128)S(1)}, u32[]{:S(2)}, u32[]{:S(2)}) async-start(f32[8,16,512]{2,1,0:T(8,128)} %base.1.after_ref), calls=%async_computation.1 | async-start | bytes 524288 | tf_op jit(solution)/shard_map/all_to_all | solution.py:585
  25.9 1.7 %collective-permute-start.4 = (bf16[10,16,512]{2,1,0:T(8,128)(2,1)S(1)}, bf16[10,16,512]{2,1,0:T(8,128)(2,1)S(1)}, u32[]{:S(2)}, u32[]{:S(2)}) collective-permute-start(bf16[10,16,512]{2,1,0:T(8,128)(2,1)S(1)} %get-tuple-element.37.pack_ref), channel_id=1, source_target_pairs={{0,8},{8,0},{16,24},{24,16},{1,9},{9,1},{17,25},{25,17},{2,10},{10... | collective-permute-start | bytes 491528 | tf_op jit(solution)/shard_map/ppermute | solution.py:565
  27.6 1.6 %collective-permute-done.2.ss_ref.refs_8_ = f32[72,512]{1,0:T(8,128)S(1)} collective-permute-done((f32[72,512]{1,0:T(8,128)S(1)}, f32[72,512]{1,0:T(8,128)S(1)}, u32[]{:S(2)}, u32[]{:S(2)}) %collective-permute-start.2) | collective-permute-done | bytes 147488 | tf_op jit(solution)/shard_map/ppermute | solution.py:565
  29.1 3.0 %all-to-all-done.1.base_ref = f32[8,16,512]{2,1,0:T(8,128)S(1)} async-done(((f32[8,16,512]{2,1,0:T(8,128)}), f32[8,16,512]{2,1,0:T(8,128)S(1)}, u32[]{:S(2)}, u32[]{:S(2)}) %all-to-all-start.1) | async-done | bytes 262176 | tf_op jit(solution)/shard_map/all_to_all | solution.py:585
  32.2 4.6 %step2.1 = (bf16[240,512]{1,0:T(8,128)(2,1)S(1)}, bf16[240,512]{1,0:T(8,128)(2,1)S(1)}, f32[240,512]{1,0:T(8,128)S(1)}, f32[240,512]{1,0:T(8,128)S(1)}, bf16[2,240,512]{2,1,0:T(8,128)(2,1)S(1)}) custom-call(f32[8,16,512]{2,1,0:T(8,128)S(1)} %all-to-all-done.1.base_ref, bf16[8,48,512]{2,1,0:T(8,128)(2,1)S(1)} %copy-done, ...), custom_call_target="tpu_custom_call" | custom-call | flops 2013265920 | bytes 8388608 | tf_op jit(solution)/shard_map/step2/pallas_call | solution.py:272
  36.8 0.6 collective-permute-start.6
  37.4 0.6 collective-permute-start.3
  38.0 2.0 %own.1 = (f32[240,512]{1,0:T(8,128)S(1)}, f32[240,512]{1,0:T(8,128)S(1)}, f32[240,128]{1,0:T(8,128)S(1)}, f32[16,128]{1,0:T(8,128)S(1)}, bf16[2,10,16,512]{3,2,1,0:T(8,128)(2,1)S(1)}) custom-call(bf16[240,512]{1,0:T(8,128)(2,1)S(1)} %get-tuple-element.32.s2o_ref, bf16[240,512]{1,0:T(8,128)(2,1)S(1)} %get-tuple-element.33.s2s_ref, ...), custom_call_target="tpu_custom_call" | custom-call | flops 503316480 | bytes 2097152 | tf_op jit(solution)/shard_map/own/pallas_call | solution.py:346
  40.0 2.8 %collective-permute-start.10 = (bf16[2,10,16,512]{3,2,1,0:T(8,128)(2,1)S(1)}, bf16[2,10,16,512]{3,2,1,0:T(8,128)(2,1)S(1)}, u32[]{:S(2)}, u32[]{:S(2)}) collective-permute-start(bf16[2,10,16,512]{3,2,1,0:T(8,128)(2,1)S(1)} %get-tuple-element.38.after_ref.refs_0_), channel_id=1, source_target_pairs={{0,16},{8,24},{16,0},{24,8},{1,17},{9,25},{17,1},{25,9},{2,18},{10... | collective-permute-start | bytes 983048 | tf_op jit(solution)/shard_map/ppermute | solution.py:565
  42.8 1.5 %collective-permute-start.8 = (bf16[240,512]{1,0:T(8,128)(2,1)S(1)}, bf16[240,512]{1,0:T(8,128)(2,1)S(1)}, u32[]{:S(2)}, u32[]{:S(2)}) collective-permute-start(bf16[240,512]{1,0:T(8,128)(2,1)S(1)} %get-tuple-element.33.s2s_ref), channel_id=1, source_target_pairs={{0,2},{1,3},{2,0},{3,1},{4,6},{5,7},{6,4},{7,5},{8,10},{9,11},{10,... | collective-permute-start | bytes 737288 | tf_op jit(solution)/shard_map/ppermute | solution.py:565
  44.3 1.4 %collective-permute-start.9 = (bf16[240,512]{1,0:T(8,128)(2,1)S(1)}, bf16[240,512]{1,0:T(8,128)(2,1)S(1)}, u32[]{:S(2)}, u32[]{:S(2)}) collective-permute-start(bf16[240,512]{1,0:T(8,128)(2,1)S(1)} %get-tuple-element.32.s2o_ref), channel_id=1, source_target_pairs={{0,4},{1,5},{2,6},{3,7},{4,0},{5,1},{6,2},{7,3},{8,12},{9,13},{10,... | collective-permute-start | bytes 737288 | tf_op jit(solution)/shard_map/ppermute | solution.py:565
  46.3 0.6 collective-permute-start.5
  46.9 2.5 %part.2 = (f32[240,512]{1,0:T(8,128)S(1)}, f32[240,512]{1,0:T(8,128)S(1)}, f32[240,128]{1,0:T(8,128)S(1)}, bf16[2,2,512,512]{3,2,1,0:T(8,128)(2,1)S(1)}) custom-call(bf16[240,512]{1,0:T(8,128)(2,1)S(1)} %tie.4.refs_0_, bf16[240,512]{1,0:T(8,128)(2,1)S(1)} %tie.5.refs_1_, bf16[4096,512]{1,0:T(8,128)(2,1)} %collective-permute-done.1.wo_hbm.refs_2_, ...), custom_call_target="tpu_custom_call" | custom-call | flops 503316480 | bytes 2097152 | tf_op jit(solution)/shard_map/part/pallas_call | solution.py:382
  49.4 2.3 %collective-permute-done.8.refs_0_ = bf16[240,512]{1,0:T(8,128)(2,1)S(1)} collective-permute-done((bf16[240,512]{1,0:T(8,128)(2,1)S(1)}, bf16[240,512]{1,0:T(8,128)(2,1)S(1)}, u32[]{:S(2)}, u32[]{:S(2)}) %collective-permute-start.8) | collective-permute-done | bytes 245792 | tf_op jit(solution)/shard_map/ppermute | solution.py:565
  51.7 1.1 %collective-permute-done.9.refs_1_ = bf16[240,512]{1,0:T(8,128)(2,1)S(1)} collective-permute-done((bf16[240,512]{1,0:T(8,128)(2,1)S(1)}, bf16[240,512]{1,0:T(8,128)(2,1)S(1)}, u32[]{:S(2)}, u32[]{:S(2)}) %collective-permute-start.9) | collective-permute-done | bytes 245792 | tf_op jit(solution)/shard_map/ppermute | solution.py:565
  52.8 2.0 %part.3 = (f32[240,512]{1,0:T(8,128)S(1)}, f32[240,512]{1,0:T(8,128)S(1)}, f32[240,128]{1,0:T(8,128)S(1)}) custom-call(bf16[240,512]{1,0:T(8,128)(2,1)S(1)} %collective-permute-done.8.refs_0_, bf16[240,512]{1,0:T(8,128)(2,1)S(1)} %collective-permute-done.9.refs_1_, bf16[4096,512]{1,0:T(8,128)(2,1)} %collective-permute-done.1.wo_hbm.refs_2_, ...), custom_call_target="tpu_custom_call" | custom-call | flops 503316480 | bytes 2097152 | tf_op jit(solution)/shard_map/part/pallas_call | solution.py:382
  54.8 0.6 collective-permute-done.5.refs_0_
  55.4 1.6 %last.1.after_ref = f32[64,128]{1,0:T(8,128)} custom-call(bf16[240,512]{1,0:T(8,128)(2,1)S(1)} %collective-permute-done.5.refs_0_, bf16[240,512]{1,0:T(8,128)(2,1)S(1)} %collective-permute-done.7.refs_1_, bf16[2,2,512,512]{3,2,1,0:T(8,128)(2,1)S(1)} %get-tuple-element.42.refs_2_, bf16[8,48,512]{2,1,0:T(8,128)(2,1)S(1)} %copy-done, ...), custom_call_target="tpu_custom_call" | custom-call | tf_op jit(solution)/shard_map/last/pallas_call | solution.py:429
  57.1 5.1 %all-to-all-start.2 = ((f32[32,2,128]{2,1,0:T(2,128)}), f32[32,2,128]{2,1,0:T(2,128)S(1)}, u32[]{:S(2)}, u32[]{:S(2)}) async-start(f32[32,2,128]{2,1,0:T(2,128)} %bitcast.6), calls=%async_computation.2 | async-start | bytes 65536 | tf_op jit(solution)/shard_map/all_to_all | solution.py:617
  62.6 6.9 %all-to-all-done.2 = f32[32,2,128]{2,1,0:T(2,128)S(1)} async-done(((f32[32,2,128]{2,1,0:T(2,128)}), f32[32,2,128]{2,1,0:T(2,128)S(1)}, u32[]{:S(2)}, u32[]{:S(2)}) %all-to-all-start.2) | async-done | bytes 32800 | tf_op jit(solution)/shard_map/all_to_all | solution.py:617
  69.5 3.0 %grad.1 = (bf16[4096,512]{1,0:T(8,128)(2,1)}, f32[32]{0:T(128)}) custom-call(f32[64,128]{1,0:T(8,128)S(1)} %bitcast.8, bf16[4096,128]{1,0:T(8,128)(2,1)S(1)} %get-tuple-element.50.pret_ref, bf16[128,512]{1,0:T(8,128)(2,1)S(1)} %get-tuple-element.51.post_ref), custom_call_target="tpu_custom_call" | custom-call | flops 1073741824 | bytes 5242880 | tf_op jit(solution)/shard_map/grad/pallas_call | solution.py:549
  (29 shorter events, 2.2 us)
Async XLA Ops:
  0.6 21.0 %collective-permute-start = (bf16[4096,512]{1,0:T(8,128)(2,1)}, bf16[4096,512]{1,0:T(8,128)(2,1)}, u32[]{:S(2)}, u32[]{:S(2)}) collective-permute-start(bf16[4096,512]{1,0:T(8,128)(2,1)} %w_hbm.1), channel_id=1, source_target_pairs={{0,1},{1,0},{2,3},{3,2},{4,5},{5,4},{6,7},{7,6},{8,9},{9,8},{10,11... | collective-permute-start | bytes 12582920 | tf_op jit(solution)/shard_map/ppermute | solution.py:565
  21.6 3.7 %copy-start.1 = (f32[72,512]{1,0:T(8,128)S(1)}, f32[72,512]{1,0:T(8,128)}, u32[]{:S(2)}) copy-start(f32[72,512]{1,0:T(8,128)} %get-tuple-element.29.side_hbm.so_ref.refs_7_) | copy-start | bytes 442372
  21.6 4.1 %copy-start = (bf16[8,48,512]{2,1,0:T(8,128)(2,1)S(1)}, bf16[8,48,512]{2,1,0:T(8,128)(2,1)}, u32[]{:S(2)}) copy-start(bf16[8,48,512]{2,1,0:T(8,128)(2,1)} %all_to_all.21.got_hbm.got_ref.rows_ref.refs_4_.refs_3_) | copy-start | bytes 1179652
  21.6 4.1 %copy-start.2 = (bf16[2,16,512]{2,1,0:T(8,128)(2,1)S(1)}, bf16[2,16,512]{2,1,0:T(8,128)(2,1)}, u32[]{:S(2)}) copy-start(bf16[2,16,512]{2,1,0:T(8,128)(2,1)} %get-tuple-element.30.post_ref) | copy-start | bytes 98308
  21.7 10.5 %collective-permute-start.1 = (bf16[4096,512]{1,0:T(8,128)(2,1)}, bf16[4096,512]{1,0:T(8,128)(2,1)}, u32[]{:S(2)}, u32[]{:S(2)}) collective-permute-start(bf16[4096,512]{1,0:T(8,128)(2,1)} %tie.3.ws_hbm.refs_3_), channel_id=1, source_target_pairs={{0,1},{1,0},{2,3},{3,2},{4,5},{5,4},{6,7},{7,6},{8,9},{9,8},{10,11... | collective-permute-start | bytes 12582920 | tf_op jit(solution)/shard_map/ppermute | solution.py:565
  21.7 10.4 %all-to-all-start.1 = ((f32[8,16,512]{2,1,0:T(8,128)}), f32[8,16,512]{2,1,0:T(8,128)S(1)}, u32[]{:S(2)}, u32[]{:S(2)}) async-start(f32[8,16,512]{2,1,0:T(8,128)} %base.1.after_ref), calls=%async_computation.1 | async-start | bytes 524288 | tf_op jit(solution)/shard_map/all_to_all | solution.py:585
  25.3 3.8 %collective-permute-start.2 = (f32[72,512]{1,0:T(8,128)S(1)}, f32[72,512]{1,0:T(8,128)S(1)}, u32[]{:S(2)}, u32[]{:S(2)}) collective-permute-start(f32[72,512]{1,0:T(8,128)S(1)} %copy-done.1), channel_id=1, source_target_pairs={{0,1},{1,0},{2,3},{3,2},{4,5},{5,4},{6,7},{7,6},{8,9},{9,8},{10,11... | collective-permute-start | bytes 442376 | tf_op jit(solution)/shard_map/ppermute | solution.py:565
  25.9 12.1 %collective-permute-start.4 = (bf16[10,16,512]{2,1,0:T(8,128)(2,1)S(1)}, bf16[10,16,512]{2,1,0:T(8,128)(2,1)S(1)}, u32[]{:S(2)}, u32[]{:S(2)}) collective-permute-start(bf16[10,16,512]{2,1,0:T(8,128)(2,1)S(1)} %get-tuple-element.37.pack_ref), channel_id=1, source_target_pairs={{0,8},{8,0},{16,24},{24,16},{1,9},{9,1},{17,25},{25,17},{2,10},{10... | collective-permute-start | bytes 491528 | tf_op jit(solution)/shard_map/ppermute | solution.py:565
  36.8 8.9 %collective-permute-start.6 = (bf16[240,512]{1,0:T(8,128)(2,1)S(1)}, bf16[240,512]{1,0:T(8,128)(2,1)S(1)}, u32[]{:S(2)}, u32[]{:S(2)}) collective-permute-start(bf16[240,512]{1,0:T(8,128)(2,1)S(1)} %get-tuple-element.33.s2s_ref), channel_id=1, source_target_pairs={{0,4},{1,5},{2,6},{3,7},{4,0},{5,1},{6,2},{7,3},{8,12},{9,13},{10,... | collective-permute-start | bytes 737288 | tf_op jit(solution)/shard_map/ppermute | solution.py:565
  37.4 8.8 %collective-permute-start.3 = (bf16[240,512]{1,0:T(8,128)(2,1)S(1)}, bf16[240,512]{1,0:T(8,128)(2,1)S(1)}, u32[]{:S(2)}, u32[]{:S(2)}) collective-permute-start(bf16[240,512]{1,0:T(8,128)(2,1)S(1)} %get-tuple-element.32.s2o_ref), channel_id=1, source_target_pairs={{0,2},{1,3},{2,0},{3,1},{4,6},{5,7},{6,4},{7,5},{8,10},{9,11},{10,... | collective-permute-start | bytes 737288 | tf_op jit(solution)/shard_map/ppermute | solution.py:565
  40.0 17.0 %collective-permute-start.10 = (bf16[2,10,16,512]{3,2,1,0:T(8,128)(2,1)S(1)}, bf16[2,10,16,512]{3,2,1,0:T(8,128)(2,1)S(1)}, u32[]{:S(2)}, u32[]{:S(2)}) collective-permute-start(bf16[2,10,16,512]{3,2,1,0:T(8,128)(2,1)S(1)} %get-tuple-element.38.after_ref.refs_0_), channel_id=1, source_target_pairs={{0,16},{8,24},{16,0},{24,8},{1,17},{9,25},{17,1},{25,9},{2,18},{10... | collective-permute-start | bytes 983048 | tf_op jit(solution)/shard_map/ppermute | solution.py:565
  42.8 8.9 %collective-permute-start.8 = (bf16[240,512]{1,0:T(8,128)(2,1)S(1)}, bf16[240,512]{1,0:T(8,128)(2,1)S(1)}, u32[]{:S(2)}, u32[]{:S(2)}) collective-permute-start(bf16[240,512]{1,0:T(8,128)(2,1)S(1)} %get-tuple-element.33.s2s_ref), channel_id=1, source_target_pairs={{0,2},{1,3},{2,0},{3,1},{4,6},{5,7},{6,4},{7,5},{8,10},{9,11},{10,... | collective-permute-start | bytes 737288 | tf_op jit(solution)/shard_map/ppermute | solution.py:565
  44.3 8.5 %collective-permute-start.9 = (bf16[240,512]{1,0:T(8,128)(2,1)S(1)}, bf16[240,512]{1,0:T(8,128)(2,1)S(1)}, u32[]{:S(2)}, u32[]{:S(2)}) collective-permute-start(bf16[240,512]{1,0:T(8,128)(2,1)S(1)} %get-tuple-element.32.s2o_ref), channel_id=1, source_target_pairs={{0,4},{1,5},{2,6},{3,7},{4,0},{5,1},{6,2},{7,3},{8,12},{9,13},{10,... | collective-permute-start | bytes 737288 | tf_op jit(solution)/shard_map/ppermute | solution.py:565
  45.7 9.1 %collective-permute-start.7 = (bf16[240,512]{1,0:T(8,128)(2,1)S(1)}, bf16[240,512]{1,0:T(8,128)(2,1)S(1)}, u32[]{:S(2)}, u32[]{:S(2)}) collective-permute-start(bf16[240,512]{1,0:T(8,128)(2,1)S(1)} %tie.5.refs_1_), channel_id=1, source_target_pairs={{0,2},{1,3},{2,0},{3,1},{4,6},{5,7},{6,4},{7,5},{8,10},{9,11},{10,... | collective-permute-start | bytes 737288 | tf_op jit(solution)/shard_map/ppermute | solution.py:565
  46.3 9.1 %collective-permute-start.5 = (bf16[240,512]{1,0:T(8,128)(2,1)S(1)}, bf16[240,512]{1,0:T(8,128)(2,1)S(1)}, u32[]{:S(2)}, u32[]{:S(2)}) collective-permute-start(bf16[240,512]{1,0:T(8,128)(2,1)S(1)} %tie.4.refs_0_), channel_id=1, source_target_pairs={{0,4},{1,5},{2,6},{3,7},{4,0},{5,1},{6,2},{7,3},{8,12},{9,13},{10,... | collective-permute-start | bytes 737288 | tf_op jit(solution)/shard_map/ppermute | solution.py:565
  51.7 10.6 %collective-permute-start.11 = (bf16[2,10,16,512]{3,2,1,0:T(8,128)(2,1)S(1)}, bf16[2,10,16,512]{3,2,1,0:T(8,128)(2,1)S(1)}, u32[]{:S(2)}, u32[]{:S(2)}) collective-permute-start(bf16[2,10,16,512]{3,2,1,0:T(8,128)(2,1)S(1)} %get-tuple-element.38.after_ref.refs_0_), channel_id=1, source_target_pairs={{0,1},{1,0},{2,3},{3,2},{4,5},{5,4},{6,7},{7,6},{8,9},{9,8},{10,11... | collective-permute-start | bytes 983048 | tf_op jit(solution)/shard_map/ppermute | solution.py:565
  52.8 2.6 %copy-start.3 = (s32[32]{0:T(128)S(1)}, s32[32]{0:T(128)}, u32[]{:S(2)}) copy-start(s32[32]{0:T(128)} %param.17) | copy-start | bytes 388
  57.0 5.2 %collective-permute-start.12 = (bf16[2,10,16,512]{3,2,1,0:T(8,128)(2,1)S(1)}, bf16[2,10,16,512]{3,2,1,0:T(8,128)(2,1)S(1)}, u32[]{:S(2)}, u32[]{:S(2)}) collective-permute-start(bf16[2,10,16,512]{3,2,1,0:T(8,128)(2,1)S(1)} %hand.1), channel_id=1, source_target_pairs={{0,1},{1,0},{2,3},{3,2},{4,5},{5,4},{6,7},{7,6},{8,9},{9,8},{10,11... | collective-permute-start | bytes 983048 | tf_op jit(solution)/shard_map/ppermute | solution.py:565
  57.1 12.4 %all-to-all-start.2 = ((f32[32,2,128]{2,1,0:T(2,128)}), f32[32,2,128]{2,1,0:T(2,128)S(1)}, u32[]{:S(2)}, u32[]{:S(2)}) async-start(f32[32,2,128]{2,1,0:T(2,128)} %bitcast.6), calls=%async_computation.2 | async-start | bytes 65536 | tf_op jit(solution)/shard_map/all_to_all | solution.py:617

commit v6 on v5

--- a/solution.py
+++ b/solution.py
@@ -437,7 +437,7 @@
             pltpu.VMEM((n, 128), f32),
         ],
         name="last",
-        **params(L_LAST, 0, 0),
+        **params(L_LAST, int(0.75 * 8 * n * width * width), int(0.75 * 8 * width * width)),
     )(*blocks, tail, rows, acco, accs, proj, side, side_sib, read, ranks)
 
 
@@ -510,7 +510,9 @@
 
     wide = jnp.concatenate([notes] * (count // 128), 1) if count > 128 else notes
     place, unit, kind, group = where_from(wide.shape)
-    match = (place == (plane ^ (group & (pop - 1)))) & ((unit & 1) == (core ^ (group >> (pop.bit_length() - 1))))
+    spot = group & (pop - 1)
+    away = (spot >> 1) | ((spot & 1) * (pop // 2))
+    match = (place == (plane ^ away)) & ((unit & 1) == (core ^ (group >> (pop.bit_length() - 1))))
     total = jnp.sum(jnp.where(match & (kind == 0), wide, 0.0), 0, keepdims=True)
     rank = jnp.sum(jnp.where(match & (kind == 1) & (unit < 2), wide, 0.0), 0, keepdims=True)
     fitness = rank / (count - 1) - 0.5 + total / plays
@@ -584,7 +586,7 @@
     w_own = swap(w_sib, "tp", 1)
     base = lax.all_to_all(base, "tp", 0, 0)
     proj1, pack = proj_call(got, post_loc)
-    near = swap(pack, "pop", 1)
+    near = swap(pack, "pop", pop // 2)
     s2o, s2s, memo, mems, s1c = step2_call(base, got, w_own, w_sib, proj1, side, side_sib, epis)
     far, order = [], []
     if tp == 8:
@@ -609,8 +611,8 @@
     notes = last_call(
         end, ends, tail, got, acco, accs, proj, side, side_sib, read, member_ranks[None], epis, pop * tp
     )
-    groups, mask = [pair], 2
-    while mask < pop:
+    groups, mask = [pair], 1
+    while mask < pop // 2:
         groups += [swap(g, "pop", mask) for g in groups]
         mask *= 2
     groups += [swap(g, "tp", 1) for g in groups[:1]] + [swap(hand_call(g, notes), "tp", 1) for g in groups[1:]]

time: 72.9 us -> 72.9 us (level)
  starting transfers between devices: 19.5 us -> 21 us
  waiting for transfers between devices: 15.5 us -> 14 us
    ppermute x13, waiting for transfers between devices: 5.62 us -> 4.07 us  [swap(): lax.ppermute(x, axis, [(i, i ^ mask) for i in range(lax.axis_size(axis))])]
    ppermute x13, starting transfers between devices: 10.8 us -> 11.6 us  [swap(): lax.ppermute(x, axis, [(i, i ^ mask) for i in range(lax.axis_size(axis))])]
  transfers between devices with their start and end apart: 15 -> 15, of which waited for: 6 -> 7; matrix products, arithmetic and copies ran while one was open for 0% -> 0% of each run, Pallas kernels for 28% -> 28%
where the time goes in v6:
time: 72.9 us; the launch traced here: 72.5 us
  Pallas kernels  23.4 us (32%)
  starting transfers between devices  21 us (29%)
  waiting for transfers between devices  14 us (19%)
  blocking collectives  13.3 us (18%)
  between operations  0.8 us (1%)
    all_to_all x1, blocking collectives, shards(): got = lax.all_to_all(load, 'tp', 0, 0)  13.3 us
    ppermute x13, starting transfers between devices, swap(): lax.ppermute(x, axis, [(i, i ^ mask) for i in range(lax.axis_size(axis))])  11.6 us
    all_to_all x1, waiting for transfers between devices, shards(): notes = lax.all_to_all(notes, ('pop', 'tp'), 0, 0, tiled=True)  6.88 us
    all_to_all x1, starting transfers between devices, shards(): notes = lax.all_to_all(notes, ('pop', 'tp'), 0, 0, tiled=True)  5.83 us
    pallas_call x1, Pallas kernels, step2_call(): pl.pallas_call(functools.partial(step2_kernel, epis=epis), in_specs=[VM,...  4.64 us
    pallas_call x2, Pallas kernels, part_call(): pl.pallas_call(functools.partial(part_kernel, order=order, tail=tail), in...  4.51 us
    ppermute x13, waiting for transfers between devices, swap(): lax.ppermute(x, axis, [(i, i ^ mask) for i in range(lax.axis_size(axis))])  4.07 us
    pallas_call x1, Pallas kernels, drive_call(): pl.pallas_call(drive_kernel, in_specs=[HB] * 7, out_specs=[VM] * 3, out_s...  3.88 us
  transfers between devices with their start and end apart: 15, of which 7 were waited for; matrix products, arithmetic and copies ran while one was open for 0% of the time, Pallas kernels for 28%

profile of v6, /device:TPU:0, one launch (start us, length us, event | category | flops | bytes accessed | tf_op | source)
XLA Modules:
  0.0 72.5 jit_solution(15282416225389568212)
XLA Ops:
  1.1 3.9 %drive.1 = (f32[72,512]{1,0:T(8,128)}, bf16[8,48,512]{2,1,0:T(8,128)(2,1)}, bf16[2,16,512]{2,1,0:T(8,128)(2,1)}) custom-call(s32[15,4,4096]{2,1,0:T(4,128)} %bitcast.10, bf16[4096,512]{1,0:T(8,128)(2,1)} %win_hbm.1, f32[1,512]{1,0:T(1,128)} %bitcast.11, f32[1,512]{1,0:T(1,128)} %bitcast.12, f32[1,512]{1,0:T(1,128)} %bitcast.13, bf16[256,512]{1,0:T(8,128)(2,1)} %table_hbm.1, ...), custom_call_target="tpu_custom_call" | custom-call | flops 268435456 | bytes 5242880 | tf_op jit(solution)/shard_map/drive/pallas_call | solution.py:116
  5.0 13.3 %all_to_all.21.got_hbm.got_ref.rows_ref.refs_4_.refs_3_ = bf16[8,48,512]{2,1,0:T(8,128)(2,1)} all-to-all(bf16[8,48,512]{2,1,0:T(8,128)(2,1)} %get-tuple-element.28), channel_id=1, replica_groups=mesh['pop'=4,'tp'=8] {'tp'}, dimensions={0} | all-to-all | bytes 786432 | tf_op jit(solution)/shard_map/all_to_all | solution.py:582
  18.4 3.2 %base.1.after_ref = f32[8,16,512]{2,1,0:T(8,128)} custom-call(bf16[8,48,512]{2,1,0:T(8,128)(2,1)} %all_to_all.21.got_hbm.got_ref.rows_ref.refs_4_.refs_3_, bf16[4096,512]{1,0:T(8,128)(2,1)} %w_hbm.1, f32[72,512]{1,0:T(8,128)} %get-tuple-element.29.side_hbm.so_ref.refs_7_), custom_call_target="tpu_custom_call" | custom-call | flops 67108864 | bytes 4194304 | tf_op jit(solution)/shard_map/base/pallas_call | solution.py:158
  21.7 3.6 %all-to-all-start.1 = ((f32[8,16,512]{2,1,0:T(8,128)}), f32[8,16,512]{2,1,0:T(8,128)S(1)}, u32[]{:S(2)}, u32[]{:S(2)}) async-start(f32[8,16,512]{2,1,0:T(8,128)} %base.1.after_ref), calls=%async_computation.1 | async-start | bytes 524288 | tf_op jit(solution)/shard_map/all_to_all | solution.py:587
  25.9 2.7 %collective-permute-start.4 = (bf16[10,16,512]{2,1,0:T(8,128)(2,1)S(1)}, bf16[10,16,512]{2,1,0:T(8,128)(2,1)S(1)}, u32[]{:S(2)}, u32[]{:S(2)}) collective-permute-start(bf16[10,16,512]{2,1,0:T(8,128)(2,1)S(1)} %get-tuple-element.37.pack_ref), channel_id=1, source_target_pairs={{0,16},{8,24},{16,0},{24,8},{1,17},{9,25},{17,1},{25,9},{2,18},{10... | collective-permute-start | bytes 491528 | tf_op jit(solution)/shard_map/ppermute | solution.py:567
  28.6 0.5 collective-permute-done.2.ss_ref.refs_8_
  29.1 3.0 %all-to-all-done.1.base_ref = f32[8,16,512]{2,1,0:T(8,128)S(1)} async-done(((f32[8,16,512]{2,1,0:T(8,128)}), f32[8,16,512]{2,1,0:T(8,128)S(1)}, u32[]{:S(2)}, u32[]{:S(2)}) %all-to-all-start.1) | async-done | bytes 262176 | tf_op jit(solution)/shard_map/all_to_all | solution.py:587
  32.2 4.6 %step2.1 = (bf16[240,512]{1,0:T(8,128)(2,1)S(1)}, bf16[240,512]{1,0:T(8,128)(2,1)S(1)}, f32[240,512]{1,0:T(8,128)S(1)}, f32[240,512]{1,0:T(8,128)S(1)}, bf16[2,240,512]{2,1,0:T(8,128)(2,1)S(1)}) custom-call(f32[8,16,512]{2,1,0:T(8,128)S(1)} %all-to-all-done.1.base_ref, bf16[8,48,512]{2,1,0:T(8,128)(2,1)S(1)} %copy-done, ...), custom_call_target="tpu_custom_call" | custom-call | flops 2013265920 | bytes 8388608 | tf_op jit(solution)/shard_map/step2/pallas_call | solution.py:272
  36.8 0.6 collective-permute-start.6
  37.4 0.6 collective-permute-start.3
  38.0 1.5 %collective-permute-start.8 = (bf16[240,512]{1,0:T(8,128)(2,1)S(1)}, bf16[240,512]{1,0:T(8,128)(2,1)S(1)}, u32[]{:S(2)}, u32[]{:S(2)}) collective-permute-start(bf16[240,512]{1,0:T(8,128)(2,1)S(1)} %get-tuple-element.33.s2s_ref), channel_id=1, source_target_pairs={{0,2},{1,3},{2,0},{3,1},{4,6},{5,7},{6,4},{7,5},{8,10},{9,11},{10,... | collective-permute-start | bytes 737288 | tf_op jit(solution)/shard_map/ppermute | solution.py:567
  39.5 1.5 %collective-permute-start.9 = (bf16[240,512]{1,0:T(8,128)(2,1)S(1)}, bf16[240,512]{1,0:T(8,128)(2,1)S(1)}, u32[]{:S(2)}, u32[]{:S(2)}) collective-permute-start(bf16[240,512]{1,0:T(8,128)(2,1)S(1)} %get-tuple-element.32.s2o_ref), channel_id=1, source_target_pairs={{0,4},{1,5},{2,6},{3,7},{4,0},{5,1},{6,2},{7,3},{8,12},{9,13},{10,... | collective-permute-start | bytes 737288 | tf_op jit(solution)/shard_map/ppermute | solution.py:567
  40.9 2.0 %own.1 = (f32[240,512]{1,0:T(8,128)S(1)}, f32[240,512]{1,0:T(8,128)S(1)}, f32[240,128]{1,0:T(8,128)S(1)}, f32[16,128]{1,0:T(8,128)S(1)}, bf16[2,10,16,512]{3,2,1,0:T(8,128)(2,1)S(1)}) custom-call(bf16[240,512]{1,0:T(8,128)(2,1)S(1)} %get-tuple-element.32.s2o_ref, bf16[240,512]{1,0:T(8,128)(2,1)S(1)} %get-tuple-element.33.s2s_ref, ...), custom_call_target="tpu_custom_call" | custom-call | flops 503316480 | bytes 2097152 | tf_op jit(solution)/shard_map/own/pallas_call | solution.py:346
  43.0 1.8 %collective-permute-start.10 = (bf16[2,10,16,512]{3,2,1,0:T(8,128)(2,1)S(1)}, bf16[2,10,16,512]{3,2,1,0:T(8,128)(2,1)S(1)}, u32[]{:S(2)}, u32[]{:S(2)}) collective-permute-start(bf16[2,10,16,512]{3,2,1,0:T(8,128)(2,1)S(1)} %get-tuple-element.38.after_ref.refs_0_), channel_id=1, source_target_pairs={{0,8},{8,0},{16,24},{24,16},{1,9},{9,1},{17,25},{25,17},{2,10},{10... | collective-permute-start | bytes 983048 | tf_op jit(solution)/shard_map/ppermute | solution.py:567
  44.7 1.1 %collective-permute-done.6.x_ref = bf16[240,512]{1,0:T(8,128)(2,1)S(1)} collective-permute-done((bf16[240,512]{1,0:T(8,128)(2,1)S(1)}, bf16[240,512]{1,0:T(8,128)(2,1)S(1)}, u32[]{:S(2)}, u32[]{:S(2)}) %collective-permute-start.6) | collective-permute-done | bytes 245792 | tf_op jit(solution)/shard_map/ppermute | solution.py:567
  46.3 1.5 %collective-permute-start.5 = (bf16[240,512]{1,0:T(8,128)(2,1)S(1)}, bf16[240,512]{1,0:T(8,128)(2,1)S(1)}, u32[]{:S(2)}, u32[]{:S(2)}) collective-permute-start(bf16[240,512]{1,0:T(8,128)(2,1)S(1)} %tie.4.refs_0_), channel_id=1, source_target_pairs={{0,4},{1,5},{2,6},{3,7},{4,0},{5,1},{6,2},{7,3},{8,12},{9,13},{10,... | collective-permute-start | bytes 737288 | tf_op jit(solution)/shard_map/ppermute | solution.py:567
  47.8 2.5 %part.2 = (f32[240,512]{1,0:T(8,128)S(1)}, f32[240,512]{1,0:T(8,128)S(1)}, f32[240,128]{1,0:T(8,128)S(1)}, bf16[2,2,512,512]{3,2,1,0:T(8,128)(2,1)S(1)}) custom-call(bf16[240,512]{1,0:T(8,128)(2,1)S(1)} %tie.4.refs_0_, bf16[240,512]{1,0:T(8,128)(2,1)S(1)} %tie.5.refs_1_, bf16[4096,512]{1,0:T(8,128)(2,1)} %collective-permute-done.1.wo_hbm.refs_2_, ...), custom_call_target="tpu_custom_call" | custom-call | flops 503316480 | bytes 2097152 | tf_op jit(solution)/shard_map/part/pallas_call | solution.py:382
  50.3 1.3 %collective-permute-done.8.refs_0_ = bf16[240,512]{1,0:T(8,128)(2,1)S(1)} collective-permute-done((bf16[240,512]{1,0:T(8,128)(2,1)S(1)}, bf16[240,512]{1,0:T(8,128)(2,1)S(1)}, u32[]{:S(2)}, u32[]{:S(2)}) %collective-permute-start.8) | collective-permute-done | bytes 245792 | tf_op jit(solution)/shard_map/ppermute | solution.py:567
  51.6 2.0 %part.3 = (f32[240,512]{1,0:T(8,128)S(1)}, f32[240,512]{1,0:T(8,128)S(1)}, f32[240,128]{1,0:T(8,128)S(1)}) custom-call(bf16[240,512]{1,0:T(8,128)(2,1)S(1)} %collective-permute-done.8.refs_0_, bf16[240,512]{1,0:T(8,128)(2,1)S(1)} %collective-permute-done.9.refs_1_, bf16[4096,512]{1,0:T(8,128)(2,1)} %collective-permute-done.1.wo_hbm.refs_2_, ...), custom_call_target="tpu_custom_call" | custom-call | flops 503316480 | bytes 2097152 | tf_op jit(solution)/shard_map/part/pallas_call | solution.py:382
  53.6 1.1 %collective-permute-done.7.refs_1_ = bf16[240,512]{1,0:T(8,128)(2,1)S(1)} collective-permute-done((bf16[240,512]{1,0:T(8,128)(2,1)S(1)}, bf16[240,512]{1,0:T(8,128)(2,1)S(1)}, u32[]{:S(2)}, u32[]{:S(2)}) %collective-permute-start.7) | collective-permute-done | bytes 245792 | tf_op jit(solution)/shard_map/ppermute | solution.py:567
  54.7 1.6 %last.1.after_ref = f32[64,128]{1,0:T(8,128)} custom-call(bf16[240,512]{1,0:T(8,128)(2,1)S(1)} %collective-permute-done.5.refs_0_, bf16[240,512]{1,0:T(8,128)(2,1)S(1)} %collective-permute-done.7.refs_1_, bf16[2,2,512,512]{3,2,1,0:T(8,128)(2,1)S(1)} %get-tuple-element.42.refs_2_, bf16[8,48,512]{2,1,0:T(8,128)(2,1)S(1)} %copy-done, ...), custom_call_target="tpu_custom_call" | custom-call | flops 377487360 | bytes 1572864 | tf_op jit(solution)/shard_map/last/pallas_call | solution.py:429
  56.4 5.8 %all-to-all-start.2 = ((f32[32,2,128]{2,1,0:T(2,128)}), f32[32,2,128]{2,1,0:T(2,128)S(1)}, u32[]{:S(2)}, u32[]{:S(2)}) async-start(f32[32,2,128]{2,1,0:T(2,128)} %bitcast.6), calls=%async_computation.2 | async-start | bytes 65536 | tf_op jit(solution)/shard_map/all_to_all | solution.py:619
  62.6 6.9 %all-to-all-done.2 = f32[32,2,128]{2,1,0:T(2,128)S(1)} async-done(((f32[32,2,128]{2,1,0:T(2,128)}), f32[32,2,128]{2,1,0:T(2,128)S(1)}, u32[]{:S(2)}, u32[]{:S(2)}) %all-to-all-start.2) | async-done | bytes 32800 | tf_op jit(solution)/shard_map/all_to_all | solution.py:619
  69.5 3.0 %grad.1 = (bf16[4096,512]{1,0:T(8,128)(2,1)}, f32[32]{0:T(128)}) custom-call(f32[64,128]{1,0:T(8,128)S(1)} %bitcast.8, bf16[4096,128]{1,0:T(8,128)(2,1)S(1)} %get-tuple-element.50.pret_ref, bf16[128,512]{1,0:T(8,128)(2,1)S(1)} %get-tuple-element.51.post_ref), custom_call_target="tpu_custom_call" | custom-call | flops 1073741824 | bytes 5242880 | tf_op jit(solution)/shard_map/grad/pallas_call | solution.py:551
  (29 shorter events, 2.2 us)
Async XLA Ops:
  0.6 21.0 %collective-permute-start = (bf16[4096,512]{1,0:T(8,128)(2,1)}, bf16[4096,512]{1,0:T(8,128)(2,1)}, u32[]{:S(2)}, u32[]{:S(2)}) collective-permute-start(bf16[4096,512]{1,0:T(8,128)(2,1)} %w_hbm.1), channel_id=1, source_target_pairs={{0,1},{1,0},{2,3},{3,2},{4,5},{5,4},{6,7},{7,6},{8,9},{9,8},{10,11... | collective-permute-start | bytes 12582920 | tf_op jit(solution)/shard_map/ppermute | solution.py:567
  21.6 3.7 %copy-start.1 = (f32[72,512]{1,0:T(8,128)S(1)}, f32[72,512]{1,0:T(8,128)}, u32[]{:S(2)}) copy-start(f32[72,512]{1,0:T(8,128)} %get-tuple-element.29.side_hbm.so_ref.refs_7_) | copy-start | bytes 442372
  21.6 4.1 %copy-start = (bf16[8,48,512]{2,1,0:T(8,128)(2,1)S(1)}, bf16[8,48,512]{2,1,0:T(8,128)(2,1)}, u32[]{:S(2)}) copy-start(bf16[8,48,512]{2,1,0:T(8,128)(2,1)} %all_to_all.21.got_hbm.got_ref.rows_ref.refs_4_.refs_3_) | copy-start | bytes 1179652
  21.6 4.1 %copy-start.2 = (bf16[2,16,512]{2,1,0:T(8,128)(2,1)S(1)}, bf16[2,16,512]{2,1,0:T(8,128)(2,1)}, u32[]{:S(2)}) copy-start(bf16[2,16,512]{2,1,0:T(8,128)(2,1)} %get-tuple-element.30.post_ref) | copy-start | bytes 98308
  21.7 10.5 %collective-permute-start.1 = (bf16[4096,512]{1,0:T(8,128)(2,1)}, bf16[4096,512]{1,0:T(8,128)(2,1)}, u32[]{:S(2)}, u32[]{:S(2)}) collective-permute-start(bf16[4096,512]{1,0:T(8,128)(2,1)} %tie.3.ws_hbm.refs_3_), channel_id=1, source_target_pairs={{0,1},{1,0},{2,3},{3,2},{4,5},{5,4},{6,7},{7,6},{8,9},{9,8},{10,11... | collective-permute-start | bytes 12582920 | tf_op jit(solution)/shard_map/ppermute | solution.py:567
  21.7 10.4 %all-to-all-start.1 = ((f32[8,16,512]{2,1,0:T(8,128)}), f32[8,16,512]{2,1,0:T(8,128)S(1)}, u32[]{:S(2)}, u32[]{:S(2)}) async-start(f32[8,16,512]{2,1,0:T(8,128)} %base.1.after_ref), calls=%async_computation.1 | async-start | bytes 524288 | tf_op jit(solution)/shard_map/all_to_all | solution.py:587
  25.3 3.8 %collective-permute-start.2 = (f32[72,512]{1,0:T(8,128)S(1)}, f32[72,512]{1,0:T(8,128)S(1)}, u32[]{:S(2)}, u32[]{:S(2)}) collective-permute-start(f32[72,512]{1,0:T(8,128)S(1)} %copy-done.1), channel_id=1, source_target_pairs={{0,1},{1,0},{2,3},{3,2},{4,5},{5,4},{6,7},{7,6},{8,9},{9,8},{10,11... | collective-permute-start | bytes 442376 | tf_op jit(solution)/shard_map/ppermute | solution.py:567
  25.9 15.1 %collective-permute-start.4 = (bf16[10,16,512]{2,1,0:T(8,128)(2,1)S(1)}, bf16[10,16,512]{2,1,0:T(8,128)(2,1)S(1)}, u32[]{:S(2)}, u32[]{:S(2)}) collective-permute-start(bf16[10,16,512]{2,1,0:T(8,128)(2,1)S(1)} %get-tuple-element.37.pack_ref), channel_id=1, source_target_pairs={{0,16},{8,24},{16,0},{24,8},{1,17},{9,25},{17,1},{25,9},{2,18},{10... | collective-permute-start | bytes 491528 | tf_op jit(solution)/shard_map/ppermute | solution.py:567
  36.8 9.0 %collective-permute-start.6 = (bf16[240,512]{1,0:T(8,128)(2,1)S(1)}, bf16[240,512]{1,0:T(8,128)(2,1)S(1)}, u32[]{:S(2)}, u32[]{:S(2)}) collective-permute-start(bf16[240,512]{1,0:T(8,128)(2,1)S(1)} %get-tuple-element.33.s2s_ref), channel_id=1, source_target_pairs={{0,4},{1,5},{2,6},{3,7},{4,0},{5,1},{6,2},{7,3},{8,12},{9,13},{10,... | collective-permute-start | bytes 737288 | tf_op jit(solution)/shard_map/ppermute | solution.py:567
  37.4 8.9 %collective-permute-start.3 = (bf16[240,512]{1,0:T(8,128)(2,1)S(1)}, bf16[240,512]{1,0:T(8,128)(2,1)S(1)}, u32[]{:S(2)}, u32[]{:S(2)}) collective-permute-start(bf16[240,512]{1,0:T(8,128)(2,1)S(1)} %get-tuple-element.32.s2o_ref), channel_id=1, source_target_pairs={{0,2},{1,3},{2,0},{3,1},{4,6},{5,7},{6,4},{7,5},{8,10},{9,11},{10,... | collective-permute-start | bytes 737288 | tf_op jit(solution)/shard_map/ppermute | solution.py:567
  38.0 13.6 %collective-permute-start.8 = (bf16[240,512]{1,0:T(8,128)(2,1)S(1)}, bf16[240,512]{1,0:T(8,128)(2,1)S(1)}, u32[]{:S(2)}, u32[]{:S(2)}) collective-permute-start(bf16[240,512]{1,0:T(8,128)(2,1)S(1)} %get-tuple-element.33.s2s_ref), channel_id=1, source_target_pairs={{0,2},{1,3},{2,0},{3,1},{4,6},{5,7},{6,4},{7,5},{8,10},{9,11},{10,... | collective-permute-start | bytes 737288 | tf_op jit(solution)/shard_map/ppermute | solution.py:567
  39.5 12.1 %collective-permute-start.9 = (bf16[240,512]{1,0:T(8,128)(2,1)S(1)}, bf16[240,512]{1,0:T(8,128)(2,1)S(1)}, u32[]{:S(2)}, u32[]{:S(2)}) collective-permute-start(bf16[240,512]{1,0:T(8,128)(2,1)S(1)} %get-tuple-element.32.s2o_ref), channel_id=1, source_target_pairs={{0,4},{1,5},{2,6},{3,7},{4,0},{5,1},{6,2},{7,3},{8,12},{9,13},{10,... | collective-permute-start | bytes 737288 | tf_op jit(solution)/shard_map/ppermute | solution.py:567
  43.0 13.3 %collective-permute-start.10 = (bf16[2,10,16,512]{3,2,1,0:T(8,128)(2,1)S(1)}, bf16[2,10,16,512]{3,2,1,0:T(8,128)(2,1)S(1)}, u32[]{:S(2)}, u32[]{:S(2)}) collective-permute-start(bf16[2,10,16,512]{3,2,1,0:T(8,128)(2,1)S(1)} %get-tuple-element.38.after_ref.refs_0_), channel_id=1, source_target_pairs={{0,8},{8,0},{16,24},{24,16},{1,9},{9,1},{17,25},{25,17},{2,10},{10... | collective-permute-start | bytes 983048 | tf_op jit(solution)/shard_map/ppermute | solution.py:567
  45.8 8.9 %collective-permute-start.7 = (bf16[240,512]{1,0:T(8,128)(2,1)S(1)}, bf16[240,512]{1,0:T(8,128)(2,1)S(1)}, u32[]{:S(2)}, u32[]{:S(2)}) collective-permute-start(bf16[240,512]{1,0:T(8,128)(2,1)S(1)} %tie.5.refs_1_), channel_id=1, source_target_pairs={{0,2},{1,3},{2,0},{3,1},{4,6},{5,7},{6,4},{7,5},{8,10},{9,11},{10,... | collective-permute-start | bytes 737288 | tf_op jit(solution)/shard_map/ppermute | solution.py:567
  46.3 8.4 %collective-permute-start.5 = (bf16[240,512]{1,0:T(8,128)(2,1)S(1)}, bf16[240,512]{1,0:T(8,128)(2,1)S(1)}, u32[]{:S(2)}, u32[]{:S(2)}) collective-permute-start(bf16[240,512]{1,0:T(8,128)(2,1)S(1)} %tie.4.refs_0_), channel_id=1, source_target_pairs={{0,4},{1,5},{2,6},{3,7},{4,0},{5,1},{6,2},{7,3},{8,12},{9,13},{10,... | collective-permute-start | bytes 737288 | tf_op jit(solution)/shard_map/ppermute | solution.py:567
  51.6 10.6 %collective-permute-start.11 = (bf16[2,10,16,512]{3,2,1,0:T(8,128)(2,1)S(1)}, bf16[2,10,16,512]{3,2,1,0:T(8,128)(2,1)S(1)}, u32[]{:S(2)}, u32[]{:S(2)}) collective-permute-start(bf16[2,10,16,512]{3,2,1,0:T(8,128)(2,1)S(1)} %get-tuple-element.38.after_ref.refs_0_), channel_id=1, source_target_pairs={{0,1},{1,0},{2,3},{3,2},{4,5},{5,4},{6,7},{7,6},{8,9},{9,8},{10,11... | collective-permute-start | bytes 983048 | tf_op jit(solution)/shard_map/ppermute | solution.py:567
  51.6 3.1 %copy-start.3 = (s32[32]{0:T(128)S(1)}, s32[32]{0:T(128)}, u32[]{:S(2)}) copy-start(s32[32]{0:T(128)} %param.17) | copy-start | bytes 388
  56.3 5.9 %collective-permute-start.12 = (bf16[2,10,16,512]{3,2,1,0:T(8,128)(2,1)S(1)}, bf16[2,10,16,512]{3,2,1,0:T(8,128)(2,1)S(1)}, u32[]{:S(2)}, u32[]{:S(2)}) collective-permute-start(bf16[2,10,16,512]{3,2,1,0:T(8,128)(2,1)S(1)} %hand.1), channel_id=1, source_target_pairs={{0,1},{1,0},{2,3},{3,2},{4,5},{5,4},{6,7},{7,6},{8,9},{9,8},{10,11... | collective-permute-start | bytes 983048 | tf_op jit(solution)/shard_map/ppermute | solution.py:567
  56.4 13.1 %all-to-all-start.2 = ((f32[32,2,128]{2,1,0:T(2,128)}), f32[32,2,128]{2,1,0:T(2,128)S(1)}, u32[]{:S(2)}, u32[]{:S(2)}) async-start(f32[32,2,128]{2,1,0:T(2,128)} %bitcast.6), calls=%async_computation.2 | async-start | bytes 65536 | tf_op jit(solution)/shard_map/all_to_all | solution.py:619
